TPU v7x, 32 devices: a whole 2x2x4 slice. The times are simulated.
32 devices in a mesh: batch: 8 (over y, x, core), latent: 4 (over z).
Axes of the slice: x: 2, y: 2, z: 4, core: 2. Of those that a mesh axis runs over, the one named last changes fastest.
Arguments:
- rows: bfloat16 [4096, 2048], P('batch', 'latent'), may hold values from -8 to 8, as said below
- targets: bfloat16 [256, 2048], P('batch', 'latent'), may hold values from -16 to 16
- w_up: bfloat16 [2048, 1024], P('latent'), may hold values from -2.5 to 2.5
- bias: float32 [1024], replicated, may hold values from -3 to 3
- history: int32 [256, 512], P('batch'), may hold values from 0 to 511, as said below
- requests: int32 [64, 64], P('batch'), may hold values from -1 to 511, as said below
- upstream: bfloat16 [256, 1024], P('batch', 'latent'), may hold values from -6 to 6
Outputs:
- output: bfloat16 [256, 1024], P('batch', 'latent')
- row_grad: float32 [4096, 2048], P('batch', 'latent')
Inputs may be any that keep to these rules, and one draw needn't show every extreme that they name: `requests`: row d * 8 + o lists distinct owner-local row numbers in its first entries and -1 after them, with at least one live entry; for the last owner and for one owner drawn anew, every list is full. `history`: every entry names a live slot of its user's device. `rows`: values of order one.
All inputs are finite; a program needn't handle non-finite values.
Results may differ from a plain program's by a relative error of at most 0.012.
The roundings to bfloat16 on the way count: a program that leaves them out, or rounds other values in their place, can miss the bound.
Values may be sent and summed in bfloat16 or wider, within the bound.
No kernel may reach another device: no remote copies, remote signals or barrier semaphores. Data moves between devices by JAX's collectives and lax.ppermute only.
A program may use at most 64 MiB of HBM per device.

v0:
```python
import jax
import jax.numpy as jnp
from jax import lax
from jax.sharding import PartitionSpec as P

DL = 2048


def on_device(rows, targets, w_up, bias, history, requests, upstream):
    score_scale = DL ** (-0.5)
    owners = lax.axis_size("batch")
    capacity = requests.shape[1]
    slot_count = owners * capacity
    members = targets.shape[0]
    row_width = rows.shape[1]
    stored = rows.shape[0]
    hidden_share = upstream.shape[1]
    wanted = lax.all_to_all(requests, "batch", split_axis=0, concat_axis=0, tiled=True)
    usable = wanted >= 0
    chosen = jnp.take(rows, jnp.maximum(wanted, 0).reshape(-1), axis=0)
    chosen = jnp.where(usable.reshape(-1, 1), chosen, jnp.zeros_like(chosen))
    arrived = lax.all_to_all(
        chosen.reshape(owners, capacity, row_width),
        "batch",
        split_axis=0,
        concat_axis=0,
        tiled=True,
    )
    fetched = arrived.reshape(slot_count, row_width)
    offsets = (jnp.arange(members, dtype=jnp.int32) * slot_count)[:, None]
    segment_ids = (history + offsets).reshape(-1)

    def slot_sums(values):
        return jax.ops.segment_sum(values.reshape(-1), segment_ids, members * slot_count).reshape(
            members, slot_count
        )

    slot_scores = jnp.einsum("ud,sd->us", targets, fetched, preferred_element_type=jnp.float32)
    whole_scores = lax.psum(slot_scores, "latent")
    scores = jnp.take_along_axis(whole_scores, history, axis=1) * score_scale
    probability = jax.nn.softmax(scores, axis=1)
    weight = slot_sums(probability)
    pooled = jnp.dot(
        weight.astype(jnp.bfloat16), fetched, preferred_element_type=jnp.float32
    ).astype(jnp.bfloat16)
    partial_hidden = jnp.dot(pooled, w_up, preferred_element_type=jnp.float32)
    column = lax.axis_index("latent") * hidden_share
    hidden = lax.psum_scatter(partial_hidden, "latent", scatter_dimension=1, tiled=True)
    hidden = hidden + lax.dynamic_slice_in_dim(bias, column, hidden_share)
    activated, backward = jax.vjp(jax.nn.gelu, hidden)
    output = activated.astype(jnp.bfloat16)
    slopes = backward(upstream.astype(jnp.float32))[0].astype(jnp.bfloat16)
    slopes_full = lax.all_gather(slopes, "latent", axis=1, tiled=True)
    pooled_grad = jnp.einsum("uh,dh->ud", slopes_full, w_up, preferred_element_type=jnp.float32)
    slot_slopes = jnp.einsum(
        "ud,sd->us", pooled_grad.astype(jnp.bfloat16), fetched, preferred_element_type=jnp.float32
    )
    whole_slopes = lax.psum(slot_slopes, "latent")
    probability_grad = jnp.take_along_axis(whole_slopes, history, axis=1)
    score_grad = probability * (
        probability_grad - jnp.sum(probability * probability_grad, axis=1, keepdims=True)
    )
    weight_grad = slot_sums(score_grad)
    destination = jnp.where(usable, wanted, stored)
    slot_grad = jnp.einsum("us,ud->sd", weight, pooled_grad, precision=lax.Precision.HIGHEST)
    slot_grad = slot_grad + score_scale * jnp.einsum(
        "us,ud->sd", weight_grad, targets.astype(jnp.float32), precision=lax.Precision.HIGHEST
    )
    returned = lax.all_to_all(
        slot_grad.reshape(owners, capacity, row_width),
        "batch",
        split_axis=0,
        concat_axis=0,
        tiled=True,
    )
    summed = jax.ops.segment_sum(
        returned.reshape(-1, row_width), destination.reshape(-1), stored + 1
    )
    return (output, summed[:stored])


def solution(mesh):
    return jax.shard_map(
        on_device,
        mesh=mesh,
        in_specs=(
            P("batch", "latent"),
            P("batch", "latent"),
            P("latent", None),
            P(),
            P("batch", None),
            P("batch", None),
            P("batch", "latent"),
        ),
        out_specs=(P("batch", "latent"), P("batch", "latent")),
        check_vma=False,
    )
```

profile of v0, /device:TPU:0, one launch (start us, length us, event | category | flops | bytes accessed | tf_op | source)
XLA Modules:
  0.0 615.2 jit_solution(12138111015020188799)
XLA Ops:
  7.2 0.0 copy-start
  7.2 9.9 %all_to_all.22 = s32[8,1,64]{2,1,0:T(1,128)S(1)} all-to-all(s32[8,1,64]{2,1,0:T(1,128)} %bitcast.59), channel_id=1, replica_groups=mesh['batch'=8,'latent'=4] {'batch'}, dimensions={0} | all-to-all | bytes 4096 | tf_op jit(solution)/shard_map/all_to_all | solution.py:18
  17.1 0.5 broadcast.171
  17.6 0.7 reduce.3
  18.3 0.1 all_to_all.16
  18.4 3.1 gather_fusion
  21.5 0.0 copy-start.1
  21.5 0.0 copy-start.2
  21.5 1.0 select_select_fusion
  22.5 3.5 all-to-all-start.1
  26.0 0.0 all-reduce.3.cloned.1.call-start
  26.0 0.0 copy-done.1
  26.1 0.1 add_bitcast_fusion
  26.1 9.5 %all-to-all-done.1 = bf16[8,64,512]{2,1,0:T(8,128)(2,1)S(1)} async-done(((bf16[8,64,512]{2,1,0:T(8,128)(2,1)}), bf16[8,64,512]{2,1,0:T(8,128)(2,1)S(1)}, u32[]{:S(2)}, u32[]{:S(2)}) %all-to-all-start.1) | async-done | bytes 524320 | tf_op jit(solution)/shard_map/all_to_all | solution.py:22
  35.7 0.0 copy-done.2
  35.7 0.9 convolution_bitcast_fusion
  36.6 0.0 all-reduce.3.cloned.1.call-update
  36.6 0.0 reduce-scatter.2.cloned.1.call-start
  36.7 33.4 %all-reduce.3.cloned.1.call-done = f32[32,512]{1,0:T(8,128)} async-done(((f32[32,512]{1,0:T(8,128)}), f32[32,512]{1,0:T(8,128)}) %all-reduce.3.cloned.1.call-update) | async-done | bytes 65552 | tf_op jit(solution)/shard_map/psum | solution.py:39
  70.1 108.9 %gather_fusion.1 = f32[16384]{0:T(1024)S(1)} fusion(f32[32,512]{1,0:T(8,128)} %all-reduce.3.cloned.1.call-done, s32[16384]{0:T(1024)S(1)} %bitcast.45), kind=kCustom, calls=%fused_computation.clone | custom fusion | bytes 262144 | tf_op jit(solution)/shard_map/jit(take_along_axis)/gather | solution.py:40
  179.0 0.1 fusion.7
  179.1 0.2 fusion.6
  179.3 0.1 fusion.25
  179.5 113.5 %scatter_custom_fusion = f32[16384]{0:T(1024)S(1)} fusion(s32[16384]{0:T(1024)S(1)} %bitcast.53, f32[16384]{0:T(1024)S(1)} %bitcast.56, f32[]{:T(128)} %constant.25.clone.1), kind=kCustom, calls=%fused_computation.46 | custom fusion | flops 16384 | bytes 65540 | tf_op jit(solution)/shard_map/scatter-add | solution.py:34
  293.0 0.0 copy-start.3
  293.0 0.0 copy-done
  293.0 1.1 fusion.1
  294.1 0.0 reduce-scatter.2.cloned.1.call-update
  294.2 0.0 all-reduce.5.cloned.1.call-start
  294.2 0.8 dynamic_slice.3
  295.0 18.2 %reduce-scatter.2.cloned.1.call-done = f32[32,256]{1,0:T(8,128)} async-done(((f32[32,1024]{1,0:T(8,128)}), f32[32,256]{1,0:T(8,128)}) %reduce-scatter.2.cloned.1.call-update) | async-done | bytes 32784 | tf_op jit(solution)/shard_map/reduce_scatter | solution.py:48
  313.2 0.0 copy-done.3
  313.2 1.4 fusion.10
  314.6 13.1 %all_gather.3 = bf16[32,1024]{1,0:T(8,128)(2,1)S(1)} all-gather(bf16[32,256]{1,0:T(8,128)(2,1)S(1)} %get-tuple-element.5), channel_id=1, replica_groups=mesh['batch'=8,'latent'=4] {'latent'}, dimensions={1}, use_global_device_ids=true | all-gather | bytes 81920 | tf_op jit(solution)/shard_map/all_gather | solution.py:53
  327.7 0.4 fusion.26
  328.1 0.9 fusion.18
  329.1 0.0 all-reduce.5.cloned.1.call-update
  329.1 1.0 fusion.27
  330.1 31.3 %all-reduce.5.cloned.1.call-done = f32[32,512]{1,0:T(8,128)} async-done(((f32[32,512]{1,0:T(8,128)}), f32[32,512]{1,0:T(8,128)}) %all-reduce.5.cloned.1.call-update) | async-done | bytes 65552 | tf_op jit(solution)/shard_map/psum | solution.py:58
  361.4 108.9 %gather_fusion.2 = f32[16384]{0:T(1024)S(1)} fusion(f32[32,512]{1,0:T(8,128)} %all-reduce.5.cloned.1.call-done, s32[16384]{0:T(1024)S(1)} %bitcast.46), kind=kCustom, calls=%fused_computation.1.clone | custom fusion | bytes 262144 | tf_op jit(solution)/shard_map/jit(take_along_axis)/gather | solution.py:59
  470.3 0.2 multiply_reduce_fusion
  470.5 0.1 multiply_bitcast_fusion
  470.6 113.5 %scatter_custom_fusion.1 = f32[16384]{0:T(1024)S(1)} fusion(s32[16384]{0:T(1024)S(1)} %bitcast.54, f32[16384]{0:T(1024)S(1)} %bitcast.55, f32[]{:T(128)} %constant.25.clone.1), kind=kCustom, calls=%fused_computation.44 | custom fusion | flops 16384 | bytes 65540 | tf_op jit(solution)/shard_map/scatter-add | solution.py:34
  584.2 0.7 fusion
  584.8 18.8 %all_to_all.23 = f32[8,64,512]{2,1,0:T(8,128)S(1)} all-to-all(f32[8,64,512]{2,1,0:T(8,128)S(1)} %bitcast.50), channel_id=1, replica_groups=mesh['batch'=8,'latent'=4] {'batch'}, dimensions={0} | all-to-all | bytes 2097152 | tf_op jit(solution)/shard_map/all_to_all | solution.py:69
  603.6 4.0 scatter_custom_fusion.2
  607.7 1.0 slice.10
  (15 shorter events, 0.2 us)
Async XLA Ops:
  7.2 285.9 %copy-start = (bf16[512,1024]{1,0:T(8,128)(2,1)S(1)}, bf16[512,1024]{1,0:T(8,128)(2,1)}, u32[]{:S(2)}) copy-start(bf16[512,1024]{1,0:T(8,128)(2,1)} %param.11) | copy-start | bytes 3145732
  21.5 4.6 copy-start.1
  21.5 14.2 %copy-start.2 = (bf16[32,512]{1,0:T(8,128)(2,1)S(1)}, bf16[32,512]{1,0:T(8,128)(2,1)}, u32[]{:S(2)}) copy-start(bf16[32,512]{1,0:T(8,128)(2,1)} %param.10) | copy-start | bytes 98308
  22.5 13.2 %all-to-all-start.1 = ((bf16[8,64,512]{2,1,0:T(8,128)(2,1)}), bf16[8,64,512]{2,1,0:T(8,128)(2,1)S(1)}, u32[]{:S(2)}, u32[]{:S(2)}) async-start(bf16[8,64,512]{2,1,0:T(8,128)(2,1)} %select_select_fusion), calls=%async_computation.1 | async-start | bytes 1048576 | tf_op jit(solution)/shard_map/all_to_all | solution.py:22
  26.0 44.1 %all-reduce.3.cloned.1.call-start = ((), (), s32[]{:S(2)}) async-start(), calls=%async_computation.4 | async-start | bytes 131072 | tf_op jit(solution)/shard_map/psum | solution.py:39
  36.6 276.6 %reduce-scatter.2.cloned.1.call-start = ((), (), s32[]{:S(2)}) async-start(), calls=%async_computation.5 | async-start | bytes 163840 | tf_op jit(solution)/shard_map/reduce_scatter | solution.py:48
  293.0 20.2 %copy-start.3 = (bf16[32,256]{1,0:T(8,128)(2,1)S(1)}, bf16[32,256]{1,0:T(8,128)(2,1)}, u32[]{:S(2)}) copy-start(bf16[32,256]{1,0:T(8,128)(2,1)} %param.15) | copy-start | bytes 49156
  294.2 67.2 %all-reduce.5.cloned.1.call-start = ((), (), s32[]{:S(2)}) async-start(), calls=%async_computation.6 | async-start | bytes 131072 | tf_op jit(solution)/shard_map/psum | solution.py:58
Sparse Core Ops, SparseCore 0:
  36.7 33.3 all-reduce.2
  294.3 18.8 reduce-scatter.1
  329.2 32.1 all-reduce.4
where the time goes:
time: 616 us; the launch traced here: 615 us
  other arithmetic  235 us (38%)
  local copies, waits for them, and re-layouts  223 us (36%)
  waiting for transfers between devices  92.5 us (15%)
  blocking collectives  41.8 us (7%)
  between operations  14 us (2%)
    scatter-add x2, other arithmetic, slot_sums(): jax.ops.segment_sum(values.reshape(-1), segment_ids, members * slot_count)  227 us
    gather x2, local copies, waits for them, and re-layouts, on_device(): scores = jnp.take_along_axis(whole_scores, history, axis=1) * score_scale  109 us
    gather x2, local copies, waits for them, and re-layouts, on_device(): probability_grad = jnp.take_along_axis(whole_slopes, history, axis=1)  109 us
    psum x1, waiting for transfers between devices, on_device(): whole_scores = lax.psum(slot_scores, 'latent')  33.4 us
    psum x1, waiting for transfers between devices, on_device(): whole_slopes = lax.psum(slot_slopes, 'latent')  31.3 us
    all_to_all x1, blocking collectives, on_device(): lax.all_to_all(slot_grad.reshape(owners, capacity, row_width), 'batch', s...  18.8 us
    reduce_scatter x1, waiting for transfers between devices, on_device(): lax.psum_scatter(partial_hidden, 'latent', scatter_dimension=1, tiled=True)  18.2 us
    all_gather x1, blocking collectives, on_device(): slopes_full = lax.all_gather(slopes, 'latent', axis=1, tiled=True)  13.1 us
  transfers between devices with their start and end apart: 4, of which 4 were waited for; matrix products, arithmetic and copies ran while one was open for 0% of the time, Pallas kernels for 0%

commit v1 on v0

v1 whole, which is shorter than its diff:
```python
import jax
import jax.numpy as jnp
from jax import lax
from jax.sharding import PartitionSpec as P

DL = 2048


def swap(x, axis, k):
    n = lax.axis_size(axis)
    return lax.ppermute(x, axis, [(i, i ^ k) for i in range(n)])


def sum_all(x, axis):
    n = lax.axis_size(axis)
    parts = [swap(x, axis, k) for k in range(1, n)]
    for part in parts:
        x = x + part
    return x


def sum_share(x, axis):
    n = lax.axis_size(axis)
    me = lax.axis_index(axis)
    width = x.shape[1] // n

    def share(k):
        return lax.dynamic_slice_in_dim(x, (me ^ k) * width, width, axis=1)

    parts = [swap(share(k), axis, k) for k in range(1, n)]
    total = share(0)
    for part in parts:
        total = total + part
    return total


def gather_columns(x, axis):
    n = lax.axis_size(axis)
    me = lax.axis_index(axis)
    parts = jnp.stack([x] + [swap(x, axis, k) for k in range(1, n)])
    ordered = [lax.dynamic_index_in_dim(parts, me ^ i, 0, keepdims=False) for i in range(n)]
    return jnp.concatenate(ordered, axis=1)


def exchange(x):
    return lax.all_to_all(x, "batch", split_axis=0, concat_axis=0, tiled=True)


def on_device(rows, targets, w_up, bias, history, requests, upstream):
    score_scale = DL ** (-0.5)
    owners = lax.axis_size("batch")
    capacity = requests.shape[1]
    slot_count = owners * capacity
    row_width = rows.shape[1]
    stored = rows.shape[0]
    hidden_share = upstream.shape[1]

    wanted = exchange(requests).reshape(-1)
    places = lax.broadcasted_iota(jnp.int32, (slot_count, stored), 1)
    chosen = jnp.dot(
        (wanted[:, None] == places).astype(jnp.bfloat16), rows, preferred_element_type=jnp.float32
    ).astype(jnp.bfloat16)
    fetched = exchange(chosen.reshape(owners, capacity, row_width)).reshape(slot_count, row_width)

    slots = lax.broadcasted_iota(jnp.int32, (1, 1, slot_count), 2)
    count = jnp.sum((history[:, :, None] == slots).astype(jnp.float32), axis=1)

    slot_scores = jnp.einsum("ud,sd->us", targets, fetched, preferred_element_type=jnp.float32)
    scores = sum_all(slot_scores, "latent") * score_scale
    top = jnp.max(jnp.where(count > 0, scores, -jnp.inf), axis=1, keepdims=True)
    raised = jnp.where(count > 0, count * jnp.exp(scores - top), 0.0)
    weight = raised / jnp.sum(raised, axis=1, keepdims=True)

    pooled = jnp.dot(
        weight.astype(jnp.bfloat16), fetched, preferred_element_type=jnp.float32
    ).astype(jnp.bfloat16)
    partial_hidden = jnp.dot(pooled, w_up, preferred_element_type=jnp.float32)
    column = lax.axis_index("latent") * hidden_share
    hidden = sum_share(partial_hidden, "latent")
    hidden = hidden + lax.dynamic_slice_in_dim(bias, column, hidden_share)
    activated, backward = jax.vjp(jax.nn.gelu, hidden)
    output = activated.astype(jnp.bfloat16)
    slopes = backward(upstream.astype(jnp.float32))[0].astype(jnp.bfloat16)
    slopes_full = gather_columns(slopes, "latent")
    pooled_grad = jnp.einsum("uh,dh->ud", slopes_full, w_up, preferred_element_type=jnp.float32)
    slot_slopes = jnp.einsum(
        "ud,sd->us", pooled_grad.astype(jnp.bfloat16), fetched, preferred_element_type=jnp.float32
    )
    whole_slopes = sum_all(slot_slopes, "latent")
    weight_grad = weight * (
        whole_slopes - jnp.sum(weight * whole_slopes, axis=1, keepdims=True)
    )
    slot_grad = jnp.einsum("us,ud->sd", weight, pooled_grad, precision=lax.Precision.HIGHEST)
    slot_grad = slot_grad + score_scale * jnp.einsum(
        "us,ud->sd", weight_grad, targets.astype(jnp.float32), precision=lax.Precision.HIGHEST
    )
    returned = exchange(
        slot_grad.astype(jnp.bfloat16).reshape(owners, capacity, row_width)
    ).reshape(slot_count, row_width)
    row_grad = jnp.dot(
        (places.T == wanted[None, :]).astype(jnp.bfloat16),
        returned,
        preferred_element_type=jnp.float32,
    )
    return (output, row_grad)


def solution(mesh):
    return jax.shard_map(
        on_device,
        mesh=mesh,
        in_specs=(
            P("batch", "latent"),
            P("batch", "latent"),
            P("latent", None),
            P(),
            P("batch", None),
            P("batch", None),
            P("batch", "latent"),
        ),
        out_specs=(P("batch", "latent"), P("batch", "latent")),
        check_vma=False,
    )
```

time: 616 us -> 76.6 us (0.12)
  other arithmetic: 235 us -> 6.52 us
  local copies, waits for them, and re-layouts: 223 us -> 1.4 us
  waiting for transfers between devices: 92.5 us -> 17.3 us
  blocking collectives: 41.8 us -> 22.2 us
  starting transfers between devices: 3.62 us -> 21 us
  between operations: 14 us -> 0.8 us
    scatter-add x3 -> x0, other arithmetic: 231 us -> none  [the longest x2 227 us: slot_sums(): jax.ops.segment_sum(values.reshape(-1), segment_ids, members * slot_count)]
    gather x5 -> x0, local copies, waits for them, and re-layouts: 221 us -> none  [the longest x2 109 us: on_device(): scores = jnp.take_along_axis(whole_scores, history, axis=1) * score_scale]
    psum x2 -> x0, waiting for transfers between devices: 64.7 us -> none  [the longest x1 33.4 us: on_device(): whole_scores = lax.psum(slot_scores, 'latent')]
    reduce_scatter x1 -> x0, waiting for transfers between devices: 18.2 us -> none  [on_device(): lax.psum_scatter(partial_hidden, 'latent', scatter_dimension=1, tiled=True)]
    ppermute x0 -> x12, starting transfers between devices: none -> 17.5 us  [swap(): return lax.ppermute(x, axis, [(i, i ^ k) for i in range(n)])]
    all_gather x1 -> x0, blocking collectives: 13.1 us -> none  [on_device(): slopes_full = lax.all_gather(slopes, 'latent', axis=1, tiled=True)]
    ppermute x0 -> x12, waiting for transfers between devices: none -> 8.29 us  [swap(): return lax.ppermute(x, axis, [(i, i ^ k) for i in range(n)])]
    all_to_all x2, blocking collectives: 28.7 us -> 22.2 us  [exchange(): return lax.all_to_all(x, 'batch', split_axis=0, concat_axis=0, tiled=True)]
  transfers between devices with their start and end apart: 4 -> 13, of which waited for: 4 -> 7; matrix products, arithmetic and copies ran while one was open for 0% -> 9% of each run, Pallas kernels for 0% -> 0%
where the time goes in v1:
time: 76.6 us; the launch traced here: 76.2 us
  blocking collectives  22.2 us (29%)
  starting transfers between devices  21 us (27%)
  waiting for transfers between devices  17.3 us (23%)
  matrix products  6.99 us (9%)
  other arithmetic  6.52 us (9%)
  local copies, waits for them, and re-layouts  1.4 us (2%)
  between operations  0.8 us (1%)
    all_to_all x2, blocking collectives, exchange(): return lax.all_to_all(x, 'batch', split_axis=0, concat_axis=0, tiled=True)  22.2 us
    ppermute x12, starting transfers between devices, swap(): return lax.ppermute(x, axis, [(i, i ^ k) for i in range(n)])  17.5 us
    all_to_all x1, waiting for transfers between devices, exchange(): return lax.all_to_all(x, 'batch', split_axis=0, concat_axis=0, tiled=True)  9.05 us
    ppermute x12, waiting for transfers between devices, swap(): return lax.ppermute(x, axis, [(i, i ^ k) for i in range(n)])  8.29 us
    reduce_sum x1, other arithmetic, on_device(): count = jnp.sum((history[:, :, None] == slots).astype(jnp.float32), axis=1)  4.65 us
    all_to_all x1, starting transfers between devices, exchange(): return lax.all_to_all(x, 'batch', split_axis=0, concat_axis=0, tiled=True)  3.49 us
    dot_general x1, matrix products, on_device(): jnp.einsum('us,ud->sd', weight_grad, targets.astype(jnp.float32), precisi...  1.54 us
    dot_general x1, matrix products, on_device(): jnp.dot((places.T == wanted[None, :]).astype(jnp.bfloat16), returned, pre...  1.54 us
  transfers between devices with their start and end apart: 13, of which 7 were waited for; matrix products, arithmetic and copies ran while one was open for 9% of the time, Pallas kernels for 0%

profile of v1, /device:TPU:0, one launch (start us, length us, event | category | flops | bytes accessed | tf_op | source)
XLA Modules:
  0.0 76.2 jit_solution(15811250271852600462)
XLA Ops:
  0.6 0.0 copy-start
  0.6 9.9 %all_to_all.19 = s32[8,1,64]{2,1,0:T(1,128)S(1)} all-to-all(s32[8,1,64]{2,1,0:T(1,128)} %bitcast.39), channel_id=1, replica_groups=mesh['batch'=8,'latent'=4] {'batch'}, dimensions={0} | all-to-all | bytes 4096 | tf_op jit(solution)/shard_map/all_to_all | solution.py:46
  10.5 0.5 broadcast.48
  11.1 0.7 reduce.3
  11.7 0.1 eq.33
  11.8 1.5 %convolution_convert_fusion = bf16[512,512]{1,0:T(8,128)(2,1)S(1)} fusion(bf16[512,512]{1,0:T(8,128)(2,1)} %param.7, s32[512]{0:T(512)S(1)} %eq.33), kind=kOutput, calls=%fused_computation.4 | convolution fusion | flops 268959744 | bytes 1050624 | tf_op jit(solution)/shard_map/dot_general | solution.py:60
  13.3 0.0 copy-start.2
  13.3 12.3 %all_to_all.20 = bf16[8,64,512]{2,1,0:T(8,128)(2,1)S(1)} all-to-all(bf16[8,64,512]{2,1,0:T(8,128)(2,1)S(1)} %bitcast.34), channel_id=1, replica_groups=mesh['batch'=8,'latent'=4] {'batch'}, dimensions={0} | all-to-all | bytes 1048576 | tf_op jit(solution)/shard_map/all_to_all | solution.py:46
  25.6 0.2 convolution_bitcast_fusion
  25.9 3.6 %collective-permute-start.2 = (f32[32,512]{1,0:T(8,128)S(1)}, f32[32,512]{1,0:T(8,128)S(1)}, u32[]{:S(2)}, u32[]{:S(2)}) collective-permute-start(f32[32,512]{1,0:T(8,128)S(1)} %convolution_bitcast_fusion), channel_id=1, source_target_pairs={{0,3},{1,2},{2,1},{3,0},{4,7},{5,6},{6,5},{7,4},{8,11},{9,10},{10,... | collective-permute-start | bytes 196616 | tf_op jit(solution)/shard_map/ppermute | solution.py:11
  29.5 0.0 collective-permute-start.1
  29.5 0.8 %collective-permute-start = (f32[32,512]{1,0:T(8,128)S(1)}, f32[32,512]{1,0:T(8,128)S(1)}, u32[]{:S(2)}, u32[]{:S(2)}) collective-permute-start(f32[32,512]{1,0:T(8,128)S(1)} %convolution_bitcast_fusion), channel_id=1, source_target_pairs={{0,1},{1,0},{2,3},{3,2},{4,5},{5,4},{6,7},{7,6},{8,9},{9,8},{10,11... | collective-permute-start | bytes 196616 | tf_op jit(solution)/shard_map/ppermute | solution.py:11
  30.3 4.6 %convert_reduce_fusion = f32[32,512]{1,0:T(8,128)S(1)} fusion(s32[32,512]{1,0:T(8,128)S(1)} %copy-done.2), kind=kLoop, calls=%fused_computation | loop fusion | flops 25149440 | bytes 131072 | tf_op jit(solution)/shard_map/reduce_sum | solution.py:66
  35.0 0.0 collective-permute-done.2
  35.0 0.0 collective-permute-done.1
  35.0 0.0 collective-permute-done
  35.0 0.1 select_reduce_fusion
  35.1 0.2 fusion.32
  35.3 0.1 broadcast_divide_fusion
  35.4 0.4 fusion.2
  35.9 1.3 %collective-permute-start.3 = (f32[32,256]{1,0:T(8,128)S(1)}, f32[32,256]{1,0:T(8,128)S(1)}, u32[]{:S(2)}, u32[]{:S(2)}) collective-permute-start(f32[32,256]{1,0:T(8,128)S(1)} %get-tuple-element.8), channel_id=1, source_target_pairs={{0,1},{1,0},{2,3},{3,2},{4,5},{5,4},{6,7},{7,6},{8,9},{9,8},{10,11... | collective-permute-start | bytes 98312 | tf_op jit(solution)/shard_map/ppermute | solution.py:11
  37.2 2.4 %collective-permute-start.5 = (f32[32,256]{1,0:T(8,128)S(1)}, f32[32,256]{1,0:T(8,128)S(1)}, u32[]{:S(2)}, u32[]{:S(2)}) collective-permute-start(f32[32,256]{1,0:T(8,128)S(1)} %get-tuple-element.9), channel_id=1, source_target_pairs={{0,3},{1,2},{2,1},{3,0},{4,7},{5,6},{6,5},{7,4},{8,11},{9,10},{10,... | collective-permute-start | bytes 98312 | tf_op jit(solution)/shard_map/ppermute | solution.py:11
  39.7 0.5 collective-permute-start.4
  40.1 0.8 dynamic_slice.32
  40.9 0.0 collective-permute-done.3
  40.9 2.0 %collective-permute-done.5 = f32[32,256]{1,0:T(8,128)S(1)} collective-permute-done((f32[32,256]{1,0:T(8,128)S(1)}, f32[32,256]{1,0:T(8,128)S(1)}, u32[]{:S(2)}, u32[]{:S(2)}) %collective-permute-start.5) | collective-permute-done | bytes 32800 | tf_op jit(solution)/shard_map/ppermute | solution.py:11
  42.9 1.6 %collective-permute-done.4 = f32[32,256]{1,0:T(8,128)S(1)} collective-permute-done((f32[32,256]{1,0:T(8,128)S(1)}, f32[32,256]{1,0:T(8,128)S(1)}, u32[]{:S(2)}, u32[]{:S(2)}) %collective-permute-start.4) | collective-permute-done | bytes 32800 | tf_op jit(solution)/shard_map/ppermute | solution.py:11
  44.5 2.0 %collective-permute-start.8 = (bf16[32,256]{1,0:T(8,128)(2,1)S(1)}, bf16[32,256]{1,0:T(8,128)(2,1)S(1)}, u32[]{:S(2)}, u32[]{:S(2)}) collective-permute-start(bf16[32,256]{1,0:T(8,128)(2,1)S(1)} %get-tuple-element.4), channel_id=1, source_target_pairs={{0,3},{1,2},{2,1},{3,0},{4,7},{5,6},{6,5},{7,4},{8,11},{9,10},{10,... | collective-permute-start | bytes 49160 | tf_op jit(solution)/shard_map/ppermute | solution.py:11
  46.5 0.6 collective-permute-start.7
  47.1 1.8 %collective-permute-start.6 = (bf16[32,256]{1,0:T(8,128)(2,1)S(1)}, bf16[32,256]{1,0:T(8,128)(2,1)S(1)}, u32[]{:S(2)}, u32[]{:S(2)}) collective-permute-start(bf16[32,256]{1,0:T(8,128)(2,1)S(1)} %get-tuple-element.4), channel_id=1, source_target_pairs={{0,1},{1,0},{2,3},{3,2},{4,5},{5,4},{6,7},{7,6},{8,9},{9,8},{10,11... | collective-permute-start | bytes 49160 | tf_op jit(solution)/shard_map/ppermute | solution.py:11
  49.0 1.1 %collective-permute-done.8 = bf16[32,256]{1,0:T(8,128)(2,1)S(1)} collective-permute-done((bf16[32,256]{1,0:T(8,128)(2,1)S(1)}, bf16[32,256]{1,0:T(8,128)(2,1)S(1)}, u32[]{:S(2)}, u32[]{:S(2)}) %collective-permute-start.8) | collective-permute-done | bytes 16416 | tf_op jit(solution)/shard_map/ppermute | solution.py:11
  50.1 1.2 %collective-permute-done.7 = bf16[32,256]{1,0:T(8,128)(2,1)S(1)} collective-permute-done((bf16[32,256]{1,0:T(8,128)(2,1)S(1)}, bf16[32,256]{1,0:T(8,128)(2,1)S(1)}, u32[]{:S(2)}, u32[]{:S(2)}) %collective-permute-start.7) | collective-permute-done | bytes 16416 | tf_op jit(solution)/shard_map/ppermute | solution.py:11
  51.3 0.0 collective-permute-done.6
  51.4 0.4 fusion.6
  51.8 0.3 fusion.27
  52.0 1.9 %collective-permute-start.11 = (f32[32,512]{1,0:T(8,128)S(1)}, f32[32,512]{1,0:T(8,128)S(1)}, u32[]{:S(2)}, u32[]{:S(2)}) collective-permute-start(f32[32,512]{1,0:T(8,128)S(1)} %fusion.27), channel_id=1, source_target_pairs={{0,3},{1,2},{2,1},{3,0},{4,7},{5,6},{6,5},{7,4},{8,11},{9,10},{10,... | collective-permute-start | bytes 196616 | tf_op jit(solution)/shard_map/ppermute | solution.py:11
  54.0 1.1 %collective-permute-start.10 = (f32[32,512]{1,0:T(8,128)S(1)}, f32[32,512]{1,0:T(8,128)S(1)}, u32[]{:S(2)}, u32[]{:S(2)}) collective-permute-start(f32[32,512]{1,0:T(8,128)S(1)} %fusion.27), channel_id=1, source_target_pairs={{0,2},{1,3},{2,0},{3,1},{4,6},{5,7},{6,4},{7,5},{8,10},{9,11},{10,... | collective-permute-start | bytes 196616 | tf_op jit(solution)/shard_map/ppermute | solution.py:11
  55.0 1.4 %collective-permute-start.9 = (f32[32,512]{1,0:T(8,128)S(1)}, f32[32,512]{1,0:T(8,128)S(1)}, u32[]{:S(2)}, u32[]{:S(2)}) collective-permute-start(f32[32,512]{1,0:T(8,128)S(1)} %fusion.27), channel_id=1, source_target_pairs={{0,1},{1,0},{2,3},{3,2},{4,5},{5,4},{6,7},{7,6},{8,9},{9,8},{10,11... | collective-permute-start | bytes 196616 | tf_op jit(solution)/shard_map/ppermute | solution.py:11
  56.4 1.0 %fusion.33 = f32[512,512]{1,0:T(8,128)S(1)} fusion(f32[32,512]{1,0:T(8,128)S(1)} %broadcast_divide_fusion, f32[32,512]{1,0:T(8,128)S(1)} %fusion.6), kind=kOutput, calls=%fused_computation.61 | convolution fusion | flops 100663296 | bytes 1179648 | tf_op jit(solution)/shard_map/us,ud->sd/dot_general | solution.py:93
  57.5 0.6 collective-permute-done.11
  58.1 1.7 %collective-permute-done.10 = f32[32,512]{1,0:T(8,128)S(1)} collective-permute-done((f32[32,512]{1,0:T(8,128)S(1)}, f32[32,512]{1,0:T(8,128)S(1)}, u32[]{:S(2)}, u32[]{:S(2)}) %collective-permute-start.10) | collective-permute-done | bytes 65568 | tf_op jit(solution)/shard_map/ppermute | solution.py:11
  59.8 0.0 collective-permute-done.9
  59.8 0.1 multiply_reduce_fusion
  60.0 1.5 %fusion.1 = bf16[512,512]{1,0:T(8,128)(2,1)} fusion(f32[512,512]{1,0:T(8,128)S(1)} %fusion.33, bf16[32,512]{1,0:T(8,128)(2,1)S(1)} %copy-done.1, f32[32,512]{1,0:T(8,128)S(1)} %broadcast_divide_fusion, f32[32,512]{1,0:T(8,128)S(1)} %get-tuple-element.3, f32[32]{0:T(128)S(1)} %get-tuple-element.2), kind=kOutput, calls=%fused_computation.5 | convolution fusion | flops 101482496 | bytes 1736832 | tf_op jit(solution)/shard_map/us,ud->sd/dot_general | solution.py:94
  61.5 3.5 %all-to-all-start.2 = ((bf16[8,64,512]{2,1,0:T(8,128)(2,1)}), bf16[8,64,512]{2,1,0:T(8,128)(2,1)S(1)}, u32[]{:S(2)}, u32[]{:S(2)}) async-start(bf16[8,64,512]{2,1,0:T(8,128)(2,1)} %bitcast.12), calls=%async_computation.2 | async-start | bytes 1048576 | tf_op jit(solution)/shard_map/all_to_all | solution.py:46
  65.0 0.6 multiply_convert_fusion
  65.6 9.0 %all-to-all-done.2 = bf16[8,64,512]{2,1,0:T(8,128)(2,1)S(1)} async-done(((bf16[8,64,512]{2,1,0:T(8,128)(2,1)}), bf16[8,64,512]{2,1,0:T(8,128)(2,1)S(1)}, u32[]{:S(2)}, u32[]{:S(2)}) %all-to-all-start.2) | async-done | bytes 524320 | tf_op jit(solution)/shard_map/all_to_all | solution.py:46
  74.7 1.5 %fusion.3 = f32[512,512]{1,0:T(8,128)} fusion(bf16[512,512]{1,0:T(8,128)(2,1)S(1)} %bitcast.33, s32[512]{0:T(512)S(1)} %eq.33), kind=kOutput, calls=%fused_computation.11 | convolution fusion | flops 268697600 | bytes 1574912 | tf_op jit(solution)/shard_map/dot_general | solution.py:100
  (10 shorter events, 0.1 us)
Async XLA Ops:
  0.6 34.8 %copy-start = (bf16[512,1024]{1,0:T(8,128)(2,1)S(1)}, bf16[512,1024]{1,0:T(8,128)(2,1)}, u32[]{:S(2)}) copy-start(bf16[512,1024]{1,0:T(8,128)(2,1)} %param.9) | copy-start | bytes 3145732
  11.8 13.8 %copy-start.1 = (bf16[32,512]{1,0:T(8,128)(2,1)S(1)}, bf16[32,512]{1,0:T(8,128)(2,1)}, u32[]{:S(2)}) copy-start(bf16[32,512]{1,0:T(8,128)(2,1)} %param.8) | copy-start | bytes 98308
  13.3 17.0 %copy-start.2 = (s32[32,512]{1,0:T(8,128)S(1)}, s32[32,512]{1,0:T(8,128)}, u32[]{:S(2)}) copy-start(s32[32,512]{1,0:T(8,128)} %param.11) | copy-start | bytes 196612
  25.9 9.1 %collective-permute-start.2 = (f32[32,512]{1,0:T(8,128)S(1)}, f32[32,512]{1,0:T(8,128)S(1)}, u32[]{:S(2)}, u32[]{:S(2)}) collective-permute-start(f32[32,512]{1,0:T(8,128)S(1)} %convolution_bitcast_fusion), channel_id=1, source_target_pairs={{0,3},{1,2},{2,1},{3,0},{4,7},{5,6},{6,5},{7,4},{8,11},{9,10},{10,... | collective-permute-start | bytes 196616 | tf_op jit(solution)/shard_map/ppermute | solution.py:11
  29.5 5.5 %collective-permute-start.1 = (f32[32,512]{1,0:T(8,128)S(1)}, f32[32,512]{1,0:T(8,128)S(1)}, u32[]{:S(2)}, u32[]{:S(2)}) collective-permute-start(f32[32,512]{1,0:T(8,128)S(1)} %convolution_bitcast_fusion), channel_id=1, source_target_pairs={{0,2},{1,3},{2,0},{3,1},{4,6},{5,7},{6,4},{7,5},{8,10},{9,11},{10,... | collective-permute-start | bytes 196616 | tf_op jit(solution)/shard_map/ppermute | solution.py:11
  29.5 5.5 %collective-permute-start = (f32[32,512]{1,0:T(8,128)S(1)}, f32[32,512]{1,0:T(8,128)S(1)}, u32[]{:S(2)}, u32[]{:S(2)}) collective-permute-start(f32[32,512]{1,0:T(8,128)S(1)} %convolution_bitcast_fusion), channel_id=1, source_target_pairs={{0,1},{1,0},{2,3},{3,2},{4,5},{5,4},{6,7},{7,6},{8,9},{9,8},{10,11... | collective-permute-start | bytes 196616 | tf_op jit(solution)/shard_map/ppermute | solution.py:11
  35.3 9.2 %copy-start.3 = (bf16[32,256]{1,0:T(8,128)(2,1)S(1)}, bf16[32,256]{1,0:T(8,128)(2,1)}, u32[]{:S(2)}) copy-start(bf16[32,256]{1,0:T(8,128)(2,1)} %param.13) | copy-start | bytes 49156
  35.9 5.0 %collective-permute-start.3 = (f32[32,256]{1,0:T(8,128)S(1)}, f32[32,256]{1,0:T(8,128)S(1)}, u32[]{:S(2)}, u32[]{:S(2)}) collective-permute-start(f32[32,256]{1,0:T(8,128)S(1)} %get-tuple-element.8), channel_id=1, source_target_pairs={{0,1},{1,0},{2,3},{3,2},{4,5},{5,4},{6,7},{7,6},{8,9},{9,8},{10,11... | collective-permute-start | bytes 98312 | tf_op jit(solution)/shard_map/ppermute | solution.py:11
  37.2 5.7 %collective-permute-start.5 = (f32[32,256]{1,0:T(8,128)S(1)}, f32[32,256]{1,0:T(8,128)S(1)}, u32[]{:S(2)}, u32[]{:S(2)}) collective-permute-start(f32[32,256]{1,0:T(8,128)S(1)} %get-tuple-element.9), channel_id=1, source_target_pairs={{0,3},{1,2},{2,1},{3,0},{4,7},{5,6},{6,5},{7,4},{8,11},{9,10},{10,... | collective-permute-start | bytes 98312 | tf_op jit(solution)/shard_map/ppermute | solution.py:11
  39.7 4.8 %collective-permute-start.4 = (f32[32,256]{1,0:T(8,128)S(1)}, f32[32,256]{1,0:T(8,128)S(1)}, u32[]{:S(2)}, u32[]{:S(2)}) collective-permute-start(f32[32,256]{1,0:T(8,128)S(1)} %get-tuple-element.10), channel_id=1, source_target_pairs={{0,2},{1,3},{2,0},{3,1},{4,6},{5,7},{6,4},{7,5},{8,10},{9,11},{10,... | collective-permute-start | bytes 98312 | tf_op jit(solution)/shard_map/ppermute | solution.py:11
  44.5 5.6 %collective-permute-start.8 = (bf16[32,256]{1,0:T(8,128)(2,1)S(1)}, bf16[32,256]{1,0:T(8,128)(2,1)S(1)}, u32[]{:S(2)}, u32[]{:S(2)}) collective-permute-start(bf16[32,256]{1,0:T(8,128)(2,1)S(1)} %get-tuple-element.4), channel_id=1, source_target_pairs={{0,3},{1,2},{2,1},{3,0},{4,7},{5,6},{6,5},{7,4},{8,11},{9,10},{10,... | collective-permute-start | bytes 49160 | tf_op jit(solution)/shard_map/ppermute | solution.py:11
  46.5 4.8 %collective-permute-start.7 = (bf16[32,256]{1,0:T(8,128)(2,1)S(1)}, bf16[32,256]{1,0:T(8,128)(2,1)S(1)}, u32[]{:S(2)}, u32[]{:S(2)}) collective-permute-start(bf16[32,256]{1,0:T(8,128)(2,1)S(1)} %get-tuple-element.4), channel_id=1, source_target_pairs={{0,2},{1,3},{2,0},{3,1},{4,6},{5,7},{6,4},{7,5},{8,10},{9,11},{10,... | collective-permute-start | bytes 49160 | tf_op jit(solution)/shard_map/ppermute | solution.py:11
  47.1 4.2 %collective-permute-start.6 = (bf16[32,256]{1,0:T(8,128)(2,1)S(1)}, bf16[32,256]{1,0:T(8,128)(2,1)S(1)}, u32[]{:S(2)}, u32[]{:S(2)}) collective-permute-start(bf16[32,256]{1,0:T(8,128)(2,1)S(1)} %get-tuple-element.4), channel_id=1, source_target_pairs={{0,1},{1,0},{2,3},{3,2},{4,5},{5,4},{6,7},{7,6},{8,9},{9,8},{10,11... | collective-permute-start | bytes 49160 | tf_op jit(solution)/shard_map/ppermute | solution.py:11
  52.0 6.1 %collective-permute-start.11 = (f32[32,512]{1,0:T(8,128)S(1)}, f32[32,512]{1,0:T(8,128)S(1)}, u32[]{:S(2)}, u32[]{:S(2)}) collective-permute-start(f32[32,512]{1,0:T(8,128)S(1)} %fusion.27), channel_id=1, source_target_pairs={{0,3},{1,2},{2,1},{3,0},{4,7},{5,6},{6,5},{7,4},{8,11},{9,10},{10,... | collective-permute-start | bytes 196616 | tf_op jit(solution)/shard_map/ppermute | solution.py:11
  54.0 5.9 %collective-permute-start.10 = (f32[32,512]{1,0:T(8,128)S(1)}, f32[32,512]{1,0:T(8,128)S(1)}, u32[]{:S(2)}, u32[]{:S(2)}) collective-permute-start(f32[32,512]{1,0:T(8,128)S(1)} %fusion.27), channel_id=1, source_target_pairs={{0,2},{1,3},{2,0},{3,1},{4,6},{5,7},{6,4},{7,5},{8,10},{9,11},{10,... | collective-permute-start | bytes 196616 | tf_op jit(solution)/shard_map/ppermute | solution.py:11
  55.0 4.8 %collective-permute-start.9 = (f32[32,512]{1,0:T(8,128)S(1)}, f32[32,512]{1,0:T(8,128)S(1)}, u32[]{:S(2)}, u32[]{:S(2)}) collective-permute-start(f32[32,512]{1,0:T(8,128)S(1)} %fusion.27), channel_id=1, source_target_pairs={{0,1},{1,0},{2,3},{3,2},{4,5},{5,4},{6,7},{7,6},{8,9},{9,8},{10,11... | collective-permute-start | bytes 196616 | tf_op jit(solution)/shard_map/ppermute | solution.py:11
  61.5 13.2 %all-to-all-start.2 = ((bf16[8,64,512]{2,1,0:T(8,128)(2,1)}), bf16[8,64,512]{2,1,0:T(8,128)(2,1)S(1)}, u32[]{:S(2)}, u32[]{:S(2)}) async-start(bf16[8,64,512]{2,1,0:T(8,128)(2,1)} %bitcast.12), calls=%async_computation.2 | async-start | bytes 1048576 | tf_op jit(solution)/shard_map/all_to_all | solution.py:46

commit v2 on v1

--- a/solution.py
+++ b/solution.py
@@ -14,23 +14,9 @@
 def sum_all(x, axis):
     n = lax.axis_size(axis)
     parts = [swap(x, axis, k) for k in range(1, n)]
+    total = x.astype(jnp.float32)
     for part in parts:
-        x = x + part
-    return x
-
-
-def sum_share(x, axis):
-    n = lax.axis_size(axis)
-    me = lax.axis_index(axis)
-    width = x.shape[1] // n
-
-    def share(k):
-        return lax.dynamic_slice_in_dim(x, (me ^ k) * width, width, axis=1)
-
-    parts = [swap(share(k), axis, k) for k in range(1, n)]
-    total = share(0)
-    for part in parts:
-        total = total + part
+        total = total + part.astype(jnp.float32)
     return total
 
 
@@ -64,6 +50,8 @@
 
     slots = lax.broadcasted_iota(jnp.int32, (1, 1, slot_count), 2)
     count = jnp.sum((history[:, :, None] == slots).astype(jnp.float32), axis=1)
+    upstream_full = gather_columns(upstream, "latent")
+    fetched, count, upstream_full = lax.optimization_barrier((fetched, count, upstream_full))
 
     slot_scores = jnp.einsum("ud,sd->us", targets, fetched, preferred_element_type=jnp.float32)
     scores = sum_all(slot_scores, "latent") * score_scale
@@ -75,14 +63,12 @@
         weight.astype(jnp.bfloat16), fetched, preferred_element_type=jnp.float32
     ).astype(jnp.bfloat16)
     partial_hidden = jnp.dot(pooled, w_up, preferred_element_type=jnp.float32)
+    hidden = sum_all(partial_hidden.astype(jnp.bfloat16), "latent") + bias
+    activated, backward = jax.vjp(jax.nn.gelu, hidden)
     column = lax.axis_index("latent") * hidden_share
-    hidden = sum_share(partial_hidden, "latent")
-    hidden = hidden + lax.dynamic_slice_in_dim(bias, column, hidden_share)
-    activated, backward = jax.vjp(jax.nn.gelu, hidden)
-    output = activated.astype(jnp.bfloat16)
-    slopes = backward(upstream.astype(jnp.float32))[0].astype(jnp.bfloat16)
-    slopes_full = gather_columns(slopes, "latent")
-    pooled_grad = jnp.einsum("uh,dh->ud", slopes_full, w_up, preferred_element_type=jnp.float32)
+    output = lax.dynamic_slice_in_dim(activated.astype(jnp.bfloat16), column, hidden_share, axis=1)
+    slopes = backward(upstream_full.astype(jnp.float32))[0].astype(jnp.bfloat16)
+    pooled_grad = jnp.einsum("uh,dh->ud", slopes, w_up, preferred_element_type=jnp.float32)
     slot_slopes = jnp.einsum(
         "ud,sd->us", pooled_grad.astype(jnp.bfloat16), fetched, preferred_element_type=jnp.float32
     )

time: 76.6 us -> 71.5 us (0.933)
  blocking collectives: 22.2 us -> 0 us
  starting transfers between devices: 21 us -> 30.1 us
  waiting for transfers between devices: 17.3 us -> 25.1 us
  matrix products: 6.99 us -> 7.8 us
  local copies, waits for them, and re-layouts: 1.4 us -> 0.63 us
    all_to_all x2 -> x0, blocking collectives: 22.2 us -> none  [exchange(): return lax.all_to_all(x, 'batch', split_axis=0, concat_axis=0, tiled=True)]
    all_to_all x1 -> x3, starting transfers between devices: 3.49 us -> 12.7 us  [exchange(): return lax.all_to_all(x, 'batch', split_axis=0, concat_axis=0, tiled=True)]
    all_to_all x1 -> x3, waiting for transfers between devices: 9.05 us -> 14.4 us  [exchange(): return lax.all_to_all(x, 'batch', split_axis=0, concat_axis=0, tiled=True)]
    ppermute x12, waiting for transfers between devices: 8.29 us -> 10.7 us  [swap(): return lax.ppermute(x, axis, [(i, i ^ k) for i in range(n)])]
    dot_general x1, matrix products: 1.53 us -> 2.35 us  [on_device(): jnp.dot((wanted[:, None] == places).astype(jnp.bfloat16), rows, preferred...]
    dynamic_slice x2 -> x0, local copies, waits for them, and re-layouts: 0.77 us -> none  [the longest x1 0.76 us: on_device(): hidden = hidden + lax.dynamic_slice_in_dim(bias, column, hidden_share)]
  transfers between devices with their start and end apart: 13 -> 15, of which waited for: 7 -> 9; matrix products, arithmetic and copies ran while one was open for 9% -> 14% of each run, Pallas kernels for 0% -> 0%
where the time goes in v2:
time: 71.5 us; the launch traced here: 71 us
  starting transfers between devices  30.1 us (42%)
  waiting for transfers between devices  25.1 us (35%)
  matrix products  7.8 us (11%)
  other arithmetic  6.58 us (9%)
  between operations  0.8 us (1%)
    ppermute x12, starting transfers between devices, swap(): return lax.ppermute(x, axis, [(i, i ^ k) for i in range(n)])  17.4 us
    all_to_all x3, waiting for transfers between devices, exchange(): return lax.all_to_all(x, 'batch', split_axis=0, concat_axis=0, tiled=True)  14.4 us
    all_to_all x3, starting transfers between devices, exchange(): return lax.all_to_all(x, 'batch', split_axis=0, concat_axis=0, tiled=True)  12.7 us
    ppermute x12, waiting for transfers between devices, swap(): return lax.ppermute(x, axis, [(i, i ^ k) for i in range(n)])  10.7 us
    reduce_sum x1, other arithmetic, on_device(): count = jnp.sum((history[:, :, None] == slots).astype(jnp.float32), axis=1)  4.66 us
    dot_general x1, matrix products, on_device(): jnp.dot((wanted[:, None] == places).astype(jnp.bfloat16), rows, preferred...  2.35 us
    dot_general x1, matrix products, on_device(): jnp.dot((places.T == wanted[None, :]).astype(jnp.bfloat16), returned, pre...  1.53 us
    dot_general x1, matrix products, on_device(): jnp.einsum('us,ud->sd', weight_grad, targets.astype(jnp.float32), precisi...  1.53 us
  transfers between devices with their start and end apart: 15, of which 9 were waited for; matrix products, arithmetic and copies ran while one was open for 14% of the time, Pallas kernels for 0%

profile of v2, /device:TPU:0, one launch (start us, length us, event | category | flops | bytes accessed | tf_op | source)
XLA Modules:
  0.0 71.0 jit_solution(4142342442463775884)
XLA Ops:
  0.6 0.0 copy-start
  0.6 5.3 %all-to-all-start = ((s32[8,1,64]{2,1,0:T(1,128)}), s32[8,1,64]{2,1,0:T(1,128)S(1)}, u32[]{:S(2)}, u32[]{:S(2)}) async-start(s32[8,1,64]{2,1,0:T(1,128)} %bitcast.38), calls=%async_computation | async-start | bytes 8192 | tf_op jit(solution)/shard_map/all_to_all | solution.py:32
  6.0 1.6 %collective-permute-start = (bf16[32,256]{1,0:T(8,128)(2,1)}, bf16[32,256]{1,0:T(8,128)(2,1)S(1)}, u32[]{:S(2)}, u32[]{:S(2)}) collective-permute-start(bf16[32,256]{1,0:T(8,128)(2,1)} %param.13), channel_id=1, source_target_pairs={{0,1},{1,0},{2,3},{3,2},{4,5},{5,4},{6,7},{7,6},{8,9},{9,8},{10,11... | collective-permute-start | bytes 49160 | tf_op jit(solution)/shard_map/ppermute | solution.py:11
  7.5 2.5 %collective-permute-start.2 = (bf16[32,256]{1,0:T(8,128)(2,1)}, bf16[32,256]{1,0:T(8,128)(2,1)S(1)}, u32[]{:S(2)}, u32[]{:S(2)}) collective-permute-start(bf16[32,256]{1,0:T(8,128)(2,1)} %param.13), channel_id=1, source_target_pairs={{0,3},{1,2},{2,1},{3,0},{4,7},{5,6},{6,5},{7,4},{8,11},{9,10},{10,... | collective-permute-start | bytes 49160 | tf_op jit(solution)/shard_map/ppermute | solution.py:11
  10.0 0.1 collective-permute-start.1
  10.1 0.4 all-to-all-done
  10.5 0.5 broadcast.72
  11.1 0.7 reduce.3
  11.7 0.1 eq.30
  11.8 2.4 %convolution_convert_fusion = bf16[512,512]{1,0:T(8,128)(2,1)} fusion(bf16[512,512]{1,0:T(8,128)(2,1)} %param.7, s32[512]{0:T(512)S(1)} %eq.30), kind=kOutput, calls=%fused_computation.4 | convolution fusion | flops 268959744 | bytes 1050624 | tf_op jit(solution)/shard_map/dot_general | solution.py:46
  14.2 3.9 %all-to-all-start.1 = ((bf16[8,64,512]{2,1,0:T(8,128)(2,1)}), bf16[8,64,512]{2,1,0:T(8,128)(2,1)S(1)}, u32[]{:S(2)}, u32[]{:S(2)}) async-start(bf16[8,64,512]{2,1,0:T(8,128)(2,1)} %bitcast.1), calls=%async_computation.1 | async-start | bytes 1048576 | tf_op jit(solution)/shard_map/all_to_all | solution.py:32
  18.1 4.7 %convert_reduce_fusion = f32[32,512]{1,0:T(8,128)S(1)} fusion(s32[32,512]{1,0:T(8,128)S(1)} %copy-done.2), kind=kLoop, calls=%fused_computation | loop fusion | flops 25149440 | bytes 131072 | tf_op jit(solution)/shard_map/reduce_sum | solution.py:52
  22.8 0.0 collective-permute-done
  22.8 0.0 collective-permute-done.2
  22.8 0.0 collective-permute-done.1
  22.9 4.9 %all-to-all-done.1 = bf16[8,64,512]{2,1,0:T(8,128)(2,1)S(1)} async-done(((bf16[8,64,512]{2,1,0:T(8,128)(2,1)}), bf16[8,64,512]{2,1,0:T(8,128)(2,1)S(1)}, u32[]{:S(2)}, u32[]{:S(2)}) %all-to-all-start.1) | async-done | bytes 524320 | tf_op jit(solution)/shard_map/all_to_all | solution.py:32
  27.8 0.2 convolution_bitcast_fusion
  28.1 3.3 %collective-permute-start.5 = (f32[32,512]{1,0:T(8,128)S(1)}, f32[32,512]{1,0:T(8,128)S(1)}, u32[]{:S(2)}, u32[]{:S(2)}) collective-permute-start(f32[32,512]{1,0:T(8,128)S(1)} %convolution_bitcast_fusion), channel_id=1, source_target_pairs={{0,3},{1,2},{2,1},{3,0},{4,7},{5,6},{6,5},{7,4},{8,11},{9,10},{10,... | collective-permute-start | bytes 196616 | tf_op jit(solution)/shard_map/ppermute | solution.py:11
  31.3 0.0 collective-permute-start.4
  31.4 1.1 %collective-permute-start.3 = (f32[32,512]{1,0:T(8,128)S(1)}, f32[32,512]{1,0:T(8,128)S(1)}, u32[]{:S(2)}, u32[]{:S(2)}) collective-permute-start(f32[32,512]{1,0:T(8,128)S(1)} %convolution_bitcast_fusion), channel_id=1, source_target_pairs={{0,1},{1,0},{2,3},{3,2},{4,5},{5,4},{6,7},{7,6},{8,9},{9,8},{10,11... | collective-permute-start | bytes 196616 | tf_op jit(solution)/shard_map/ppermute | solution.py:11
  32.5 2.1 %collective-permute-done.5 = f32[32,512]{1,0:T(8,128)S(1)} collective-permute-done((f32[32,512]{1,0:T(8,128)S(1)}, f32[32,512]{1,0:T(8,128)S(1)}, u32[]{:S(2)}, u32[]{:S(2)}) %collective-permute-start.5) | collective-permute-done | bytes 65568 | tf_op jit(solution)/shard_map/ppermute | solution.py:11
  34.6 2.1 %collective-permute-done.4 = f32[32,512]{1,0:T(8,128)S(1)} collective-permute-done((f32[32,512]{1,0:T(8,128)S(1)}, f32[32,512]{1,0:T(8,128)S(1)}, u32[]{:S(2)}, u32[]{:S(2)}) %collective-permute-start.4) | collective-permute-done | bytes 65568 | tf_op jit(solution)/shard_map/ppermute | solution.py:11
  36.8 0.0 collective-permute-done.3
  36.8 0.1 select_reduce_fusion
  36.9 0.2 fusion.37
  37.1 0.1 broadcast_divide_fusion
  37.2 0.4 convolution_convert_fusion.1
  37.7 1.8 %collective-permute-start.8 = (bf16[32,1024]{1,0:T(8,128)(2,1)S(1)}, bf16[32,1024]{1,0:T(8,128)(2,1)S(1)}, u32[]{:S(2)}, u32[]{:S(2)}) collective-permute-start(bf16[32,1024]{1,0:T(8,128)(2,1)S(1)} %convolution_convert_fusion.1), channel_id=1, source_target_pairs={{0,3},{1,2},{2,1},{3,0},{4,7},{5,6},{6,5},{7,4},{8,11},{9,10},{10,... | collective-permute-start | bytes 196616 | tf_op jit(solution)/shard_map/ppermute | solution.py:11
  39.4 0.1 collective-permute-start.7
  39.5 2.5 %collective-permute-start.6 = (bf16[32,1024]{1,0:T(8,128)(2,1)S(1)}, bf16[32,1024]{1,0:T(8,128)(2,1)S(1)}, u32[]{:S(2)}, u32[]{:S(2)}) collective-permute-start(bf16[32,1024]{1,0:T(8,128)(2,1)S(1)} %convolution_convert_fusion.1), channel_id=1, source_target_pairs={{0,1},{1,0},{2,3},{3,2},{4,5},{5,4},{6,7},{7,6},{8,9},{9,8},{10,11... | collective-permute-start | bytes 196616 | tf_op jit(solution)/shard_map/ppermute | solution.py:11
  42.1 1.7 %collective-permute-done.8 = bf16[32,1024]{1,0:T(8,128)(2,1)S(1)} collective-permute-done((bf16[32,1024]{1,0:T(8,128)(2,1)S(1)}, bf16[32,1024]{1,0:T(8,128)(2,1)S(1)}, u32[]{:S(2)}, u32[]{:S(2)}) %collective-permute-start.8) | collective-permute-done | bytes 65568 | tf_op jit(solution)/shard_map/ppermute | solution.py:11
  43.8 2.6 %collective-permute-done.7 = bf16[32,1024]{1,0:T(8,128)(2,1)S(1)} collective-permute-done((bf16[32,1024]{1,0:T(8,128)(2,1)S(1)}, bf16[32,1024]{1,0:T(8,128)(2,1)S(1)}, u32[]{:S(2)}, u32[]{:S(2)}) %collective-permute-start.7) | collective-permute-done | bytes 65568 | tf_op jit(solution)/shard_map/ppermute | solution.py:11
  46.4 0.0 collective-permute-done.6
  46.4 0.1 add_multiply_fusion
  46.5 0.4 fusion.15
  46.9 0.3 fusion.27
  47.2 1.6 %collective-permute-start.11 = (f32[32,512]{1,0:T(8,128)S(1)}, f32[32,512]{1,0:T(8,128)S(1)}, u32[]{:S(2)}, u32[]{:S(2)}) collective-permute-start(f32[32,512]{1,0:T(8,128)S(1)} %fusion.27), channel_id=1, source_target_pairs={{0,3},{1,2},{2,1},{3,0},{4,7},{5,6},{6,5},{7,4},{8,11},{9,10},{10,... | collective-permute-start | bytes 196616 | tf_op jit(solution)/shard_map/ppermute | solution.py:11
  48.7 0.5 collective-permute-start.10
  49.3 2.3 %collective-permute-start.9 = (f32[32,512]{1,0:T(8,128)S(1)}, f32[32,512]{1,0:T(8,128)S(1)}, u32[]{:S(2)}, u32[]{:S(2)}) collective-permute-start(f32[32,512]{1,0:T(8,128)S(1)} %fusion.27), channel_id=1, source_target_pairs={{0,1},{1,0},{2,3},{3,2},{4,5},{5,4},{6,7},{7,6},{8,9},{9,8},{10,11... | collective-permute-start | bytes 196616 | tf_op jit(solution)/shard_map/ppermute | solution.py:11
  51.6 1.0 %fusion.38 = f32[512,512]{1,0:T(8,128)S(1)} fusion(f32[32,512]{1,0:T(8,128)S(1)} %broadcast_divide_fusion, f32[32,512]{1,0:T(8,128)S(1)} %fusion.15), kind=kOutput, calls=%fused_computation.65 | convolution fusion | flops 100663296 | bytes 1179648 | tf_op jit(solution)/shard_map/us,ud->sd/dot_general | solution.py:79
  52.6 0.7 collective-permute-done.11
  53.3 1.4 %collective-permute-done.10 = f32[32,512]{1,0:T(8,128)S(1)} collective-permute-done((f32[32,512]{1,0:T(8,128)S(1)}, f32[32,512]{1,0:T(8,128)S(1)}, u32[]{:S(2)}, u32[]{:S(2)}) %collective-permute-start.10) | collective-permute-done | bytes 65568 | tf_op jit(solution)/shard_map/ppermute | solution.py:11
  54.7 0.1 multiply_reduce_fusion
  54.8 1.5 %fusion.1 = bf16[512,512]{1,0:T(8,128)(2,1)} fusion(f32[512,512]{1,0:T(8,128)S(1)} %fusion.38, bf16[32,512]{1,0:T(8,128)(2,1)S(1)} %copy-done.1, f32[32,512]{1,0:T(8,128)S(1)} %broadcast_divide_fusion, f32[32,512]{1,0:T(8,128)S(1)} %get-tuple-element.9, f32[32]{0:T(128)S(1)} %get-tuple-element.8), kind=kOutput, calls=%fused_computation.5 | convolution fusion | flops 101482496 | bytes 1736832 | tf_op jit(solution)/shard_map/us,ud->sd/dot_general | solution.py:80
  56.3 3.5 %all-to-all-start.2 = ((bf16[8,64,512]{2,1,0:T(8,128)(2,1)}), bf16[8,64,512]{2,1,0:T(8,128)(2,1)S(1)}, u32[]{:S(2)}, u32[]{:S(2)}) async-start(bf16[8,64,512]{2,1,0:T(8,128)(2,1)} %bitcast.12), calls=%async_computation.2 | async-start | bytes 1048576 | tf_op jit(solution)/shard_map/all_to_all | solution.py:32
  59.8 0.6 fusion.25
  60.4 9.1 %all-to-all-done.2 = bf16[8,64,512]{2,1,0:T(8,128)(2,1)S(1)} async-done(((bf16[8,64,512]{2,1,0:T(8,128)(2,1)}), bf16[8,64,512]{2,1,0:T(8,128)(2,1)S(1)}, u32[]{:S(2)}, u32[]{:S(2)}) %all-to-all-start.2) | async-done | bytes 524320 | tf_op jit(solution)/shard_map/all_to_all | solution.py:32
  69.5 1.5 %fusion.2 = f32[512,512]{1,0:T(8,128)} fusion(bf16[512,512]{1,0:T(8,128)(2,1)S(1)} %bitcast.33, s32[512]{0:T(512)S(1)} %eq.30), kind=kOutput, calls=%fused_computation.11 | convolution fusion | flops 268697600 | bytes 1574912 | tf_op jit(solution)/shard_map/dot_general | solution.py:86
  (13 shorter events, 0.1 us)
Async XLA Ops:
  0.6 36.6 %copy-start = (bf16[512,1024]{1,0:T(8,128)(2,1)S(1)}, bf16[512,1024]{1,0:T(8,128)(2,1)}, u32[]{:S(2)}) copy-start(bf16[512,1024]{1,0:T(8,128)(2,1)} %param.9) | copy-start | bytes 3145732
  0.6 9.9 %all-to-all-start = ((s32[8,1,64]{2,1,0:T(1,128)}), s32[8,1,64]{2,1,0:T(1,128)S(1)}, u32[]{:S(2)}, u32[]{:S(2)}) async-start(s32[8,1,64]{2,1,0:T(1,128)} %bitcast.38), calls=%async_computation | async-start | bytes 8192 | tf_op jit(solution)/shard_map/all_to_all | solution.py:32
  6.0 16.8 %collective-permute-start = (bf16[32,256]{1,0:T(8,128)(2,1)}, bf16[32,256]{1,0:T(8,128)(2,1)S(1)}, u32[]{:S(2)}, u32[]{:S(2)}) collective-permute-start(bf16[32,256]{1,0:T(8,128)(2,1)} %param.13), channel_id=1, source_target_pairs={{0,1},{1,0},{2,3},{3,2},{4,5},{5,4},{6,7},{7,6},{8,9},{9,8},{10,11... | collective-permute-start | bytes 49160 | tf_op jit(solution)/shard_map/ppermute | solution.py:11
  7.5 15.3 %collective-permute-start.2 = (bf16[32,256]{1,0:T(8,128)(2,1)}, bf16[32,256]{1,0:T(8,128)(2,1)S(1)}, u32[]{:S(2)}, u32[]{:S(2)}) collective-permute-start(bf16[32,256]{1,0:T(8,128)(2,1)} %param.13), channel_id=1, source_target_pairs={{0,3},{1,2},{2,1},{3,0},{4,7},{5,6},{6,5},{7,4},{8,11},{9,10},{10,... | collective-permute-start | bytes 49160 | tf_op jit(solution)/shard_map/ppermute | solution.py:11
  10.0 12.8 %collective-permute-start.1 = (bf16[32,256]{1,0:T(8,128)(2,1)}, bf16[32,256]{1,0:T(8,128)(2,1)S(1)}, u32[]{:S(2)}, u32[]{:S(2)}) collective-permute-start(bf16[32,256]{1,0:T(8,128)(2,1)} %param.13), channel_id=1, source_target_pairs={{0,2},{1,3},{2,0},{3,1},{4,6},{5,7},{6,4},{7,5},{8,10},{9,11},{10,... | collective-permute-start | bytes 49160 | tf_op jit(solution)/shard_map/ppermute | solution.py:11
  11.8 6.3 %copy-start.2 = (s32[32,512]{1,0:T(8,128)S(1)}, s32[32,512]{1,0:T(8,128)}, u32[]{:S(2)}) copy-start(s32[32,512]{1,0:T(8,128)} %param.11) | copy-start | bytes 196612
  11.8 11.0 %copy-start.3 = (bf16[32,256]{1,0:T(8,128)(2,1)S(1)}, bf16[32,256]{1,0:T(8,128)(2,1)}, u32[]{:S(2)}) copy-start(bf16[32,256]{1,0:T(8,128)(2,1)} %param.13) | copy-start | bytes 49156
  14.2 13.7 %copy-start.1 = (bf16[32,512]{1,0:T(8,128)(2,1)S(1)}, bf16[32,512]{1,0:T(8,128)(2,1)}, u32[]{:S(2)}) copy-start(bf16[32,512]{1,0:T(8,128)(2,1)} %param.8) | copy-start | bytes 98308
  14.2 13.7 %all-to-all-start.1 = ((bf16[8,64,512]{2,1,0:T(8,128)(2,1)}), bf16[8,64,512]{2,1,0:T(8,128)(2,1)S(1)}, u32[]{:S(2)}, u32[]{:S(2)}) async-start(bf16[8,64,512]{2,1,0:T(8,128)(2,1)} %bitcast.1), calls=%async_computation.1 | async-start | bytes 1048576 | tf_op jit(solution)/shard_map/all_to_all | solution.py:32
  28.1 6.6 %collective-permute-start.5 = (f32[32,512]{1,0:T(8,128)S(1)}, f32[32,512]{1,0:T(8,128)S(1)}, u32[]{:S(2)}, u32[]{:S(2)}) collective-permute-start(f32[32,512]{1,0:T(8,128)S(1)} %convolution_bitcast_fusion), channel_id=1, source_target_pairs={{0,3},{1,2},{2,1},{3,0},{4,7},{5,6},{6,5},{7,4},{8,11},{9,10},{10,... | collective-permute-start | bytes 196616 | tf_op jit(solution)/shard_map/ppermute | solution.py:11
  31.3 5.4 %collective-permute-start.4 = (f32[32,512]{1,0:T(8,128)S(1)}, f32[32,512]{1,0:T(8,128)S(1)}, u32[]{:S(2)}, u32[]{:S(2)}) collective-permute-start(f32[32,512]{1,0:T(8,128)S(1)} %convolution_bitcast_fusion), channel_id=1, source_target_pairs={{0,2},{1,3},{2,0},{3,1},{4,6},{5,7},{6,4},{7,5},{8,10},{9,11},{10,... | collective-permute-start | bytes 196616 | tf_op jit(solution)/shard_map/ppermute | solution.py:11
  31.4 5.4 %collective-permute-start.3 = (f32[32,512]{1,0:T(8,128)S(1)}, f32[32,512]{1,0:T(8,128)S(1)}, u32[]{:S(2)}, u32[]{:S(2)}) collective-permute-start(f32[32,512]{1,0:T(8,128)S(1)} %convolution_bitcast_fusion), channel_id=1, source_target_pairs={{0,1},{1,0},{2,3},{3,2},{4,5},{5,4},{6,7},{7,6},{8,9},{9,8},{10,11... | collective-permute-start | bytes 196616 | tf_op jit(solution)/shard_map/ppermute | solution.py:11
  36.9 9.5 %copy-start.4 = (f32[1024]{0:T(1024)S(1)}, f32[1024]{0:T(1024)}, u32[]{:S(2)}) copy-start(f32[1024]{0:T(1024)} %param.10) | copy-start | bytes 12292
  37.7 6.1 %collective-permute-start.8 = (bf16[32,1024]{1,0:T(8,128)(2,1)S(1)}, bf16[32,1024]{1,0:T(8,128)(2,1)S(1)}, u32[]{:S(2)}, u32[]{:S(2)}) collective-permute-start(bf16[32,1024]{1,0:T(8,128)(2,1)S(1)} %convolution_convert_fusion.1), channel_id=1, source_target_pairs={{0,3},{1,2},{2,1},{3,0},{4,7},{5,6},{6,5},{7,4},{8,11},{9,10},{10,... | collective-permute-start | bytes 196616 | tf_op jit(solution)/shard_map/ppermute | solution.py:11
  39.4 7.0 %collective-permute-start.7 = (bf16[32,1024]{1,0:T(8,128)(2,1)S(1)}, bf16[32,1024]{1,0:T(8,128)(2,1)S(1)}, u32[]{:S(2)}, u32[]{:S(2)}) collective-permute-start(bf16[32,1024]{1,0:T(8,128)(2,1)S(1)} %convolution_convert_fusion.1), channel_id=1, source_target_pairs={{0,2},{1,3},{2,0},{3,1},{4,6},{5,7},{6,4},{7,5},{8,10},{9,11},{10,... | collective-permute-start | bytes 196616 | tf_op jit(solution)/shard_map/ppermute | solution.py:11
  39.5 6.9 %collective-permute-start.6 = (bf16[32,1024]{1,0:T(8,128)(2,1)S(1)}, bf16[32,1024]{1,0:T(8,128)(2,1)S(1)}, u32[]{:S(2)}, u32[]{:S(2)}) collective-permute-start(bf16[32,1024]{1,0:T(8,128)(2,1)S(1)} %convolution_convert_fusion.1), channel_id=1, source_target_pairs={{0,1},{1,0},{2,3},{3,2},{4,5},{5,4},{6,7},{7,6},{8,9},{9,8},{10,11... | collective-permute-start | bytes 196616 | tf_op jit(solution)/shard_map/ppermute | solution.py:11
  47.2 6.1 %collective-permute-start.11 = (f32[32,512]{1,0:T(8,128)S(1)}, f32[32,512]{1,0:T(8,128)S(1)}, u32[]{:S(2)}, u32[]{:S(2)}) collective-permute-start(f32[32,512]{1,0:T(8,128)S(1)} %fusion.27), channel_id=1, source_target_pairs={{0,3},{1,2},{2,1},{3,0},{4,7},{5,6},{6,5},{7,4},{8,11},{9,10},{10,... | collective-permute-start | bytes 196616 | tf_op jit(solution)/shard_map/ppermute | solution.py:11
  48.7 5.9 %collective-permute-start.10 = (f32[32,512]{1,0:T(8,128)S(1)}, f32[32,512]{1,0:T(8,128)S(1)}, u32[]{:S(2)}, u32[]{:S(2)}) collective-permute-start(f32[32,512]{1,0:T(8,128)S(1)} %fusion.27), channel_id=1, source_target_pairs={{0,2},{1,3},{2,0},{3,1},{4,6},{5,7},{6,4},{7,5},{8,10},{9,11},{10,... | collective-permute-start | bytes 196616 | tf_op jit(solution)/shard_map/ppermute | solution.py:11
  49.3 5.4 %collective-permute-start.9 = (f32[32,512]{1,0:T(8,128)S(1)}, f32[32,512]{1,0:T(8,128)S(1)}, u32[]{:S(2)}, u32[]{:S(2)}) collective-permute-start(f32[32,512]{1,0:T(8,128)S(1)} %fusion.27), channel_id=1, source_target_pairs={{0,1},{1,0},{2,3},{3,2},{4,5},{5,4},{6,7},{7,6},{8,9},{9,8},{10,11... | collective-permute-start | bytes 196616 | tf_op jit(solution)/shard_map/ppermute | solution.py:11
  56.3 13.2 %all-to-all-start.2 = ((bf16[8,64,512]{2,1,0:T(8,128)(2,1)}), bf16[8,64,512]{2,1,0:T(8,128)(2,1)S(1)}, u32[]{:S(2)}, u32[]{:S(2)}) async-start(bf16[8,64,512]{2,1,0:T(8,128)(2,1)} %bitcast.12), calls=%async_computation.2 | async-start | bytes 1048576 | tf_op jit(solution)/shard_map/all_to_all | solution.py:32

commit v3 on v2

v3 whole, which is shorter than its diff:
```python
import functools

import jax
import jax.numpy as jnp
from jax import lax
from jax.experimental import pallas as pl
from jax.experimental.pallas import tpu as pltpu
from jax.sharding import PartitionSpec as P

DL = 2048


def swap(x, axis, k):
    n = lax.axis_size(axis)
    return lax.ppermute(x, axis, [(i, i ^ k) for i in range(n)])


def sum_all(x, axis):
    n = lax.axis_size(axis)
    parts = [swap(x, axis, k) for k in range(1, n)]
    total = x.astype(jnp.float32)
    for part in parts:
        total = total + part.astype(jnp.float32)
    return total


def gather_columns(x, axis):
    n = lax.axis_size(axis)
    me = lax.axis_index(axis)
    parts = jnp.stack([x] + [swap(x, axis, k) for k in range(1, n)])
    ordered = [lax.dynamic_index_in_dim(parts, me ^ i, 0, keepdims=False) for i in range(n)]
    return jnp.concatenate(ordered, axis=1)


def exchange(x):
    return lax.all_to_all(x, "batch", split_axis=0, concat_axis=0, tiled=True)


def gather_chips(x, axis):
    n = lax.axis_size(axis)
    return jnp.concatenate([x] + [swap(x, axis, k) for k in range(2, n, 2)], axis=0)


def pick_rows(wanted_ref, rows_ref, out_ref):
    owners, capacity = wanted_ref.shape[0], wanted_ref.shape[2]
    stored = rows_ref.shape[0]
    listed = wanted_ref[...].reshape(owners, capacity).T
    places = lax.broadcasted_iota(jnp.int32, (capacity, stored), 1)
    chosen = jnp.concatenate(
        [(listed[:, d : d + 1] == places).astype(jnp.bfloat16) for d in range(owners)], axis=0
    )
    out_ref[...] = jnp.dot(chosen, rows_ref[...], preferred_element_type=jnp.float32).astype(
        jnp.bfloat16
    )


def add_rows(
    latents,
    me_ref,
    wanted_ref,
    sent_ref,
    even_targets_ref,
    odd_targets_ref,
    even_grads_ref,
    odd_grads_ref,
    out_ref,
    left_ref,
    right_ref,
):
    owners, capacity = wanted_ref.shape[0], wanted_ref.shape[2]
    stored = out_ref.shape[0]
    members = even_grads_ref.shape[0] // (owners // 2)
    half = members // 2
    share = half // latents
    places = lax.broadcasted_iota(jnp.int32, (stored, capacity), 0)
    me = me_ref[0]

    def unpack(x):
        return jnp.concatenate([x[:, :capacity], x[:, capacity:]], axis=0)

    for k in range(owners):
        d = me ^ k
        block = sent_ref[pl.ds(d * latents, latents)]
        slope = block[0, :half]
        for z in range(1, latents):
            slope = slope + block[z, :half]
        weight = jnp.concatenate([block[z, half : half + share] for z in range(latents)], axis=0)
        factor = jnp.concatenate([unpack(weight), unpack(slope)], axis=0)
        high = factor.astype(jnp.bfloat16)
        low = (factor - high.astype(jnp.float32)).astype(jnp.bfloat16)
        chosen = (wanted_ref[d] == places).astype(jnp.bfloat16)
        spread = lax.dot_general(
            chosen,
            jnp.concatenate([high, low], axis=0),
            (((1,), (1,)), ((), ())),
            preferred_element_type=jnp.float32,
        )
        depth = 4 * members
        left_ref[:, k * depth : (k + 1) * depth] = spread.astype(jnp.bfloat16)
        grads_ref, targets_ref = (
            (odd_grads_ref, odd_targets_ref) if k % 2 else (even_grads_ref, even_targets_ref)
        )
        piece = pl.ds((k // 2) * members, members)
        for twice in range(2):
            at = k * depth + twice * 2 * members
            right_ref[at : at + members, :] = grads_ref[piece, :]
            right_ref[at + members : at + 2 * members, :] = targets_ref[piece, :]
    out_ref[...] = jnp.dot(left_ref[...], right_ref[...], preferred_element_type=jnp.float32)


def on_device(rows, targets, w_up, bias, history, requests, upstream):
    score_scale = DL ** (-0.5)
    owners = lax.axis_size("batch")
    latents = lax.axis_size("latent")
    latent = lax.axis_index("latent")
    capacity = requests.shape[1]
    slot_count = owners * capacity
    members, row_width = targets.shape
    stored = rows.shape[0]
    hidden_share = upstream.shape[1]
    half = members // 2
    whole = pl.BlockSpec(memory_space=pltpu.VMEM)
    params = pltpu.CompilerParams(vmem_limit_bytes=32 * 1024 * 1024)

    wanted = exchange(requests.reshape(owners, 1, capacity))
    chosen = pl.pallas_call(
        pick_rows,
        out_shape=jax.ShapeDtypeStruct((slot_count, row_width), jnp.bfloat16),
        in_specs=[whole, whole],
        out_specs=whole,
        compiler_params=params,
        name="pick_rows",
    )(wanted, rows)
    fetched = exchange(chosen.reshape(owners, capacity, row_width)).reshape(slot_count, row_width)

    slots = lax.broadcasted_iota(jnp.int32, (1, 1, slot_count), 2)
    count = jnp.sum((history[:, :, None] == slots).astype(jnp.float32), axis=1)
    upstream_full = gather_columns(upstream, "latent")
    even_targets = gather_chips(targets, "batch")
    odd_targets = swap(even_targets, "batch", 1)
    fetched, count, upstream_full, even_targets, odd_targets = lax.optimization_barrier(
        (fetched, count, upstream_full, even_targets, odd_targets)
    )

    slot_scores = jnp.einsum("ud,sd->us", targets, fetched, preferred_element_type=jnp.float32)
    scores = sum_all(slot_scores, "latent") * score_scale
    top = jnp.max(jnp.where(count > 0, scores, -jnp.inf), axis=1, keepdims=True)
    raised = jnp.where(count > 0, count * jnp.exp(scores - top), 0.0)
    weight = raised / jnp.sum(raised, axis=1, keepdims=True)

    def pack(x):
        return (
            x.reshape(2, half, owners, capacity)
            .transpose(2, 1, 0, 3)
            .reshape(owners, half, 2 * capacity)
        )

    share = half // latents
    weight_share = lax.dynamic_slice_in_dim(pack(weight), latent * share, share, axis=1)

    pooled = jnp.dot(
        weight.astype(jnp.bfloat16), fetched, preferred_element_type=jnp.float32
    ).astype(jnp.bfloat16)
    partial_hidden = jnp.dot(pooled, w_up, preferred_element_type=jnp.float32)
    hidden = sum_all(partial_hidden.astype(jnp.bfloat16), "latent") + bias
    activated, backward = jax.vjp(jax.nn.gelu, hidden)
    output = lax.dynamic_slice_in_dim(
        activated.astype(jnp.bfloat16), latent * hidden_share, hidden_share, axis=1
    )
    slopes = backward(upstream_full.astype(jnp.float32))[0].astype(jnp.bfloat16)
    pooled_grad = jnp.einsum(
        "uh,dh->ud", slopes, w_up, preferred_element_type=jnp.float32
    ).astype(jnp.bfloat16)
    slot_slopes = jnp.einsum(
        "ud,sd->us", pooled_grad, fetched, preferred_element_type=jnp.float32
    )
    part = weight * (slot_slopes - jnp.sum(weight * slot_slopes, axis=1, keepdims=True))
    sending = jnp.concatenate([pack(part * score_scale), weight_share], axis=1)
    sent = lax.all_to_all(
        jnp.broadcast_to(sending[:, None], (owners, latents) + sending.shape[1:]).reshape(
            owners * latents, half + share, 2 * capacity
        ),
        ("batch", "latent"),
        split_axis=0,
        concat_axis=0,
        tiled=True,
    )
    even_grads = gather_chips(pooled_grad, "batch")
    odd_grads = swap(even_grads, "batch", 1)
    depth = owners * 4 * members
    row_grad = pl.pallas_call(
        functools.partial(add_rows, latents),
        out_shape=jax.ShapeDtypeStruct((stored, row_width), jnp.float32),
        in_specs=[pl.BlockSpec(memory_space=pltpu.SMEM)] + [whole] * 6,
        out_specs=whole,
        scratch_shapes=[
            pltpu.VMEM((stored, depth), jnp.bfloat16),
            pltpu.VMEM((depth, row_width), jnp.bfloat16),
        ],
        compiler_params=params,
        name="add_rows",
    )(
        lax.axis_index("batch").reshape(1).astype(jnp.int32),
        wanted,
        sent,
        even_targets,
        odd_targets,
        even_grads,
        odd_grads,
    )
    return (output, row_grad)


def solution(mesh):
    return jax.shard_map(
        on_device,
        mesh=mesh,
        in_specs=(
            P("batch", "latent"),
            P("batch", "latent"),
            P("latent", None),
            P(),
            P("batch", None),
            P("batch", None),
            P("batch", "latent"),
        ),
        out_specs=(P("batch", "latent"), P("batch", "latent")),
        check_vma=False,
    )
```

time: 71.5 us -> 76.6 us (1.071); the launches traced: 71 us -> 75.2 us
  matrix products: 7.8 us -> 1.48 us
  starting transfers between devices: 30.1 us -> 34 us
  Pallas kernels: 0 us -> 3.4 us
  local copies, waits for them, and re-layouts: 0.63 us -> 3.28 us
    all_to_all x3 -> x2, waiting for transfers between devices: 14.4 us -> 0.01 us  [exchange(): return lax.all_to_all(x, 'batch', split_axis=0, concat_axis=0, tiled=True)]
    ppermute x12 -> x17, waiting for transfers between devices: 10.7 us -> 22.4 us  [swap(): return lax.ppermute(x, axis, [(i, i ^ k) for i in range(n)])]
    dot_general x5 -> x1, matrix products: 6.7 us -> 0.38 us  [on_device(): jnp.einsum('ud,sd->us', pooled_grad, fetched, preferred_element_type=jnp....]
    ppermute x12 -> x17, starting transfers between devices: 17.4 us -> 23.2 us  [swap(): return lax.ppermute(x, axis, [(i, i ^ k) for i in range(n)])]
    all_to_all x3 -> x2, starting transfers between devices: 12.7 us -> 7.43 us  [exchange(): return lax.all_to_all(x, 'batch', split_axis=0, concat_axis=0, tiled=True)]
    pallas_call x0 -> x2, Pallas kernels: none -> 3.4 us  [the longest x1 2.06 us: on_device(): pl.pallas_call(functools.partial(add_rows, latents), out_shape=jax.ShapeD...]
    all_to_all x0 -> x1, starting transfers between devices: none -> 3.31 us  [on_device(): lax.all_to_all(jnp.broadcast_to(sending[:, None], (owners, latents) + sen...]
    all_to_all x0 -> x1, waiting for transfers between devices: none -> 2.64 us  [on_device(): lax.all_to_all(jnp.broadcast_to(sending[:, None], (owners, latents) + sen...]
  transfers between devices with their start and end apart: 15 -> 20, of which waited for: 9 -> 10; matrix products, arithmetic and copies ran while one was open for 14% -> 10% of each run, Pallas kernels for 0% -> 2%
where the time goes in v3:
time: 76.6 us; the launch traced here: 75.2 us
  starting transfers between devices  34 us (44%)
  waiting for transfers between devices  25 us (33%)
  other arithmetic  7.18 us (9%)
  Pallas kernels  3.4 us (4%)
  local copies, waits for them, and re-layouts  3.28 us (4%)
  matrix products  1.48 us (2%)
  between operations  0.83 us (1%)
    ppermute x17, starting transfers between devices, swap(): return lax.ppermute(x, axis, [(i, i ^ k) for i in range(n)])  23.2 us
    ppermute x17, waiting for transfers between devices, swap(): return lax.ppermute(x, axis, [(i, i ^ k) for i in range(n)])  22.4 us
    all_to_all x2, starting transfers between devices, exchange(): return lax.all_to_all(x, 'batch', split_axis=0, concat_axis=0, tiled=True)  7.43 us
    reduce_sum x1, other arithmetic, on_device(): count = jnp.sum((history[:, :, None] == slots).astype(jnp.float32), axis=1)  5.94 us
    all_to_all x1, starting transfers between devices, on_device(): lax.all_to_all(jnp.broadcast_to(sending[:, None], (owners, latents) + sen...  3.31 us
    all_to_all x1, waiting for transfers between devices, on_device(): lax.all_to_all(jnp.broadcast_to(sending[:, None], (owners, latents) + sen...  2.64 us
    pallas_call x1, Pallas kernels, on_device(): pl.pallas_call(functools.partial(add_rows, latents), out_shape=jax.ShapeD...  2.06 us
    unnamed x13, local copies, waits for them, and re-layouts  1.83 us
  transfers between devices with their start and end apart: 20, of which 10 were waited for; matrix products, arithmetic and copies ran while one was open for 10% of the time, Pallas kernels for 2%

profile of v3, /device:TPU:0, one launch (start us, length us, event | category | flops | bytes accessed | tf_op | source)
XLA Modules:
  0.0 75.2 jit_solution(832525533875647432)
XLA Ops:
  0.6 3.1 %collective-permute-start = (bf16[32,256]{1,0:T(8,128)(2,1)}, bf16[32,256]{1,0:T(8,128)(2,1)S(1)}, u32[]{:S(2)}, u32[]{:S(2)}) collective-permute-start(bf16[32,256]{1,0:T(8,128)(2,1)} %param.13), channel_id=1, source_target_pairs={{0,1},{1,0},{2,3},{3,2},{4,5},{5,4},{6,7},{7,6},{8,9},{9,8},{10,11... | collective-permute-start | bytes 49160 | tf_op jit(solution)/shard_map/ppermute | solution.py:15
  3.7 2.5 %collective-permute-start.2 = (bf16[32,256]{1,0:T(8,128)(2,1)}, bf16[32,256]{1,0:T(8,128)(2,1)S(1)}, u32[]{:S(2)}, u32[]{:S(2)}) collective-permute-start(bf16[32,256]{1,0:T(8,128)(2,1)} %param.13), channel_id=1, source_target_pairs={{0,3},{1,2},{2,1},{3,0},{4,7},{5,6},{6,5},{7,4},{8,11},{9,10},{10,... | collective-permute-start | bytes 49160 | tf_op jit(solution)/shard_map/ppermute | solution.py:15
  6.2 0.1 collective-permute-start.1
  6.3 2.4 %collective-permute-start.5 = (bf16[32,512]{1,0:T(8,128)(2,1)}, bf16[32,512]{1,0:T(8,128)(2,1)S(1)}, u32[]{:S(2)}, u32[]{:S(2)}) collective-permute-start(bf16[32,512]{1,0:T(8,128)(2,1)} %param.8), channel_id=1, source_target_pairs={{0,24},{4,28},{8,16},{12,20},{16,8},{20,12},{24,0},{28,4},{1,25},{... | collective-permute-start | bytes 98312 | tf_op jit(solution)/shard_map/ppermute | solution.py:15
  8.8 0.5 collective-permute-start.4
  9.3 3.3 %all-to-all-start = ((s32[8,1,64]{2,1,0:T(1,128)}), s32[8,1,64]{2,1,0:T(1,128)S(1)}, u32[]{:S(2)}, u32[]{:S(2)}) async-start(s32[8,1,64]{2,1,0:T(1,128)} %bitcast.41), calls=%async_computation | async-start | bytes 8192 | tf_op jit(solution)/shard_map/all_to_all | solution.py:36
  12.6 5.9 %convert_reduce_fusion = f32[32,512]{1,0:T(8,128)S(1)} fusion(s32[32,512]{1,0:T(8,128)} %param.11), kind=kLoop, calls=%fused_computation | loop fusion | flops 25149440 | bytes 131072 | tf_op jit(solution)/shard_map/reduce_sum | solution.py:137
  18.5 0.8 %constant_dynamic-update-slice_fusion.3 = bf16[128,512]{1,0:T(8,128)(2,1)S(1)} fusion(bf16[32,512]{1,0:T(8,128)(2,1)} %param.8), kind=kLoop, calls=%fused_computation.51 | loop fusion | bytes 65536
  19.3 1.0 %copy-done.1 = bf16[512,512]{1,0:T(8,128)(2,1)S(1)} copy-done((bf16[512,512]{1,0:T(8,128)(2,1)S(1)}, bf16[512,512]{1,0:T(8,128)(2,1)}, u32[]{:S(2)}) %copy-start.1) | copy-done | bytes 524312
  20.4 1.3 %pick_rows.1 = bf16[512,512]{1,0:T(8,128)(2,1)} custom-call(s32[8,1,64]{2,1,0:T(1,128)S(1)} %all-to-all-done.wanted_ref, bf16[512,512]{1,0:T(8,128)(2,1)S(1)} %copy-done.1), custom_call_target="tpu_custom_call" | custom-call | tf_op jit(solution)/shard_map/pick_rows/pallas_call | solution.py:126
  21.7 4.1 %all-to-all-start.1 = ((bf16[8,64,512]{2,1,0:T(8,128)(2,1)}), bf16[8,64,512]{2,1,0:T(8,128)(2,1)S(1)}, u32[]{:S(2)}, u32[]{:S(2)}) async-start(bf16[8,64,512]{2,1,0:T(8,128)(2,1)} %bitcast.1), calls=%async_computation.1 | async-start | bytes 1048576 | tf_op jit(solution)/shard_map/all_to_all | solution.py:36
  25.9 2.1 %collective-permute-start.3 = (bf16[32,512]{1,0:T(8,128)(2,1)S(1)}, bf16[32,512]{1,0:T(8,128)(2,1)S(1)}, u32[]{:S(2)}, u32[]{:S(2)}) collective-permute-start(bf16[32,512]{1,0:T(8,128)(2,1)S(1)} %copy-done.2), channel_id=1, source_target_pairs={{0,8},{4,12},{8,0},{12,4},{16,24},{20,28},{24,16},{28,20},{1,9},{5... | collective-permute-start | bytes 98312 | tf_op jit(solution)/shard_map/ppermute | solution.py:15
  28.0 7.4 %collective-permute-done.3 = bf16[32,512]{1,0:T(8,128)(2,1)S(1)} collective-permute-done((bf16[32,512]{1,0:T(8,128)(2,1)S(1)}, bf16[32,512]{1,0:T(8,128)(2,1)S(1)}, u32[]{:S(2)}, u32[]{:S(2)}) %collective-permute-start.3) | collective-permute-done | bytes 32800 | tf_op jit(solution)/shard_map/ppermute | solution.py:15
  35.5 1.3 %collective-permute-done.6.odd_targets_ref = bf16[128,512]{1,0:T(8,128)(2,1)S(1)} collective-permute-done((bf16[128,512]{1,0:T(8,128)(2,1)S(1)}, bf16[128,512]{1,0:T(8,128)(2,1)S(1)}, u32[]{:S(2)}, u32[]{:S(2)}) %collective-permute-start.6) | collective-permute-done | bytes 131104 | tf_op jit(solution)/shard_map/ppermute | solution.py:15
  36.8 0.2 convolution_bitcast_fusion
  37.1 2.9 %collective-permute-start.9 = (f32[32,512]{1,0:T(8,128)S(1)}, f32[32,512]{1,0:T(8,128)S(1)}, u32[]{:S(2)}, u32[]{:S(2)}) collective-permute-start(f32[32,512]{1,0:T(8,128)S(1)} %convolution_bitcast_fusion), channel_id=1, source_target_pairs={{0,3},{1,2},{2,1},{3,0},{4,7},{5,6},{6,5},{7,4},{8,11},{9,10},{10,... | collective-permute-start | bytes 196616 | tf_op jit(solution)/shard_map/ppermute | solution.py:15
  40.0 0.3 collective-permute-start.8
  40.4 1.1 %collective-permute-start.7 = (f32[32,512]{1,0:T(8,128)S(1)}, f32[32,512]{1,0:T(8,128)S(1)}, u32[]{:S(2)}, u32[]{:S(2)}) collective-permute-start(f32[32,512]{1,0:T(8,128)S(1)} %convolution_bitcast_fusion), channel_id=1, source_target_pairs={{0,1},{1,0},{2,3},{3,2},{4,5},{5,4},{6,7},{7,6},{8,9},{9,8},{10,11... | collective-permute-start | bytes 196616 | tf_op jit(solution)/shard_map/ppermute | solution.py:15
  41.5 1.8 %collective-permute-done.9 = f32[32,512]{1,0:T(8,128)S(1)} collective-permute-done((f32[32,512]{1,0:T(8,128)S(1)}, f32[32,512]{1,0:T(8,128)S(1)}, u32[]{:S(2)}, u32[]{:S(2)}) %collective-permute-start.9) | collective-permute-done | bytes 65568 | tf_op jit(solution)/shard_map/ppermute | solution.py:15
  43.2 3.5 %collective-permute-done.8 = f32[32,512]{1,0:T(8,128)S(1)} collective-permute-done((f32[32,512]{1,0:T(8,128)S(1)}, f32[32,512]{1,0:T(8,128)S(1)}, u32[]{:S(2)}, u32[]{:S(2)}) %collective-permute-start.8) | collective-permute-done | bytes 65568 | tf_op jit(solution)/shard_map/ppermute | solution.py:15
  46.7 0.1 select_reduce_fusion
  46.8 0.2 fusion.26
  47.0 0.1 broadcast_divide_fusion
  47.1 0.4 convolution_convert_fusion
  47.6 2.5 %collective-permute-start.12 = (bf16[32,1024]{1,0:T(8,128)(2,1)S(1)}, bf16[32,1024]{1,0:T(8,128)(2,1)S(1)}, u32[]{:S(2)}, u32[]{:S(2)}) collective-permute-start(bf16[32,1024]{1,0:T(8,128)(2,1)S(1)} %convolution_convert_fusion), channel_id=1, source_target_pairs={{0,3},{1,2},{2,1},{3,0},{4,7},{5,6},{6,5},{7,4},{8,11},{9,10},{10,... | collective-permute-start | bytes 196616 | tf_op jit(solution)/shard_map/ppermute | solution.py:15
  50.1 1.9 %collective-permute-start.10 = (bf16[32,1024]{1,0:T(8,128)(2,1)S(1)}, bf16[32,1024]{1,0:T(8,128)(2,1)S(1)}, u32[]{:S(2)}, u32[]{:S(2)}) collective-permute-start(bf16[32,1024]{1,0:T(8,128)(2,1)S(1)} %convolution_convert_fusion), channel_id=1, source_target_pairs={{0,1},{1,0},{2,3},{3,2},{4,5},{5,4},{6,7},{7,6},{8,9},{9,8},{10,11... | collective-permute-start | bytes 196616 | tf_op jit(solution)/shard_map/ppermute | solution.py:15
  52.0 0.1 reshape.43
  52.1 0.1 copy.15
  52.2 0.1 reshape.44
  52.3 1.5 %collective-permute-done.12 = bf16[32,1024]{1,0:T(8,128)(2,1)S(1)} collective-permute-done((bf16[32,1024]{1,0:T(8,128)(2,1)S(1)}, bf16[32,1024]{1,0:T(8,128)(2,1)S(1)}, u32[]{:S(2)}, u32[]{:S(2)}) %collective-permute-start.12) | collective-permute-done | bytes 65568 | tf_op jit(solution)/shard_map/ppermute | solution.py:15
  53.9 2.0 %collective-permute-done.11 = bf16[32,1024]{1,0:T(8,128)(2,1)S(1)} collective-permute-done((bf16[32,1024]{1,0:T(8,128)(2,1)S(1)}, bf16[32,1024]{1,0:T(8,128)(2,1)S(1)}, u32[]{:S(2)}, u32[]{:S(2)}) %collective-permute-start.11) | collective-permute-done | bytes 65568 | tf_op jit(solution)/shard_map/ppermute | solution.py:15
  55.9 0.1 add_multiply_fusion
  56.0 0.4 convolution_convert_fusion.1
  56.4 0.4 multiply_reduce_fusion
  56.8 0.1 reshape.41
  56.9 0.1 copy.16
  57.0 0.1 reshape.42
  57.2 0.8 %broadcast_in_dim.8 = f32[8,4,20,128]{3,2,1,0:T(8,128)} broadcast(f32[8,20,128]{2,1,0:T(8,128)S(1)} %pad_maximum_fusion.1), dimensions={0,2,3} | broadcast | bytes 409600 | tf_op jit(solution)/shard_map/broadcast_in_dim | solution.py:180
  58.0 3.3 %all-to-all-start.2 = ((f32[32,20,128]{2,1,0:T(8,128)}), f32[32,20,128]{2,1,0:T(8,128)S(1)}, u32[]{:S(2)}, u32[]{:S(2)}) async-start(f32[32,20,128]{2,1,0:T(8,128)} %bitcast.15), calls=%async_computation.2 | async-start | bytes 786432 | tf_op jit(solution)/shard_map/all_to_all | solution.py:179
  61.3 2.7 %collective-permute-start.15 = (bf16[32,512]{1,0:T(8,128)(2,1)S(1)}, bf16[32,512]{1,0:T(8,128)(2,1)S(1)}, u32[]{:S(2)}, u32[]{:S(2)}) collective-permute-start(bf16[32,512]{1,0:T(8,128)(2,1)S(1)} %convolution_convert_fusion.1), channel_id=1, source_target_pairs={{0,24},{4,28},{8,16},{12,20},{16,8},{20,12},{24,0},{28,4},{1,25},{... | collective-permute-start | bytes 98312 | tf_op jit(solution)/shard_map/ppermute | solution.py:15
  64.0 0.6 collective-permute-start.14
  64.6 0.3 collective-permute-start.13
  64.8 3.2 %collective-permute-done.15 = bf16[32,512]{1,0:T(8,128)(2,1)S(1)} collective-permute-done((bf16[32,512]{1,0:T(8,128)(2,1)S(1)}, bf16[32,512]{1,0:T(8,128)(2,1)S(1)}, u32[]{:S(2)}, u32[]{:S(2)}) %collective-permute-start.15) | collective-permute-done | bytes 32800 | tf_op jit(solution)/shard_map/ppermute | solution.py:15
  68.1 1.0 %collective-permute-done.14 = bf16[32,512]{1,0:T(8,128)(2,1)S(1)} collective-permute-done((bf16[32,512]{1,0:T(8,128)(2,1)S(1)}, bf16[32,512]{1,0:T(8,128)(2,1)S(1)}, u32[]{:S(2)}, u32[]{:S(2)}) %collective-permute-start.14) | collective-permute-done | bytes 32800 | tf_op jit(solution)/shard_map/ppermute | solution.py:15
  69.1 0.6 fusion.17
  69.8 0.7 collective-permute-done.16.odd_grads_ref
  70.5 2.6 %all-to-all-done.2.sent_ref = f32[32,20,128]{2,1,0:T(8,128)S(1)} async-done(((f32[32,20,128]{2,1,0:T(8,128)}), f32[32,20,128]{2,1,0:T(8,128)S(1)}, u32[]{:S(2)}, u32[]{:S(2)}) %all-to-all-start.2) | async-done | bytes 327712 | tf_op jit(solution)/shard_map/all_to_all | solution.py:179
  73.1 2.1 %add_rows.1 = f32[512,512]{1,0:T(8,128)} custom-call(s32[1]{0:T(128)} %bitcast.12.me_ref, s32[8,1,64]{2,1,0:T(1,128)S(1)} %all-to-all-done.wanted_ref, f32[32,20,128]{2,1,0:T(8,128)S(1)} %all-to-all-done.2.sent_ref, bf16[128,512]{1,0:T(8,128)(2,1)S(1)} %constant_dynamic-update-slice_fusion.even_targets_ref, ...), custom_call_target="tpu_custom_call" | custom-call | tf_op jit(solution)/shard_map/add_rows/pallas_call | solution.py:191
  (32 shorter events, 0.3 us)
Async XLA Ops:
  0.6 46.5 %copy-start = (bf16[512,1024]{1,0:T(8,128)(2,1)S(1)}, bf16[512,1024]{1,0:T(8,128)(2,1)}, u32[]{:S(2)}) copy-start(bf16[512,1024]{1,0:T(8,128)(2,1)} %param.9) | copy-start | bytes 3145732
  0.6 25.2 %collective-permute-start = (bf16[32,256]{1,0:T(8,128)(2,1)}, bf16[32,256]{1,0:T(8,128)(2,1)S(1)}, u32[]{:S(2)}, u32[]{:S(2)}) collective-permute-start(bf16[32,256]{1,0:T(8,128)(2,1)} %param.13), channel_id=1, source_target_pairs={{0,1},{1,0},{2,3},{3,2},{4,5},{5,4},{6,7},{7,6},{8,9},{9,8},{10,11... | collective-permute-start | bytes 49160 | tf_op jit(solution)/shard_map/ppermute | solution.py:15
  3.7 24.2 %collective-permute-start.2 = (bf16[32,256]{1,0:T(8,128)(2,1)}, bf16[32,256]{1,0:T(8,128)(2,1)S(1)}, u32[]{:S(2)}, u32[]{:S(2)}) collective-permute-start(bf16[32,256]{1,0:T(8,128)(2,1)} %param.13), channel_id=1, source_target_pairs={{0,3},{1,2},{2,1},{3,0},{4,7},{5,6},{6,5},{7,4},{8,11},{9,10},{10,... | collective-permute-start | bytes 49160 | tf_op jit(solution)/shard_map/ppermute | solution.py:15
  6.2 21.7 %collective-permute-start.1 = (bf16[32,256]{1,0:T(8,128)(2,1)}, bf16[32,256]{1,0:T(8,128)(2,1)S(1)}, u32[]{:S(2)}, u32[]{:S(2)}) collective-permute-start(bf16[32,256]{1,0:T(8,128)(2,1)} %param.13), channel_id=1, source_target_pairs={{0,2},{1,3},{2,0},{3,1},{4,6},{5,7},{6,4},{7,5},{8,10},{9,11},{10,... | collective-permute-start | bytes 49160 | tf_op jit(solution)/shard_map/ppermute | solution.py:15
  6.3 29.1 %collective-permute-start.5 = (bf16[32,512]{1,0:T(8,128)(2,1)}, bf16[32,512]{1,0:T(8,128)(2,1)S(1)}, u32[]{:S(2)}, u32[]{:S(2)}) collective-permute-start(bf16[32,512]{1,0:T(8,128)(2,1)} %param.8), channel_id=1, source_target_pairs={{0,24},{4,28},{8,16},{12,20},{16,8},{20,12},{24,0},{28,4},{1,25},{... | collective-permute-start | bytes 98312 | tf_op jit(solution)/shard_map/ppermute | solution.py:15
  8.8 26.6 %collective-permute-start.4 = (bf16[32,512]{1,0:T(8,128)(2,1)}, bf16[32,512]{1,0:T(8,128)(2,1)S(1)}, u32[]{:S(2)}, u32[]{:S(2)}) collective-permute-start(bf16[32,512]{1,0:T(8,128)(2,1)} %param.8), channel_id=1, source_target_pairs={{0,16},{4,20},{8,24},{12,28},{16,0},{20,4},{24,8},{28,12},{1,17},{... | collective-permute-start | bytes 98312 | tf_op jit(solution)/shard_map/ppermute | solution.py:15
  9.3 10.0 %all-to-all-start = ((s32[8,1,64]{2,1,0:T(1,128)}), s32[8,1,64]{2,1,0:T(1,128)S(1)}, u32[]{:S(2)}, u32[]{:S(2)}) async-start(s32[8,1,64]{2,1,0:T(1,128)} %bitcast.41), calls=%async_computation | async-start | bytes 8192 | tf_op jit(solution)/shard_map/all_to_all | solution.py:36
  19.3 1.0 %copy-start.1 = (bf16[512,512]{1,0:T(8,128)(2,1)S(1)}, bf16[512,512]{1,0:T(8,128)(2,1)}, u32[]{:S(2)}) copy-start(bf16[512,512]{1,0:T(8,128)(2,1)} %rows_ref.1) | copy-start | bytes 1572868
  20.4 5.5 %copy-start.2 = (bf16[32,512]{1,0:T(8,128)(2,1)S(1)}, bf16[32,512]{1,0:T(8,128)(2,1)}, u32[]{:S(2)}) copy-start(bf16[32,512]{1,0:T(8,128)(2,1)} %param.8) | copy-start | bytes 98308
  20.4 7.6 %copy-start.3 = (bf16[32,256]{1,0:T(8,128)(2,1)S(1)}, bf16[32,256]{1,0:T(8,128)(2,1)}, u32[]{:S(2)}) copy-start(bf16[32,256]{1,0:T(8,128)(2,1)} %param.13) | copy-start | bytes 49156
  21.7 15.1 %all-to-all-start.1 = ((bf16[8,64,512]{2,1,0:T(8,128)(2,1)}), bf16[8,64,512]{2,1,0:T(8,128)(2,1)S(1)}, u32[]{:S(2)}, u32[]{:S(2)}) async-start(bf16[8,64,512]{2,1,0:T(8,128)(2,1)} %bitcast.1), calls=%async_computation.1 | async-start | bytes 1048576 | tf_op jit(solution)/shard_map/all_to_all | solution.py:36
  25.9 9.5 %collective-permute-start.3 = (bf16[32,512]{1,0:T(8,128)(2,1)S(1)}, bf16[32,512]{1,0:T(8,128)(2,1)S(1)}, u32[]{:S(2)}, u32[]{:S(2)}) collective-permute-start(bf16[32,512]{1,0:T(8,128)(2,1)S(1)} %copy-done.2), channel_id=1, source_target_pairs={{0,8},{4,12},{8,0},{12,4},{16,24},{20,28},{24,16},{28,20},{1,9},{5... | collective-permute-start | bytes 98312 | tf_op jit(solution)/shard_map/ppermute | solution.py:15
  35.4 1.4 %collective-permute-start.6 = (bf16[128,512]{1,0:T(8,128)(2,1)S(1)}, bf16[128,512]{1,0:T(8,128)(2,1)S(1)}, u32[]{:S(2)}, u32[]{:S(2)}) collective-permute-start(bf16[128,512]{1,0:T(8,128)(2,1)S(1)} %constant_dynamic-update-slice_fusion.even_targets_ref), channel_id=1, source_target_pairs={{0,4},{4,0},{8,12},{12,8},{16,20},{20,16},{24,28},{28,24},{1,5},{5... | collective-permute-start | bytes 393224 | tf_op jit(solution)/shard_map/ppermute | solution.py:15
  37.1 6.2 %collective-permute-start.9 = (f32[32,512]{1,0:T(8,128)S(1)}, f32[32,512]{1,0:T(8,128)S(1)}, u32[]{:S(2)}, u32[]{:S(2)}) collective-permute-start(f32[32,512]{1,0:T(8,128)S(1)} %convolution_bitcast_fusion), channel_id=1, source_target_pairs={{0,3},{1,2},{2,1},{3,0},{4,7},{5,6},{6,5},{7,4},{8,11},{9,10},{10,... | collective-permute-start | bytes 196616 | tf_op jit(solution)/shard_map/ppermute | solution.py:15
  40.0 6.7 %collective-permute-start.8 = (f32[32,512]{1,0:T(8,128)S(1)}, f32[32,512]{1,0:T(8,128)S(1)}, u32[]{:S(2)}, u32[]{:S(2)}) collective-permute-start(f32[32,512]{1,0:T(8,128)S(1)} %convolution_bitcast_fusion), channel_id=1, source_target_pairs={{0,2},{1,3},{2,0},{3,1},{4,6},{5,7},{6,4},{7,5},{8,10},{9,11},{10,... | collective-permute-start | bytes 196616 | tf_op jit(solution)/shard_map/ppermute | solution.py:15
  40.4 6.3 %collective-permute-start.7 = (f32[32,512]{1,0:T(8,128)S(1)}, f32[32,512]{1,0:T(8,128)S(1)}, u32[]{:S(2)}, u32[]{:S(2)}) collective-permute-start(f32[32,512]{1,0:T(8,128)S(1)} %convolution_bitcast_fusion), channel_id=1, source_target_pairs={{0,1},{1,0},{2,3},{3,2},{4,5},{5,4},{6,7},{7,6},{8,9},{9,8},{10,11... | collective-permute-start | bytes 196616 | tf_op jit(solution)/shard_map/ppermute | solution.py:15
  47.1 8.7 %copy-start.4 = (f32[1024]{0:T(1024)S(1)}, f32[1024]{0:T(1024)}, u32[]{:S(2)}) copy-start(f32[1024]{0:T(1024)} %param.10) | copy-start | bytes 12292
  47.6 6.3 %collective-permute-start.12 = (bf16[32,1024]{1,0:T(8,128)(2,1)S(1)}, bf16[32,1024]{1,0:T(8,128)(2,1)S(1)}, u32[]{:S(2)}, u32[]{:S(2)}) collective-permute-start(bf16[32,1024]{1,0:T(8,128)(2,1)S(1)} %convolution_convert_fusion), channel_id=1, source_target_pairs={{0,3},{1,2},{2,1},{3,0},{4,7},{5,6},{6,5},{7,4},{8,11},{9,10},{10,... | collective-permute-start | bytes 196616 | tf_op jit(solution)/shard_map/ppermute | solution.py:15
  50.1 5.7 %collective-permute-start.11 = (bf16[32,1024]{1,0:T(8,128)(2,1)S(1)}, bf16[32,1024]{1,0:T(8,128)(2,1)S(1)}, u32[]{:S(2)}, u32[]{:S(2)}) collective-permute-start(bf16[32,1024]{1,0:T(8,128)(2,1)S(1)} %convolution_convert_fusion), channel_id=1, source_target_pairs={{0,2},{1,3},{2,0},{3,1},{4,6},{5,7},{6,4},{7,5},{8,10},{9,11},{10,... | collective-permute-start | bytes 196616 | tf_op jit(solution)/shard_map/ppermute | solution.py:15
  50.1 5.7 %collective-permute-start.10 = (bf16[32,1024]{1,0:T(8,128)(2,1)S(1)}, bf16[32,1024]{1,0:T(8,128)(2,1)S(1)}, u32[]{:S(2)}, u32[]{:S(2)}) collective-permute-start(bf16[32,1024]{1,0:T(8,128)(2,1)S(1)} %convolution_convert_fusion), channel_id=1, source_target_pairs={{0,1},{1,0},{2,3},{3,2},{4,5},{5,4},{6,7},{7,6},{8,9},{9,8},{10,11... | collective-permute-start | bytes 196616 | tf_op jit(solution)/shard_map/ppermute | solution.py:15
  58.0 15.1 %all-to-all-start.2 = ((f32[32,20,128]{2,1,0:T(8,128)}), f32[32,20,128]{2,1,0:T(8,128)S(1)}, u32[]{:S(2)}, u32[]{:S(2)}) async-start(f32[32,20,128]{2,1,0:T(8,128)} %bitcast.15), calls=%async_computation.2 | async-start | bytes 786432 | tf_op jit(solution)/shard_map/all_to_all | solution.py:179
  61.3 6.8 %collective-permute-start.15 = (bf16[32,512]{1,0:T(8,128)(2,1)S(1)}, bf16[32,512]{1,0:T(8,128)(2,1)S(1)}, u32[]{:S(2)}, u32[]{:S(2)}) collective-permute-start(bf16[32,512]{1,0:T(8,128)(2,1)S(1)} %convolution_convert_fusion.1), channel_id=1, source_target_pairs={{0,24},{4,28},{8,16},{12,20},{16,8},{20,12},{24,0},{28,4},{1,25},{... | collective-permute-start | bytes 98312 | tf_op jit(solution)/shard_map/ppermute | solution.py:15
  64.0 5.0 %collective-permute-start.14 = (bf16[32,512]{1,0:T(8,128)(2,1)S(1)}, bf16[32,512]{1,0:T(8,128)(2,1)S(1)}, u32[]{:S(2)}, u32[]{:S(2)}) collective-permute-start(bf16[32,512]{1,0:T(8,128)(2,1)S(1)} %convolution_convert_fusion.1), channel_id=1, source_target_pairs={{0,16},{4,20},{8,24},{12,28},{16,0},{20,4},{24,8},{28,12},{1,17},{... | collective-permute-start | bytes 98312 | tf_op jit(solution)/shard_map/ppermute | solution.py:15
  64.6 4.5 %collective-permute-start.13 = (bf16[32,512]{1,0:T(8,128)(2,1)S(1)}, bf16[32,512]{1,0:T(8,128)(2,1)S(1)}, u32[]{:S(2)}, u32[]{:S(2)}) collective-permute-start(bf16[32,512]{1,0:T(8,128)(2,1)S(1)} %convolution_convert_fusion.1), channel_id=1, source_target_pairs={{0,8},{4,12},{8,0},{12,4},{16,24},{20,28},{24,16},{28,20},{1,9},{5... | collective-permute-start | bytes 98312 | tf_op jit(solution)/shard_map/ppermute | solution.py:15
  69.1 1.4 %collective-permute-start.16 = (bf16[128,512]{1,0:T(8,128)(2,1)S(1)}, bf16[128,512]{1,0:T(8,128)(2,1)S(1)}, u32[]{:S(2)}, u32[]{:S(2)}) collective-permute-start(bf16[128,512]{1,0:T(8,128)(2,1)S(1)} %pad_maximum_fusion.even_grads_ref), channel_id=1, source_target_pairs={{0,4},{4,0},{8,12},{12,8},{16,20},{20,16},{24,28},{28,24},{1,5},{5... | collective-permute-start | bytes 393224 | tf_op jit(solution)/shard_map/ppermute | solution.py:15

commit v4 on v3

--- a/solution.py
+++ b/solution.py
@@ -41,17 +41,28 @@
     return jnp.concatenate([x] + [swap(x, axis, k) for k in range(2, n, 2)], axis=0)
 
 
-def pick_rows(wanted_ref, rows_ref, out_ref):
+def pick_rows(wanted_ref, rows_ref, out_ref, held_ref, sems):
     owners, capacity = wanted_ref.shape[0], wanted_ref.shape[2]
-    stored = rows_ref.shape[0]
+    stored, width = held_ref.shape
+    copies = []
+    for c in range(2):
+        for r in range(2):
+            part = (pl.ds(r * stored // 2, stored // 2), pl.ds(c * width // 2, width // 2))
+            copy = pltpu.make_async_copy(rows_ref.at[part], held_ref.at[part], sems.at[c, r])
+            copy.start()
+            copies.append(copy)
     listed = wanted_ref[...].reshape(owners, capacity).T
     places = lax.broadcasted_iota(jnp.int32, (capacity, stored), 1)
     chosen = jnp.concatenate(
         [(listed[:, d : d + 1] == places).astype(jnp.bfloat16) for d in range(owners)], axis=0
     )
-    out_ref[...] = jnp.dot(chosen, rows_ref[...], preferred_element_type=jnp.float32).astype(
-        jnp.bfloat16
-    )
+    for c in range(2):
+        copies[2 * c].wait()
+        copies[2 * c + 1].wait()
+        columns = pl.ds(c * width // 2, width // 2)
+        out_ref[:, columns] = jnp.dot(
+            chosen, held_ref[:, columns], preferred_element_type=jnp.float32
+        ).astype(jnp.bfloat16)
 
 
 def add_rows(
@@ -59,17 +70,15 @@
     me_ref,
     wanted_ref,
     sent_ref,
-    even_targets_ref,
-    odd_targets_ref,
-    even_grads_ref,
-    odd_grads_ref,
+    even_ref,
+    odd_ref,
     out_ref,
     left_ref,
     right_ref,
 ):
     owners, capacity = wanted_ref.shape[0], wanted_ref.shape[2]
     stored = out_ref.shape[0]
-    members = even_grads_ref.shape[0] // (owners // 2)
+    members = even_ref.shape[0] // owners
     half = members // 2
     share = half // latents
     places = lax.broadcasted_iota(jnp.int32, (stored, capacity), 0)
@@ -97,14 +106,12 @@
         )
         depth = 4 * members
         left_ref[:, k * depth : (k + 1) * depth] = spread.astype(jnp.bfloat16)
-        grads_ref, targets_ref = (
-            (odd_grads_ref, odd_targets_ref) if k % 2 else (even_grads_ref, even_targets_ref)
+        side_ref = odd_ref if k % 2 else even_ref
+        targets = side_ref[pl.ds((k // 2) * members, members), :]
+        grads = side_ref[pl.ds((owners // 2 + k // 2) * members, members), :]
+        right_ref[k * depth : (k + 1) * depth, :] = jnp.concatenate(
+            [grads, targets, grads, targets], axis=0
         )
-        piece = pl.ds((k // 2) * members, members)
-        for twice in range(2):
-            at = k * depth + twice * 2 * members
-            right_ref[at : at + members, :] = grads_ref[piece, :]
-            right_ref[at + members : at + 2 * members, :] = targets_ref[piece, :]
     out_ref[...] = jnp.dot(left_ref[...], right_ref[...], preferred_element_type=jnp.float32)
 
 
@@ -126,24 +133,28 @@
     chosen = pl.pallas_call(
         pick_rows,
         out_shape=jax.ShapeDtypeStruct((slot_count, row_width), jnp.bfloat16),
-        in_specs=[whole, whole],
+        in_specs=[whole, pl.BlockSpec(memory_space=pltpu.HBM)],
         out_specs=whole,
-        compiler_params=params,
+        scratch_shapes=[
+            pltpu.VMEM((stored, row_width), jnp.bfloat16),
+            pltpu.SemaphoreType.DMA((2, 2)),
+        ],
+        compiler_params=pltpu.CompilerParams(vmem_limit_bytes=60 * 1024 * 1024),
         name="pick_rows",
     )(wanted, rows)
-    fetched = exchange(chosen.reshape(owners, capacity, row_width)).reshape(slot_count, row_width)
 
     slots = lax.broadcasted_iota(jnp.int32, (1, 1, slot_count), 2)
     count = jnp.sum((history[:, :, None] == slots).astype(jnp.float32), axis=1)
-    upstream_full = gather_columns(upstream, "latent")
-    even_targets = gather_chips(targets, "batch")
-    odd_targets = swap(even_targets, "batch", 1)
-    fetched, count, upstream_full, even_targets, odd_targets = lax.optimization_barrier(
-        (fetched, count, upstream_full, even_targets, odd_targets)
-    )
+    fetched = exchange(chosen.reshape(owners, capacity, row_width)).reshape(slot_count, row_width)
+    count, late_upstream = lax.optimization_barrier((count, upstream))
+    upstream_full = gather_columns(late_upstream, "latent")
+    fetched, count, upstream_full = lax.optimization_barrier((fetched, count, upstream_full))
 
     slot_scores = jnp.einsum("ud,sd->us", targets, fetched, preferred_element_type=jnp.float32)
-    scores = sum_all(slot_scores, "latent") * score_scale
+    parts = [swap(slot_scores, "latent", k) for k in range(1, latents)]
+    parts[0], late_targets = lax.optimization_barrier((parts[0], targets))
+    even_targets = gather_chips(late_targets, "batch")
+    scores = functools.reduce(jnp.add, parts, slot_scores) * score_scale
     top = jnp.max(jnp.where(count > 0, scores, -jnp.inf), axis=1, keepdims=True)
     raised = jnp.where(count > 0, count * jnp.exp(scores - top), 0.0)
     weight = raised / jnp.sum(raised, axis=1, keepdims=True)
@@ -186,12 +197,13 @@
         tiled=True,
     )
     even_grads = gather_chips(pooled_grad, "batch")
-    odd_grads = swap(even_grads, "batch", 1)
+    even = jnp.concatenate([even_targets, even_grads], axis=0)
+    odd = swap(even, "batch", 1)
     depth = owners * 4 * members
     row_grad = pl.pallas_call(
         functools.partial(add_rows, latents),
         out_shape=jax.ShapeDtypeStruct((stored, row_width), jnp.float32),
-        in_specs=[pl.BlockSpec(memory_space=pltpu.SMEM)] + [whole] * 6,
+        in_specs=[pl.BlockSpec(memory_space=pltpu.SMEM)] + [whole] * 4,
         out_specs=whole,
         scratch_shapes=[
             pltpu.VMEM((stored, depth), jnp.bfloat16),
@@ -203,10 +215,8 @@
         lax.axis_index("batch").reshape(1).astype(jnp.int32),
         wanted,
         sent,
-        even_targets,
-        odd_targets,
-        even_grads,
-        odd_grads,
+        even,
+        odd,
     )
     return (output, row_grad)
 

time: 76.6 us -> 70.3 us (0.918)
  blocking collectives: 0 us -> 9.85 us
  waiting for transfers between devices: 25 us -> 16.2 us
  starting transfers between devices: 34 us -> 28 us
  Pallas kernels: 3.4 us -> 5.4 us
  local copies, waits for them, and re-layouts: 3.28 us -> 1.5 us
  other arithmetic: 7.18 us -> 5.89 us
    all_to_all x0 -> x1, blocking collectives: none -> 9.85 us  [exchange(): return lax.all_to_all(x, 'batch', split_axis=0, concat_axis=0, tiled=True)]
    ppermute x17 -> x16, waiting for transfers between devices: 22.4 us -> 14 us  [swap(): return lax.ppermute(x, axis, [(i, i ^ k) for i in range(n)])]
    all_to_all x2 -> x1, starting transfers between devices: 7.43 us -> 3.51 us  [exchange(): return lax.all_to_all(x, 'batch', split_axis=0, concat_axis=0, tiled=True)]
    ppermute x17 -> x16, starting transfers between devices: 23.2 us -> 19.6 us  [swap(): return lax.ppermute(x, axis, [(i, i ^ k) for i in range(n)])]
    pallas_call x1, Pallas kernels: 1.35 us -> 3.35 us  [on_device(): pl.pallas_call(pick_rows, out_shape=jax.ShapeDtypeStruct((slot_count, row...]
    unnamed x13 -> x18, local copies, waits for them, and re-layouts: 1.83 us -> 0.06 us
    all_to_all x1, starting transfers between devices: 3.31 us -> 4.88 us  [on_device(): lax.all_to_all(jnp.broadcast_to(sending[:, None], (owners, latents) + sen...]
    reduce_sum x1, other arithmetic: 5.94 us -> 4.66 us  [on_device(): count = jnp.sum((history[:, :, None] == slots).astype(jnp.float32), axis=1)]
  transfers between devices with their start and end apart: 20 -> 18, of which waited for: 10 -> 10; matrix products, arithmetic and copies ran while one was open for 10% -> 9% of each run, Pallas kernels for 2% -> 0%
where the time goes in v4:
time: 70.3 us; the launch traced here: 69.1 us
  starting transfers between devices  28 us (40%)
  waiting for transfers between devices  16.2 us (23%)
  blocking collectives  9.85 us (14%)
  other arithmetic  5.89 us (8%)
  Pallas kernels  5.4 us (8%)
  local copies, waits for them, and re-layouts  1.5 us (2%)
  matrix products  1.48 us (2%)
  between operations  0.88 us (1%)
    ppermute x16, starting transfers between devices, swap(): return lax.ppermute(x, axis, [(i, i ^ k) for i in range(n)])  19.6 us
    ppermute x16, waiting for transfers between devices, swap(): return lax.ppermute(x, axis, [(i, i ^ k) for i in range(n)])  14 us
    all_to_all x1, blocking collectives, exchange(): return lax.all_to_all(x, 'batch', split_axis=0, concat_axis=0, tiled=True)  9.85 us
    all_to_all x1, starting transfers between devices, on_device(): lax.all_to_all(jnp.broadcast_to(sending[:, None], (owners, latents) + sen...  4.88 us
    reduce_sum x1, other arithmetic, on_device(): count = jnp.sum((history[:, :, None] == slots).astype(jnp.float32), axis=1)  4.66 us
    all_to_all x1, starting transfers between devices, exchange(): return lax.all_to_all(x, 'batch', split_axis=0, concat_axis=0, tiled=True)  3.51 us
    pallas_call x1, Pallas kernels, on_device(): pl.pallas_call(pick_rows, out_shape=jax.ShapeDtypeStruct((slot_count, row...  3.35 us
    all_to_all x1, waiting for transfers between devices, on_device(): lax.all_to_all(jnp.broadcast_to(sending[:, None], (owners, latents) + sen...  2.16 us
  transfers between devices with their start and end apart: 18, of which 10 were waited for; matrix products, arithmetic and copies ran while one was open for 9% of the time, Pallas kernels for 0%

profile of v4, /device:TPU:0, one launch (start us, length us, event | category | flops | bytes accessed | tf_op | source)
XLA Modules:
  0.0 69.1 jit_solution(8294630041457036575)
XLA Ops:
  0.6 0.0 copy-start
  0.6 9.8 %all_to_all.15.wanted_ref = s32[8,1,64]{2,1,0:T(1,128)} all-to-all(s32[8,1,64]{2,1,0:T(1,128)} %bitcast.42), channel_id=1, replica_groups=mesh['batch'=8,'latent'=4] {'batch'}, dimensions={0} | all-to-all | bytes 4096 | tf_op jit(solution)/shard_map/all_to_all | solution.py:36
  10.5 3.4 %pick_rows.1 = bf16[512,512]{1,0:T(8,128)(2,1)} custom-call(s32[8,1,64]{2,1,0:T(1,128)} %all_to_all.15.wanted_ref, bf16[512,512]{1,0:T(8,128)(2,1)} %rows_ref.1), custom_call_target="tpu_custom_call" | custom-call | tf_op jit(solution)/shard_map/pick_rows/pallas_call | solution.py:133
  13.9 0.0 copy-start.2
  13.9 3.5 %all-to-all-start.1 = ((bf16[8,64,512]{2,1,0:T(8,128)(2,1)}), bf16[8,64,512]{2,1,0:T(8,128)(2,1)S(1)}, u32[]{:S(2)}, u32[]{:S(2)}) async-start(bf16[8,64,512]{2,1,0:T(8,128)(2,1)} %bitcast.35), calls=%async_computation.1 | async-start | bytes 1048576 | tf_op jit(solution)/shard_map/all_to_all | solution.py:36
  17.4 4.7 %convert_reduce_fusion = f32[32,512]{1,0:T(8,128)S(1)} fusion(s32[32,512]{1,0:T(8,128)S(1)} %copy-done.3), kind=kLoop, calls=%fused_computation | loop fusion | flops 25149440 | bytes 131072 | tf_op jit(solution)/shard_map/reduce_sum | solution.py:147
  22.1 3.8 %collective-permute-start.2 = (bf16[32,256]{1,0:T(8,128)(2,1)S(1)}, bf16[32,256]{1,0:T(8,128)(2,1)S(1)}, u32[]{:S(2)}, u32[]{:S(2)}) collective-permute-start(bf16[32,256]{1,0:T(8,128)(2,1)S(1)} %copy-done.4), channel_id=1, source_target_pairs={{0,3},{1,2},{2,1},{3,0},{4,7},{5,6},{6,5},{7,4},{8,11},{9,10},{10,... | collective-permute-start | bytes 49160 | tf_op jit(solution)/shard_map/ppermute | solution.py:15
  25.9 0.7 %collective-permute-start = (bf16[32,256]{1,0:T(8,128)(2,1)S(1)}, bf16[32,256]{1,0:T(8,128)(2,1)S(1)}, u32[]{:S(2)}, u32[]{:S(2)}) collective-permute-start(bf16[32,256]{1,0:T(8,128)(2,1)S(1)} %copy-done.4), channel_id=1, source_target_pairs={{0,1},{1,0},{2,3},{3,2},{4,5},{5,4},{6,7},{7,6},{8,9},{9,8},{10,11... | collective-permute-start | bytes 49160 | tf_op jit(solution)/shard_map/ppermute | solution.py:15
  26.6 1.1 %collective-permute-done.2 = bf16[32,256]{1,0:T(8,128)(2,1)S(1)} collective-permute-done((bf16[32,256]{1,0:T(8,128)(2,1)S(1)}, bf16[32,256]{1,0:T(8,128)(2,1)S(1)}, u32[]{:S(2)}, u32[]{:S(2)}) %collective-permute-start.2) | collective-permute-done | bytes 16416 | tf_op jit(solution)/shard_map/ppermute | solution.py:15
  27.7 2.8 %collective-permute-done.1 = bf16[32,256]{1,0:T(8,128)(2,1)S(1)} collective-permute-done((bf16[32,256]{1,0:T(8,128)(2,1)S(1)}, bf16[32,256]{1,0:T(8,128)(2,1)S(1)}, u32[]{:S(2)}, u32[]{:S(2)}) %collective-permute-start.1) | collective-permute-done | bytes 16416 | tf_op jit(solution)/shard_map/ppermute | solution.py:15
  30.6 0.2 convolution_bitcast_fusion
  30.8 3.5 %collective-permute-start.5 = (f32[32,512]{1,0:T(8,128)S(1)}, f32[32,512]{1,0:T(8,128)S(1)}, u32[]{:S(2)}, u32[]{:S(2)}) collective-permute-start(f32[32,512]{1,0:T(8,128)S(1)} %convolution_bitcast_fusion), channel_id=1, source_target_pairs={{0,3},{1,2},{2,1},{3,0},{4,7},{5,6},{6,5},{7,4},{8,11},{9,10},{10,... | collective-permute-start | bytes 196616 | tf_op jit(solution)/shard_map/ppermute | solution.py:15
  34.3 1.5 %collective-permute-done.3 = f32[32,512]{1,0:T(8,128)S(1)} collective-permute-done((f32[32,512]{1,0:T(8,128)S(1)}, f32[32,512]{1,0:T(8,128)S(1)}, u32[]{:S(2)}, u32[]{:S(2)}) %collective-permute-start.3) | collective-permute-done | bytes 65568 | tf_op jit(solution)/shard_map/ppermute | solution.py:15
  35.8 2.5 %collective-permute-start.11 = (bf16[32,512]{1,0:T(8,128)(2,1)S(1)}, bf16[32,512]{1,0:T(8,128)(2,1)S(1)}, u32[]{:S(2)}, u32[]{:S(2)}) collective-permute-start(bf16[32,512]{1,0:T(8,128)(2,1)S(1)} %copy-done.2), channel_id=1, source_target_pairs={{0,24},{4,28},{8,16},{12,20},{16,8},{20,12},{24,0},{28,4},{1,25},{... | collective-permute-start | bytes 98312 | tf_op jit(solution)/shard_map/ppermute | solution.py:15
  38.3 0.5 collective-permute-start.10
  38.8 0.5 collective-permute-start.9
  39.3 0.2 collective-permute-done.4
  39.5 0.1 select_reduce_fusion
  39.6 0.2 fusion.26
  39.8 0.1 broadcast_divide_fusion
  39.9 0.4 convolution_convert_fusion
  40.4 2.5 %collective-permute-start.8 = (bf16[32,1024]{1,0:T(8,128)(2,1)S(1)}, bf16[32,1024]{1,0:T(8,128)(2,1)S(1)}, u32[]{:S(2)}, u32[]{:S(2)}) collective-permute-start(bf16[32,1024]{1,0:T(8,128)(2,1)S(1)} %convolution_convert_fusion), channel_id=1, source_target_pairs={{0,3},{1,2},{2,1},{3,0},{4,7},{5,6},{6,5},{7,4},{8,11},{9,10},{10,... | collective-permute-start | bytes 196616 | tf_op jit(solution)/shard_map/ppermute | solution.py:15
  42.9 0.1 reshape.43
  43.0 0.1 copy.15
  43.1 0.1 reshape.44
  43.2 2.0 %collective-permute-start.6 = (bf16[32,1024]{1,0:T(8,128)(2,1)S(1)}, bf16[32,1024]{1,0:T(8,128)(2,1)S(1)}, u32[]{:S(2)}, u32[]{:S(2)}) collective-permute-start(bf16[32,1024]{1,0:T(8,128)(2,1)S(1)} %convolution_convert_fusion), channel_id=1, source_target_pairs={{0,1},{1,0},{2,3},{3,2},{4,5},{5,4},{6,7},{7,6},{8,9},{9,8},{10,11... | collective-permute-start | bytes 196616 | tf_op jit(solution)/shard_map/ppermute | solution.py:15
  45.3 1.5 %collective-permute-done.8 = bf16[32,1024]{1,0:T(8,128)(2,1)S(1)} collective-permute-done((bf16[32,1024]{1,0:T(8,128)(2,1)S(1)}, bf16[32,1024]{1,0:T(8,128)(2,1)S(1)}, u32[]{:S(2)}, u32[]{:S(2)}) %collective-permute-start.8) | collective-permute-done | bytes 65568 | tf_op jit(solution)/shard_map/ppermute | solution.py:15
  46.7 1.5 %collective-permute-done.7 = bf16[32,1024]{1,0:T(8,128)(2,1)S(1)} collective-permute-done((bf16[32,1024]{1,0:T(8,128)(2,1)S(1)}, bf16[32,1024]{1,0:T(8,128)(2,1)S(1)}, u32[]{:S(2)}, u32[]{:S(2)}) %collective-permute-start.7) | collective-permute-done | bytes 65568 | tf_op jit(solution)/shard_map/ppermute | solution.py:15
  48.2 0.0 collective-permute-done.6
  48.3 0.1 add_multiply_fusion
  48.3 0.4 constant_dynamic-update-slice_fusion.3
  48.8 0.4 multiply_reduce_fusion
  49.1 0.1 multiply_multiply_fusion.2
  49.2 0.1 reshape.41
  49.3 0.1 copy.16
  49.4 0.1 reshape.42
  49.6 0.8 %broadcast_in_dim.8 = f32[8,4,20,128]{3,2,1,0:T(8,128)} broadcast(f32[8,20,128]{2,1,0:T(8,128)S(1)} %pad_maximum_fusion), dimensions={0,2,3} | broadcast | bytes 409600 | tf_op jit(solution)/shard_map/broadcast_in_dim | solution.py:191
  50.4 4.9 %all-to-all-start.2 = ((f32[32,20,128]{2,1,0:T(8,128)}), f32[32,20,128]{2,1,0:T(8,128)S(1)}, u32[]{:S(2)}, u32[]{:S(2)}) async-start(f32[32,20,128]{2,1,0:T(8,128)} %bitcast.15), calls=%async_computation.2 | async-start | bytes 786432 | tf_op jit(solution)/shard_map/all_to_all | solution.py:190
  55.3 1.8 %collective-permute-start.12 = (bf16[32,512]{1,0:T(8,128)(2,1)S(1)}, bf16[32,512]{1,0:T(8,128)(2,1)S(1)}, u32[]{:S(2)}, u32[]{:S(2)}) collective-permute-start(bf16[32,512]{1,0:T(8,128)(2,1)S(1)} %get-tuple-element.27), channel_id=1, source_target_pairs={{0,8},{4,12},{8,0},{12,4},{16,24},{20,28},{24,16},{28,20},{1,9},{5... | collective-permute-start | bytes 98312 | tf_op jit(solution)/shard_map/ppermute | solution.py:15
  57.1 1.5 %collective-permute-start.14 = (bf16[32,512]{1,0:T(8,128)(2,1)S(1)}, bf16[32,512]{1,0:T(8,128)(2,1)S(1)}, u32[]{:S(2)}, u32[]{:S(2)}) collective-permute-start(bf16[32,512]{1,0:T(8,128)(2,1)S(1)} %get-tuple-element.27), channel_id=1, source_target_pairs={{0,24},{4,28},{8,16},{12,20},{16,8},{20,12},{24,0},{28,4},{1,25},{... | collective-permute-start | bytes 98312 | tf_op jit(solution)/shard_map/ppermute | solution.py:15
  58.5 0.3 collective-permute-start.13
  58.8 2.4 %collective-permute-done.12 = bf16[32,512]{1,0:T(8,128)(2,1)S(1)} collective-permute-done((bf16[32,512]{1,0:T(8,128)(2,1)S(1)}, bf16[32,512]{1,0:T(8,128)(2,1)S(1)}, u32[]{:S(2)}, u32[]{:S(2)}) %collective-permute-start.12) | collective-permute-done | bytes 32800 | tf_op jit(solution)/shard_map/ppermute | solution.py:15
  61.2 2.1 %collective-permute-done.13 = bf16[32,512]{1,0:T(8,128)(2,1)S(1)} collective-permute-done((bf16[32,512]{1,0:T(8,128)(2,1)S(1)}, bf16[32,512]{1,0:T(8,128)(2,1)S(1)}, u32[]{:S(2)}, u32[]{:S(2)}) %collective-permute-start.13) | collective-permute-done | bytes 32800 | tf_op jit(solution)/shard_map/ppermute | solution.py:15
  63.3 0.1 collective-permute-start.15
  63.4 0.6 fusion.17
  64.0 0.9 %collective-permute-done.15.odd_ref = bf16[256,512]{1,0:T(8,128)(2,1)S(1)} collective-permute-done((bf16[256,512]{1,0:T(8,128)(2,1)S(1)}, bf16[256,512]{1,0:T(8,128)(2,1)S(1)}, u32[]{:S(2)}, u32[]{:S(2)}) %collective-permute-start.15) | collective-permute-done | bytes 262176 | tf_op jit(solution)/shard_map/ppermute | solution.py:15
  64.9 2.2 %all-to-all-done.2.sent_ref = f32[32,20,128]{2,1,0:T(8,128)S(1)} async-done(((f32[32,20,128]{2,1,0:T(8,128)}), f32[32,20,128]{2,1,0:T(8,128)S(1)}, u32[]{:S(2)}, u32[]{:S(2)}) %all-to-all-start.2) | async-done | bytes 327712 | tf_op jit(solution)/shard_map/all_to_all | solution.py:190
  67.1 2.0 %add_rows.1 = f32[512,512]{1,0:T(8,128)} custom-call(s32[1]{0:T(128)} %bitcast.12.me_ref, s32[8,1,64]{2,1,0:T(1,128)S(1)} %copy-done.1, f32[32,20,128]{2,1,0:T(8,128)S(1)} %all-to-all-done.2.sent_ref, bf16[256,512]{1,0:T(8,128)(2,1)S(1)} %constant_dynamic-update-slice_fusion.even_ref, bf16[256,512]{1,0:T(8,128)(2,1)S(1)} %collective-permute-done.15.odd_ref), custom_call_target="tpu_custom_call" | custom-call | tf_op jit(solution)/shard_map/add_rows/pallas_call | solution.py:203
  (33 shorter events, 0.1 us)
Async XLA Ops:
  0.6 39.3 %copy-start = (bf16[512,1024]{1,0:T(8,128)(2,1)S(1)}, bf16[512,1024]{1,0:T(8,128)(2,1)}, u32[]{:S(2)}) copy-start(bf16[512,1024]{1,0:T(8,128)(2,1)} %param.9) | copy-start | bytes 3145732
  10.5 6.9 %copy-start.3 = (s32[32,512]{1,0:T(8,128)S(1)}, s32[32,512]{1,0:T(8,128)}, u32[]{:S(2)}) copy-start(s32[32,512]{1,0:T(8,128)} %param.11) | copy-start | bytes 196612
  10.5 11.6 %copy-start.4 = (bf16[32,256]{1,0:T(8,128)(2,1)S(1)}, bf16[32,256]{1,0:T(8,128)(2,1)}, u32[]{:S(2)}) copy-start(bf16[32,256]{1,0:T(8,128)(2,1)} %param.13) | copy-start | bytes 49156
  13.9 16.7 %copy-start.2 = (bf16[32,512]{1,0:T(8,128)(2,1)S(1)}, bf16[32,512]{1,0:T(8,128)(2,1)}, u32[]{:S(2)}) copy-start(bf16[32,512]{1,0:T(8,128)(2,1)} %param.8) | copy-start | bytes 98308
  13.9 16.7 %all-to-all-start.1 = ((bf16[8,64,512]{2,1,0:T(8,128)(2,1)}), bf16[8,64,512]{2,1,0:T(8,128)(2,1)S(1)}, u32[]{:S(2)}, u32[]{:S(2)}) async-start(bf16[8,64,512]{2,1,0:T(8,128)(2,1)} %bitcast.35), calls=%async_computation.1 | async-start | bytes 1048576 | tf_op jit(solution)/shard_map/all_to_all | solution.py:36
  22.1 5.6 %collective-permute-start.2 = (bf16[32,256]{1,0:T(8,128)(2,1)S(1)}, bf16[32,256]{1,0:T(8,128)(2,1)S(1)}, u32[]{:S(2)}, u32[]{:S(2)}) collective-permute-start(bf16[32,256]{1,0:T(8,128)(2,1)S(1)} %copy-done.4), channel_id=1, source_target_pairs={{0,3},{1,2},{2,1},{3,0},{4,7},{5,6},{6,5},{7,4},{8,11},{9,10},{10,... | collective-permute-start | bytes 49160 | tf_op jit(solution)/shard_map/ppermute | solution.py:15
  25.9 4.6 %collective-permute-start.1 = (bf16[32,256]{1,0:T(8,128)(2,1)S(1)}, bf16[32,256]{1,0:T(8,128)(2,1)S(1)}, u32[]{:S(2)}, u32[]{:S(2)}) collective-permute-start(bf16[32,256]{1,0:T(8,128)(2,1)S(1)} %copy-done.4), channel_id=1, source_target_pairs={{0,2},{1,3},{2,0},{3,1},{4,6},{5,7},{6,4},{7,5},{8,10},{9,11},{10,... | collective-permute-start | bytes 49160 | tf_op jit(solution)/shard_map/ppermute | solution.py:15
  25.9 4.6 %collective-permute-start = (bf16[32,256]{1,0:T(8,128)(2,1)S(1)}, bf16[32,256]{1,0:T(8,128)(2,1)S(1)}, u32[]{:S(2)}, u32[]{:S(2)}) collective-permute-start(bf16[32,256]{1,0:T(8,128)(2,1)S(1)} %copy-done.4), channel_id=1, source_target_pairs={{0,1},{1,0},{2,3},{3,2},{4,5},{5,4},{6,7},{7,6},{8,9},{9,8},{10,11... | collective-permute-start | bytes 49160 | tf_op jit(solution)/shard_map/ppermute | solution.py:15
  30.8 5.0 %collective-permute-start.3 = (f32[32,512]{1,0:T(8,128)S(1)}, f32[32,512]{1,0:T(8,128)S(1)}, u32[]{:S(2)}, u32[]{:S(2)}) collective-permute-start(f32[32,512]{1,0:T(8,128)S(1)} %convolution_bitcast_fusion), channel_id=1, source_target_pairs={{0,1},{1,0},{2,3},{3,2},{4,5},{5,4},{6,7},{7,6},{8,9},{9,8},{10,11... | collective-permute-start | bytes 196616 | tf_op jit(solution)/shard_map/ppermute | solution.py:15
  30.8 8.5 %collective-permute-start.5 = (f32[32,512]{1,0:T(8,128)S(1)}, f32[32,512]{1,0:T(8,128)S(1)}, u32[]{:S(2)}, u32[]{:S(2)}) collective-permute-start(f32[32,512]{1,0:T(8,128)S(1)} %convolution_bitcast_fusion), channel_id=1, source_target_pairs={{0,3},{1,2},{2,1},{3,0},{4,7},{5,6},{6,5},{7,4},{8,11},{9,10},{10,... | collective-permute-start | bytes 196616 | tf_op jit(solution)/shard_map/ppermute | solution.py:15
  34.3 5.2 %collective-permute-start.4 = (f32[32,512]{1,0:T(8,128)S(1)}, f32[32,512]{1,0:T(8,128)S(1)}, u32[]{:S(2)}, u32[]{:S(2)}) collective-permute-start(f32[32,512]{1,0:T(8,128)S(1)} %convolution_bitcast_fusion), channel_id=1, source_target_pairs={{0,2},{1,3},{2,0},{3,1},{4,6},{5,7},{6,4},{7,5},{8,10},{9,11},{10,... | collective-permute-start | bytes 196616 | tf_op jit(solution)/shard_map/ppermute | solution.py:15
  35.8 9.4 %collective-permute-start.11 = (bf16[32,512]{1,0:T(8,128)(2,1)S(1)}, bf16[32,512]{1,0:T(8,128)(2,1)S(1)}, u32[]{:S(2)}, u32[]{:S(2)}) collective-permute-start(bf16[32,512]{1,0:T(8,128)(2,1)S(1)} %copy-done.2), channel_id=1, source_target_pairs={{0,24},{4,28},{8,16},{12,20},{16,8},{20,12},{24,0},{28,4},{1,25},{... | collective-permute-start | bytes 98312 | tf_op jit(solution)/shard_map/ppermute | solution.py:15
  38.3 7.0 %collective-permute-start.10 = (bf16[32,512]{1,0:T(8,128)(2,1)S(1)}, bf16[32,512]{1,0:T(8,128)(2,1)S(1)}, u32[]{:S(2)}, u32[]{:S(2)}) collective-permute-start(bf16[32,512]{1,0:T(8,128)(2,1)S(1)} %copy-done.2), channel_id=1, source_target_pairs={{0,16},{4,20},{8,24},{12,28},{16,0},{20,4},{24,8},{28,12},{1,17},{... | collective-permute-start | bytes 98312 | tf_op jit(solution)/shard_map/ppermute | solution.py:15
  38.8 4.4 %collective-permute-start.9 = (bf16[32,512]{1,0:T(8,128)(2,1)S(1)}, bf16[32,512]{1,0:T(8,128)(2,1)S(1)}, u32[]{:S(2)}, u32[]{:S(2)}) collective-permute-start(bf16[32,512]{1,0:T(8,128)(2,1)S(1)} %copy-done.2), channel_id=1, source_target_pairs={{0,8},{4,12},{8,0},{12,4},{16,24},{20,28},{24,16},{28,20},{1,9},{5... | collective-permute-start | bytes 98312 | tf_op jit(solution)/shard_map/ppermute | solution.py:15
  39.9 8.3 %copy-start.5 = (f32[1024]{0:T(1024)S(1)}, f32[1024]{0:T(1024)}, u32[]{:S(2)}) copy-start(f32[1024]{0:T(1024)} %param.10) | copy-start | bytes 12292
  40.4 6.4 %collective-permute-start.8 = (bf16[32,1024]{1,0:T(8,128)(2,1)S(1)}, bf16[32,1024]{1,0:T(8,128)(2,1)S(1)}, u32[]{:S(2)}, u32[]{:S(2)}) collective-permute-start(bf16[32,1024]{1,0:T(8,128)(2,1)S(1)} %convolution_convert_fusion), channel_id=1, source_target_pairs={{0,3},{1,2},{2,1},{3,0},{4,7},{5,6},{6,5},{7,4},{8,11},{9,10},{10,... | collective-permute-start | bytes 196616 | tf_op jit(solution)/shard_map/ppermute | solution.py:15
  42.9 5.4 %collective-permute-start.7 = (bf16[32,1024]{1,0:T(8,128)(2,1)S(1)}, bf16[32,1024]{1,0:T(8,128)(2,1)S(1)}, u32[]{:S(2)}, u32[]{:S(2)}) collective-permute-start(bf16[32,1024]{1,0:T(8,128)(2,1)S(1)} %convolution_convert_fusion), channel_id=1, source_target_pairs={{0,2},{1,3},{2,0},{3,1},{4,6},{5,7},{6,4},{7,5},{8,10},{9,11},{10,... | collective-permute-start | bytes 196616 | tf_op jit(solution)/shard_map/ppermute | solution.py:15
  43.2 5.0 %collective-permute-start.6 = (bf16[32,1024]{1,0:T(8,128)(2,1)S(1)}, bf16[32,1024]{1,0:T(8,128)(2,1)S(1)}, u32[]{:S(2)}, u32[]{:S(2)}) collective-permute-start(bf16[32,1024]{1,0:T(8,128)(2,1)S(1)} %convolution_convert_fusion), channel_id=1, source_target_pairs={{0,1},{1,0},{2,3},{3,2},{4,5},{5,4},{6,7},{7,6},{8,9},{9,8},{10,11... | collective-permute-start | bytes 196616 | tf_op jit(solution)/shard_map/ppermute | solution.py:15
  49.3 17.8 %copy-start.1 = (s32[8,1,64]{2,1,0:T(1,128)S(1)}, s32[8,1,64]{2,1,0:T(1,128)}, u32[]{:S(2)}) copy-start(s32[8,1,64]{2,1,0:T(1,128)} %all_to_all.15.wanted_ref) | copy-start | bytes 6148
  50.4 16.7 %all-to-all-start.2 = ((f32[32,20,128]{2,1,0:T(8,128)}), f32[32,20,128]{2,1,0:T(8,128)S(1)}, u32[]{:S(2)}, u32[]{:S(2)}) async-start(f32[32,20,128]{2,1,0:T(8,128)} %bitcast.15), calls=%async_computation.2 | async-start | bytes 786432 | tf_op jit(solution)/shard_map/all_to_all | solution.py:190
  55.3 6.0 %collective-permute-start.12 = (bf16[32,512]{1,0:T(8,128)(2,1)S(1)}, bf16[32,512]{1,0:T(8,128)(2,1)S(1)}, u32[]{:S(2)}, u32[]{:S(2)}) collective-permute-start(bf16[32,512]{1,0:T(8,128)(2,1)S(1)} %get-tuple-element.27), channel_id=1, source_target_pairs={{0,8},{4,12},{8,0},{12,4},{16,24},{20,28},{24,16},{28,20},{1,9},{5... | collective-permute-start | bytes 98312 | tf_op jit(solution)/shard_map/ppermute | solution.py:15
  57.1 6.2 %collective-permute-start.14 = (bf16[32,512]{1,0:T(8,128)(2,1)S(1)}, bf16[32,512]{1,0:T(8,128)(2,1)S(1)}, u32[]{:S(2)}, u32[]{:S(2)}) collective-permute-start(bf16[32,512]{1,0:T(8,128)(2,1)S(1)} %get-tuple-element.27), channel_id=1, source_target_pairs={{0,24},{4,28},{8,16},{12,20},{16,8},{20,12},{24,0},{28,4},{1,25},{... | collective-permute-start | bytes 98312 | tf_op jit(solution)/shard_map/ppermute | solution.py:15
  58.5 4.7 %collective-permute-start.13 = (bf16[32,512]{1,0:T(8,128)(2,1)S(1)}, bf16[32,512]{1,0:T(8,128)(2,1)S(1)}, u32[]{:S(2)}, u32[]{:S(2)}) collective-permute-start(bf16[32,512]{1,0:T(8,128)(2,1)S(1)} %get-tuple-element.27), channel_id=1, source_target_pairs={{0,16},{4,20},{8,24},{12,28},{16,0},{20,4},{24,8},{28,12},{1,17},{... | collective-permute-start | bytes 98312 | tf_op jit(solution)/shard_map/ppermute | solution.py:15
  63.3 1.6 %collective-permute-start.15 = (bf16[256,512]{1,0:T(8,128)(2,1)S(1)}, bf16[256,512]{1,0:T(8,128)(2,1)S(1)}, u32[]{:S(2)}, u32[]{:S(2)}) collective-permute-start(bf16[256,512]{1,0:T(8,128)(2,1)S(1)} %constant_dynamic-update-slice_fusion.even_ref), channel_id=1, source_target_pairs={{0,4},{4,0},{8,12},{12,8},{16,20},{20,16},{24,28},{28,24},{1,5},{5... | collective-permute-start | bytes 786440 | tf_op jit(solution)/shard_map/ppermute | solution.py:15

commit v5 on v2

v5 whole, which is shorter than its diff:
```python
import functools

import jax
import jax.numpy as jnp
from jax import lax
from jax.experimental import pallas as pl
from jax.experimental.pallas import tpu as pltpu
from jax.sharding import PartitionSpec as P

DL = 2048
SCALE = DL ** (-0.5)


def swap(x, axis, k):
    n = lax.axis_size(axis)
    return lax.ppermute(x, axis, [(i, i ^ k) for i in range(n)])


def exchange(x):
    return lax.all_to_all(x, "batch", split_axis=0, concat_axis=0, tiled=True)


def call(kernel, shapes, operands, specs, scratch=()):
    return pl.pallas_call(
        kernel,
        out_shape=shapes,
        in_specs=specs,
        out_specs=jax.tree.map(lambda _: pl.BlockSpec(memory_space=pltpu.VMEM), shapes),
        scratch_shapes=list(scratch),
        compiler_params=pltpu.CompilerParams(vmem_limit_bytes=32 * 1024 * 1024),
        name=getattr(kernel, "func", kernel).__name__,
    )(*operands)


def pick_rows(wanted_ref, rows_ref, out_ref):
    owners, capacity = wanted_ref.shape[0], wanted_ref.shape[2]
    stored = rows_ref.shape[0]
    listed = wanted_ref[...].reshape(owners, capacity).T
    places = lax.broadcasted_iota(jnp.int32, (capacity, stored), 1)
    chosen = jnp.concatenate(
        [(listed[:, d : d + 1] == places).astype(jnp.bfloat16) for d in range(owners)], axis=0
    )
    out_ref[...] = jnp.dot(chosen, rows_ref[...], preferred_element_type=jnp.float32).astype(
        jnp.bfloat16
    )


def turn(owners, upstream_ref, bias_ref, w_up_ref, fetched_ref, weight_ref, *refs):
    part_refs, (activated_ref, grad_ref, sending_ref) = refs[:-3], refs[-3:]
    latents = len(part_refs)
    members, slot_count = weight_ref.shape
    capacity = slot_count // owners
    half = members // 2
    hidden = part_refs[0][...].astype(jnp.float32)
    for part_ref in part_refs[1:]:
        hidden = hidden + part_ref[...].astype(jnp.float32)
    hidden = hidden + bias_ref[...]
    activated, backward = jax.vjp(jax.nn.gelu, hidden)
    activated_ref[...] = activated.astype(jnp.bfloat16)
    slopes = backward(upstream_ref[...].astype(jnp.float32))[0].astype(jnp.bfloat16)
    along = (((1,), (1,)), ((), ()))
    grad = lax.dot_general(
        slopes, w_up_ref[...], along, preferred_element_type=jnp.float32
    ).astype(jnp.bfloat16)
    grad_ref[...] = grad
    slot_slopes = lax.dot_general(
        grad, fetched_ref[...], along, preferred_element_type=jnp.float32
    )
    weight = weight_ref[...]
    part = weight * (slot_slopes - jnp.sum(weight * slot_slopes, axis=1, keepdims=True)) * SCALE
    for o in range(owners):
        block = part[:, o * capacity : (o + 1) * capacity]
        block = jnp.concatenate([block[:half], block[half:]], axis=1)
        for z in range(latents):
            sending_ref[o * latents + z] = block


def make_late(me_ref, weight_ref, grad_ref, out_ref):
    count, _, width = out_ref.shape
    pair = (width - grad_ref.shape[1]) // 2
    for i in range(count):
        first = pl.multiple_of((me_ref[0] // 2 ^ i) * pair, pair)
        weight = weight_ref[:, pl.ds(first, pair)]
        high = weight.astype(jnp.bfloat16)
        out_ref[i, :, :pair] = high
        out_ref[i, :, pair : 2 * pair] = (weight - high.astype(jnp.float32)).astype(jnp.bfloat16)
        out_ref[i, :, 2 * pair :] = grad_ref[...]


def add_rows(latents, me_ref, wanted_ref, sent_ref, *refs):
    target_refs, late_refs, (out_ref, left_ref, right_ref) = refs[:2], refs[2:4], refs[4:]
    owners, capacity = wanted_ref.shape[0], wanted_ref.shape[2]
    stored, width = out_ref.shape
    members = late_refs[0].shape[0] // (owners // 2)
    pair = 2 * capacity
    depth = 4 * members
    places = lax.broadcasted_iota(jnp.int32, (stored, capacity), 0)
    me = me_ref[0]
    first = me % 2 == 0

    def of_me(x):
        x = x.astype(jnp.float32)
        return jnp.where(first, x[:, :capacity], x[:, capacity:]).astype(jnp.bfloat16)

    for k in range(owners):
        d = me ^ k
        block = sent_ref[pl.ds(d * latents, latents)]
        slope = block[0]
        for z in range(1, latents):
            slope = slope + block[z]
        slope = jnp.concatenate([slope[:, :capacity], slope[:, capacity:]], axis=0)
        slope_high = slope.astype(jnp.bfloat16)
        slope_low = (slope - slope_high.astype(jnp.float32)).astype(jnp.bfloat16)
        piece = slice((k // 2) * members, (k // 2 + 1) * members)
        targets = target_refs[k % 2][piece, :]
        side = late_refs[k % 2][piece, :]
        grads = side[:, 2 * pair :]
        weight_high = of_me(side[:, :pair])
        weight_low = of_me(side[:, pair : 2 * pair])
        chosen = (wanted_ref[d] == places).astype(jnp.bfloat16)
        spread = lax.dot_general(
            chosen,
            jnp.concatenate([weight_high, slope_high, weight_low, slope_low], axis=0),
            (((1,), (1,)), ((), ())),
            preferred_element_type=jnp.float32,
        )
        left_ref[:, k * depth : (k + 1) * depth] = spread.astype(jnp.bfloat16)
        right_ref[k * depth : (k + 1) * depth, :] = jnp.concatenate(
            [grads, targets, grads, targets], axis=0
        )
    out_ref[...] = jnp.dot(left_ref[...], right_ref[...], preferred_element_type=jnp.float32)


def on_device(rows, targets, w_up, bias, history, requests, upstream):
    owners = lax.axis_size("batch")
    latents = lax.axis_size("latent")
    latent = lax.axis_index("latent")
    me = lax.axis_index("batch").reshape(1).astype(jnp.int32)
    capacity = requests.shape[1]
    slot_count = owners * capacity
    members, row_width = targets.shape
    stored = rows.shape[0]
    hidden_share = upstream.shape[1]
    half = members // 2
    vmem = pl.BlockSpec(memory_space=pltpu.VMEM)
    smem = pl.BlockSpec(memory_space=pltpu.SMEM)
    shape = jax.ShapeDtypeStruct
    bf16 = jnp.bfloat16

    wanted = exchange(requests.reshape(owners, 1, capacity))
    parts = jnp.stack([upstream] + [swap(upstream, "latent", k) for k in range(1, latents)])
    upstream_full = jnp.concatenate(
        [lax.dynamic_index_in_dim(parts, latent ^ z, 0, keepdims=False) for z in range(latents)],
        axis=1,
    )
    chosen = call(
        pick_rows, shape((slot_count, row_width), bf16), (wanted, rows), [vmem, vmem]
    )

    slots = lax.broadcasted_iota(jnp.int32, (1, 1, slot_count), 2)
    count = jnp.sum((history[:, :, None] == slots).astype(jnp.float32), axis=1)
    fetched = exchange(chosen.reshape(owners, capacity, row_width)).reshape(slot_count, row_width)
    fetched, count, upstream_full = lax.optimization_barrier((fetched, count, upstream_full))

    slot_scores = jnp.einsum("ud,sd->us", targets, fetched, preferred_element_type=jnp.float32)
    parts = [slot_scores] + [swap(slot_scores, "latent", k) for k in range(1, latents)]
    parts[1], late_targets = lax.optimization_barrier((parts[1], targets))
    even_targets = [targets] + [swap(late_targets, "batch", k) for k in range(2, owners, 2)]
    scores = sum(parts[1:], parts[0]) * SCALE
    top = jnp.max(jnp.where(count > 0, scores, -jnp.inf), axis=1, keepdims=True)
    raised = jnp.where(count > 0, count * jnp.exp(scores - top), 0.0)
    weight = raised / jnp.sum(raised, axis=1, keepdims=True)

    pooled = jnp.dot(weight.astype(bf16), fetched, preferred_element_type=jnp.float32).astype(bf16)
    partial_hidden = jnp.dot(pooled, w_up, preferred_element_type=jnp.float32).astype(bf16)
    parts = [partial_hidden] + [swap(partial_hidden, "latent", k) for k in range(1, latents)]
    parts, even_targets = lax.optimization_barrier((parts, even_targets))
    even_targets = jnp.concatenate(even_targets, axis=0)
    odd_targets = swap(even_targets, "batch", 1)
    activated, pooled_grad, sending = call(
        functools.partial(turn, owners),
        (
            shape(partial_hidden.shape, bf16),
            shape((members, row_width), bf16),
            shape((owners * latents, half, 2 * capacity), jnp.float32),
        ),
        (upstream_full, bias.reshape(1, -1), w_up, fetched, weight, *parts),
        [vmem] * (5 + latents),
    )
    output = lax.dynamic_slice_in_dim(activated, latent * hidden_share, hidden_share, axis=1)

    sent = lax.all_to_all(sending, ("batch", "latent"), split_axis=0, concat_axis=0, tiled=True)
    late = call(
        make_late,
        shape((owners // 2, members, 4 * capacity + row_width), bf16),
        (me, weight, pooled_grad),
        [smem, vmem, vmem],
    )
    even_late = [late[0]] + [swap(late[k // 2], "batch", k) for k in range(2, owners, 2)]
    even_late = jnp.concatenate(even_late, axis=0)
    odd_late = swap(even_late, "batch", 1)
    depth = owners * 4 * members
    row_grad = call(
        functools.partial(add_rows, latents),
        shape((stored, row_width), jnp.float32),
        (me, wanted, sent, even_targets, odd_targets, even_late, odd_late),
        [smem] + [vmem] * 6,
        [pltpu.VMEM((stored, depth), bf16), pltpu.VMEM((depth, row_width), bf16)],
    )
    return (output, row_grad)


def solution(mesh):
    return jax.shard_map(
        on_device,
        mesh=mesh,
        in_specs=(
            P("batch", "latent"),
            P("batch", "latent"),
            P("latent", None),
            P(),
            P("batch", None),
            P("batch", None),
            P("batch", "latent"),
        ),
        out_specs=(P("batch", "latent"), P("batch", "latent")),
        check_vma=False,
    )
```

time: 71.5 us -> 65.8 us (0.920)
  matrix products: 7.8 us -> 0.68 us
  waiting for transfers between devices: 25.1 us -> 19.6 us
  Pallas kernels: 0 us -> 4.93 us
  starting transfers between devices: 30.1 us -> 32.5 us
  other arithmetic: 6.58 us -> 5.11 us
  local copies, waits for them, and re-layouts: 0.63 us -> 1.72 us
    all_to_all x3 -> x2, waiting for transfers between devices: 14.4 us -> 5.35 us  [exchange(): return lax.all_to_all(x, 'batch', split_axis=0, concat_axis=0, tiled=True)]
    dot_general x7 -> x1, matrix products: 7.56 us -> 0.44 us  [on_device(): jnp.dot(pooled, w_up, preferred_element_type=jnp.float32).astype(bf16)]
    pallas_call x0 -> x4, Pallas kernels: none -> 4.93 us  [call(): pl.pallas_call(kernel, out_shape=shapes, in_specs=specs, out_specs=jax.tr...]
    all_to_all x3 -> x2, starting transfers between devices: 12.7 us -> 9.1 us  [exchange(): return lax.all_to_all(x, 'batch', split_axis=0, concat_axis=0, tiled=True)]
    ppermute x12 -> x17, starting transfers between devices: 17.4 us -> 20.6 us  [swap(): return lax.ppermute(x, axis, [(i, i ^ k) for i in range(n)])]
    ppermute x12 -> x17, waiting for transfers between devices: 10.7 us -> 13.6 us  [swap(): return lax.ppermute(x, axis, [(i, i ^ k) for i in range(n)])]
    all_to_all x0 -> x1, starting transfers between devices: none -> 2.82 us  [on_device(): lax.all_to_all(sending, ('batch', 'latent'), split_axis=0, concat_axis=0,...]
    unnamed x10 -> x15, local copies, waits for them, and re-layouts: 0.02 us -> 1.07 us
  transfers between devices with their start and end apart: 15 -> 20, of which waited for: 9 -> 11; matrix products, arithmetic and copies ran while one was open for 14% -> 9% of each run, Pallas kernels for 0% -> 2%
where the time goes in v5:
time: 65.8 us; the launch traced here: 65.4 us
  starting transfers between devices  32.5 us (49%)
  waiting for transfers between devices  19.6 us (30%)
  other arithmetic  5.11 us (8%)
  Pallas kernels  4.93 us (7%)
  local copies, waits for them, and re-layouts  1.72 us (3%)
  between operations  0.82 us (1%)
  matrix products  0.68 us (1%)
    ppermute x17, starting transfers between devices, swap(): return lax.ppermute(x, axis, [(i, i ^ k) for i in range(n)])  20.6 us
    ppermute x17, waiting for transfers between devices, swap(): return lax.ppermute(x, axis, [(i, i ^ k) for i in range(n)])  13.6 us
    all_to_all x2, starting transfers between devices, exchange(): return lax.all_to_all(x, 'batch', split_axis=0, concat_axis=0, tiled=True)  9.1 us
    all_to_all x2, waiting for transfers between devices, exchange(): return lax.all_to_all(x, 'batch', split_axis=0, concat_axis=0, tiled=True)  5.35 us
    pallas_call x4, Pallas kernels, call(): pl.pallas_call(kernel, out_shape=shapes, in_specs=specs, out_specs=jax.tr...  4.93 us
    reduce_sum x1, other arithmetic, on_device(): count = jnp.sum((history[:, :, None] == slots).astype(jnp.float32), axis=1)  4.66 us
    all_to_all x1, starting transfers between devices, on_device(): lax.all_to_all(sending, ('batch', 'latent'), split_axis=0, concat_axis=0,...  2.82 us
  transfers between devices with their start and end apart: 20, of which 11 were waited for; matrix products, arithmetic and copies ran while one was open for 9% of the time, Pallas kernels for 2%

profile of v5, /device:TPU:0, one launch (start us, length us, event | category | flops | bytes accessed | tf_op | source)
XLA Modules:
  0.0 65.4 jit_solution(2065139818491420943)
XLA Ops:
  0.6 5.2 %all-to-all-start = ((s32[8,1,64]{2,1,0:T(1,128)}), s32[8,1,64]{2,1,0:T(1,128)S(1)}, u32[]{:S(2)}, u32[]{:S(2)}) async-start(s32[8,1,64]{2,1,0:T(1,128)} %bitcast.39), calls=%async_computation | async-start | bytes 8192 | tf_op jit(solution)/shard_map/all_to_all | solution.py:20
  5.8 1.6 %collective-permute-start = (bf16[32,256]{1,0:T(8,128)(2,1)}, bf16[32,256]{1,0:T(8,128)(2,1)S(1)}, u32[]{:S(2)}, u32[]{:S(2)}) collective-permute-start(bf16[32,256]{1,0:T(8,128)(2,1)} %param.13), channel_id=1, source_target_pairs={{0,1},{1,0},{2,3},{3,2},{4,5},{5,4},{6,7},{7,6},{8,9},{9,8},{10,11... | collective-permute-start | bytes 49160 | tf_op jit(solution)/shard_map/ppermute | solution.py:16
  7.4 2.5 %collective-permute-start.2 = (bf16[32,256]{1,0:T(8,128)(2,1)}, bf16[32,256]{1,0:T(8,128)(2,1)S(1)}, u32[]{:S(2)}, u32[]{:S(2)}) collective-permute-start(bf16[32,256]{1,0:T(8,128)(2,1)} %param.13), channel_id=1, source_target_pairs={{0,3},{1,2},{2,1},{3,0},{4,7},{5,6},{6,5},{7,4},{8,11},{9,10},{10,... | collective-permute-start | bytes 49160 | tf_op jit(solution)/shard_map/ppermute | solution.py:16
  9.9 0.1 collective-permute-start.1
  10.0 0.4 all-to-all-done.wanted_ref
  10.4 1.0 %copy-done.1 = bf16[512,512]{1,0:T(8,128)(2,1)S(1)} copy-done((bf16[512,512]{1,0:T(8,128)(2,1)S(1)}, bf16[512,512]{1,0:T(8,128)(2,1)}, u32[]{:S(2)}) %copy-start.1) | copy-done | bytes 524312
  11.4 1.3 %pick_rows.1 = bf16[512,512]{1,0:T(8,128)(2,1)} custom-call(s32[8,1,64]{2,1,0:T(1,128)S(1)} %all-to-all-done.wanted_ref, bf16[512,512]{1,0:T(8,128)(2,1)S(1)} %copy-done.1), custom_call_target="tpu_custom_call" | custom-call | tf_op jit(solution)/shard_map/pick_rows/pallas_call | solution.py:24
  12.8 3.9 %all-to-all-start.1 = ((bf16[8,64,512]{2,1,0:T(8,128)(2,1)}), bf16[8,64,512]{2,1,0:T(8,128)(2,1)S(1)}, u32[]{:S(2)}, u32[]{:S(2)}) async-start(bf16[8,64,512]{2,1,0:T(8,128)(2,1)} %bitcast.1), calls=%async_computation.1 | async-start | bytes 1048576 | tf_op jit(solution)/shard_map/all_to_all | solution.py:20
  16.7 0.0 copy-start
  16.7 4.7 %convert_reduce_fusion = f32[32,512]{1,0:T(8,128)S(1)} fusion(s32[32,512]{1,0:T(8,128)S(1)} %copy-done.4), kind=kLoop, calls=%fused_computation | loop fusion | flops 25149440 | bytes 131072 | tf_op jit(solution)/shard_map/reduce_sum | solution.py:161
  21.4 0.0 collective-permute-done
  21.4 0.0 collective-permute-done.2
  21.5 4.9 %all-to-all-done.1 = bf16[8,64,512]{2,1,0:T(8,128)(2,1)S(1)} async-done(((bf16[8,64,512]{2,1,0:T(8,128)(2,1)}), bf16[8,64,512]{2,1,0:T(8,128)(2,1)S(1)}, u32[]{:S(2)}, u32[]{:S(2)}) %all-to-all-start.1) | async-done | bytes 524320 | tf_op jit(solution)/shard_map/all_to_all | solution.py:20
  26.5 0.2 convolution_bitcast_fusion
  26.7 1.8 %collective-permute-start.3 = (f32[32,512]{1,0:T(8,128)S(1)}, f32[32,512]{1,0:T(8,128)S(1)}, u32[]{:S(2)}, u32[]{:S(2)}) collective-permute-start(f32[32,512]{1,0:T(8,128)S(1)} %convolution_bitcast_fusion), channel_id=1, source_target_pairs={{0,1},{1,0},{2,3},{3,2},{4,5},{5,4},{6,7},{7,6},{8,9},{9,8},{10,11... | collective-permute-start | bytes 196616 | tf_op jit(solution)/shard_map/ppermute | solution.py:16
  28.5 2.5 %collective-permute-start.5 = (f32[32,512]{1,0:T(8,128)S(1)}, f32[32,512]{1,0:T(8,128)S(1)}, u32[]{:S(2)}, u32[]{:S(2)}) collective-permute-start(f32[32,512]{1,0:T(8,128)S(1)} %convolution_bitcast_fusion), channel_id=1, source_target_pairs={{0,3},{1,2},{2,1},{3,0},{4,7},{5,6},{6,5},{7,4},{8,11},{9,10},{10,... | collective-permute-start | bytes 196616 | tf_op jit(solution)/shard_map/ppermute | solution.py:16
  31.0 0.0 collective-permute-start.4
  31.0 0.5 collective-permute-done.3
  31.5 3.1 %collective-permute-done.5 = f32[32,512]{1,0:T(8,128)S(1)} collective-permute-done((f32[32,512]{1,0:T(8,128)S(1)}, f32[32,512]{1,0:T(8,128)S(1)}, u32[]{:S(2)}, u32[]{:S(2)}) %collective-permute-start.5) | collective-permute-done | bytes 65568 | tf_op jit(solution)/shard_map/ppermute | solution.py:16
  34.6 1.8 %collective-permute-done.4 = f32[32,512]{1,0:T(8,128)S(1)} collective-permute-done((f32[32,512]{1,0:T(8,128)S(1)}, f32[32,512]{1,0:T(8,128)S(1)}, u32[]{:S(2)}, u32[]{:S(2)}) %collective-permute-start.4) | collective-permute-done | bytes 65568 | tf_op jit(solution)/shard_map/ppermute | solution.py:16
  36.4 0.1 select_reduce_fusion
  36.5 0.2 fusion.2
  36.7 0.1 broadcast_divide_fusion.weight_ref
  36.8 1.6 %collective-permute-start.11 = (bf16[32,512]{1,0:T(8,128)(2,1)S(1)}, bf16[32,512]{1,0:T(8,128)(2,1)S(1)}, u32[]{:S(2)}, u32[]{:S(2)}) collective-permute-start(bf16[32,512]{1,0:T(8,128)(2,1)S(1)} %copy-done.3), channel_id=1, source_target_pairs={{0,24},{4,28},{8,16},{12,20},{16,8},{20,12},{24,0},{28,4},{1,25},{... | collective-permute-start | bytes 98312 | tf_op jit(solution)/shard_map/ppermute | solution.py:16
  38.4 0.4 convolution_convert_fusion.refs_0_
  38.8 2.6 %collective-permute-start.8 = (bf16[32,1024]{1,0:T(8,128)(2,1)S(1)}, bf16[32,1024]{1,0:T(8,128)(2,1)S(1)}, u32[]{:S(2)}, u32[]{:S(2)}) collective-permute-start(bf16[32,1024]{1,0:T(8,128)(2,1)S(1)} %convolution_convert_fusion.refs_0_), channel_id=1, source_target_pairs={{0,3},{1,2},{2,1},{3,0},{4,7},{5,6},{6,5},{7,4},{8,11},{9,10},{10,... | collective-permute-start | bytes 196616 | tf_op jit(solution)/shard_map/ppermute | solution.py:16
  41.4 0.0 collective-permute-start.7
  41.4 1.8 %collective-permute-start.6 = (bf16[32,1024]{1,0:T(8,128)(2,1)S(1)}, bf16[32,1024]{1,0:T(8,128)(2,1)S(1)}, u32[]{:S(2)}, u32[]{:S(2)}) collective-permute-start(bf16[32,1024]{1,0:T(8,128)(2,1)S(1)} %convolution_convert_fusion.refs_0_), channel_id=1, source_target_pairs={{0,1},{1,0},{2,3},{3,2},{4,5},{5,4},{6,7},{7,6},{8,9},{9,8},{10,11... | collective-permute-start | bytes 196616 | tf_op jit(solution)/shard_map/ppermute | solution.py:16
  43.3 1.6 %collective-permute-start.10 = (bf16[32,512]{1,0:T(8,128)(2,1)S(1)}, bf16[32,512]{1,0:T(8,128)(2,1)S(1)}, u32[]{:S(2)}, u32[]{:S(2)}) collective-permute-start(bf16[32,512]{1,0:T(8,128)(2,1)S(1)} %copy-done.3), channel_id=1, source_target_pairs={{0,16},{4,20},{8,24},{12,28},{16,0},{20,4},{24,8},{28,12},{1,17},{... | collective-permute-start | bytes 98312 | tf_op jit(solution)/shard_map/ppermute | solution.py:16
  44.8 0.0 collective-permute-done.11
  44.8 0.4 collective-permute-start.9
  45.3 1.9 %collective-permute-done.10 = bf16[32,512]{1,0:T(8,128)(2,1)S(1)} collective-permute-done((bf16[32,512]{1,0:T(8,128)(2,1)S(1)}, bf16[32,512]{1,0:T(8,128)(2,1)S(1)}, u32[]{:S(2)}, u32[]{:S(2)}) %collective-permute-start.10) | collective-permute-done | bytes 32800 | tf_op jit(solution)/shard_map/ppermute | solution.py:16
  47.2 1.6 %collective-permute-done.9 = bf16[32,512]{1,0:T(8,128)(2,1)S(1)} collective-permute-done((bf16[32,512]{1,0:T(8,128)(2,1)S(1)}, bf16[32,512]{1,0:T(8,128)(2,1)S(1)}, u32[]{:S(2)}, u32[]{:S(2)}) %collective-permute-start.9) | collective-permute-done | bytes 32800 | tf_op jit(solution)/shard_map/ppermute | solution.py:16
  48.8 0.0 collective-permute-done.7.refs_2_
  48.8 0.0 collective-permute-done.6.refs_1_
  48.8 1.5 %turn.1 = (bf16[32,1024]{1,0:T(8,128)(2,1)S(1)}, bf16[32,512]{1,0:T(8,128)(2,1)S(1)}, f32[32,16,128]{2,1,0:T(8,128)}) custom-call(bf16[32,1024]{1,0:T(8,128)(2,1)S(1)} %pad_maximum_fusion.2.upstream_ref, f32[1,1024]{1,0:T(1,128)S(1)} %bitcast.34, bf16[512,1024]{1,0:T(8,128)(2,1)S(1)} %copy-done, bf16[512,512]{1,0:T(8,128)(2,1)S(1)} %bitcast.33, ...), custom_call_target="tpu_custom_call" | custom-call | tf_op jit(solution)/shard_map/turn/pallas_call | solution.py:24
  50.3 2.8 %all-to-all-start.2 = ((f32[32,16,128]{2,1,0:T(8,128)}), f32[32,16,128]{2,1,0:T(8,128)S(1)}, u32[]{:S(2)}, u32[]{:S(2)}) async-start(f32[32,16,128]{2,1,0:T(8,128)} %get-tuple-element.28), calls=%async_computation.2 | async-start | bytes 524288 | tf_op jit(solution)/shard_map/all_to_all | solution.py:192
  53.1 2.7 %collective-permute-start.15 = (bf16[32,768]{1,0:T(8,128)(2,1)S(1)}, bf16[32,768]{1,0:T(8,128)(2,1)S(1)}, u32[]{:S(2)}, u32[]{:S(2)}) collective-permute-start(bf16[32,768]{1,0:T(8,128)(2,1)S(1)} %get-tuple-element.37), channel_id=1, source_target_pairs={{0,24},{4,28},{8,16},{12,20},{16,8},{20,12},{24,0},{28,4},{1,25},{... | collective-permute-start | bytes 147464 | tf_op jit(solution)/shard_map/ppermute | solution.py:16
  55.9 0.6 collective-permute-start.14
  56.4 0.3 collective-permute-start.13
  56.7 3.0 %collective-permute-done.15 = bf16[32,768]{1,0:T(8,128)(2,1)S(1)} collective-permute-done((bf16[32,768]{1,0:T(8,128)(2,1)S(1)}, bf16[32,768]{1,0:T(8,128)(2,1)S(1)}, u32[]{:S(2)}, u32[]{:S(2)}) %collective-permute-start.15) | collective-permute-done | bytes 49184 | tf_op jit(solution)/shard_map/ppermute | solution.py:16
  59.7 1.2 %collective-permute-done.14 = bf16[32,768]{1,0:T(8,128)(2,1)S(1)} collective-permute-done((bf16[32,768]{1,0:T(8,128)(2,1)S(1)}, bf16[32,768]{1,0:T(8,128)(2,1)S(1)}, u32[]{:S(2)}, u32[]{:S(2)}) %collective-permute-start.14) | collective-permute-done | bytes 49184 | tf_op jit(solution)/shard_map/ppermute | solution.py:16
  60.9 0.1 collective-permute-start.16
  61.0 0.5 collective-permute-start.12
  61.5 0.6 constant_dynamic-slice_fusion
  62.1 0.5 collective-permute-done.12.refs_1_
  62.6 0.7 %all-to-all-done.2.sent_ref = f32[32,16,128]{2,1,0:T(8,128)S(1)} async-done(((f32[32,16,128]{2,1,0:T(8,128)}), f32[32,16,128]{2,1,0:T(8,128)S(1)}, u32[]{:S(2)}, u32[]{:S(2)}) %all-to-all-start.2) | async-done | bytes 262176 | tf_op jit(solution)/shard_map/all_to_all | solution.py:192
  63.3 2.1 %add_rows.1 = f32[512,512]{1,0:T(8,128)} custom-call(s32[1]{0:T(128)} %bitcast.13.me_ref, s32[8,1,64]{2,1,0:T(1,128)S(1)} %all-to-all-done.wanted_ref, f32[32,16,128]{2,1,0:T(8,128)S(1)} %all-to-all-done.2.sent_ref, bf16[128,512]{1,0:T(8,128)(2,1)S(1)} %constant_dynamic-update-slice_fusion.refs_0_, bf16[128,512]{1,0:T(8,128)(2,1)S(1)} %collective-permute-done.12.refs_1_, ...), custom_call_target="tpu_custom_call" | custom-call | tf_op jit(solution)/shard_map/add_rows/pallas_call | solution.py:24
  (24 shorter events, 0.1 us)
Async XLA Ops:
  0.6 9.8 %all-to-all-start = ((s32[8,1,64]{2,1,0:T(1,128)}), s32[8,1,64]{2,1,0:T(1,128)S(1)}, u32[]{:S(2)}, u32[]{:S(2)}) async-start(s32[8,1,64]{2,1,0:T(1,128)} %bitcast.39), calls=%async_computation | async-start | bytes 8192 | tf_op jit(solution)/shard_map/all_to_all | solution.py:20
  5.8 15.6 %collective-permute-start = (bf16[32,256]{1,0:T(8,128)(2,1)}, bf16[32,256]{1,0:T(8,128)(2,1)S(1)}, u32[]{:S(2)}, u32[]{:S(2)}) collective-permute-start(bf16[32,256]{1,0:T(8,128)(2,1)} %param.13), channel_id=1, source_target_pairs={{0,1},{1,0},{2,3},{3,2},{4,5},{5,4},{6,7},{7,6},{8,9},{9,8},{10,11... | collective-permute-start | bytes 49160 | tf_op jit(solution)/shard_map/ppermute | solution.py:16
  7.4 14.0 %collective-permute-start.2 = (bf16[32,256]{1,0:T(8,128)(2,1)}, bf16[32,256]{1,0:T(8,128)(2,1)S(1)}, u32[]{:S(2)}, u32[]{:S(2)}) collective-permute-start(bf16[32,256]{1,0:T(8,128)(2,1)} %param.13), channel_id=1, source_target_pairs={{0,3},{1,2},{2,1},{3,0},{4,7},{5,6},{6,5},{7,4},{8,11},{9,10},{10,... | collective-permute-start | bytes 49160 | tf_op jit(solution)/shard_map/ppermute | solution.py:16
  9.9 11.6 %collective-permute-start.1 = (bf16[32,256]{1,0:T(8,128)(2,1)}, bf16[32,256]{1,0:T(8,128)(2,1)S(1)}, u32[]{:S(2)}, u32[]{:S(2)}) collective-permute-start(bf16[32,256]{1,0:T(8,128)(2,1)} %param.13), channel_id=1, source_target_pairs={{0,2},{1,3},{2,0},{3,1},{4,6},{5,7},{6,4},{7,5},{8,10},{9,11},{10,... | collective-permute-start | bytes 49160 | tf_op jit(solution)/shard_map/ppermute | solution.py:16
  10.4 1.0 %copy-start.1 = (bf16[512,512]{1,0:T(8,128)(2,1)S(1)}, bf16[512,512]{1,0:T(8,128)(2,1)}, u32[]{:S(2)}) copy-start(bf16[512,512]{1,0:T(8,128)(2,1)} %rows_ref.1) | copy-start | bytes 1572868
  11.4 5.3 %copy-start.4 = (s32[32,512]{1,0:T(8,128)S(1)}, s32[32,512]{1,0:T(8,128)}, u32[]{:S(2)}) copy-start(s32[32,512]{1,0:T(8,128)} %param.11) | copy-start | bytes 196612
  11.4 10.0 %copy-start.5 = (bf16[32,256]{1,0:T(8,128)(2,1)S(1)}, bf16[32,256]{1,0:T(8,128)(2,1)}, u32[]{:S(2)}) copy-start(bf16[32,256]{1,0:T(8,128)(2,1)} %param.13) | copy-start | bytes 49156
  12.8 13.7 %copy-start.3 = (bf16[32,512]{1,0:T(8,128)(2,1)S(1)}, bf16[32,512]{1,0:T(8,128)(2,1)}, u32[]{:S(2)}) copy-start(bf16[32,512]{1,0:T(8,128)(2,1)} %param.8) | copy-start | bytes 98308
  12.8 13.7 %all-to-all-start.1 = ((bf16[8,64,512]{2,1,0:T(8,128)(2,1)}), bf16[8,64,512]{2,1,0:T(8,128)(2,1)S(1)}, u32[]{:S(2)}, u32[]{:S(2)}) async-start(bf16[8,64,512]{2,1,0:T(8,128)(2,1)} %bitcast.1), calls=%async_computation.1 | async-start | bytes 1048576 | tf_op jit(solution)/shard_map/all_to_all | solution.py:20
  16.7 21.7 %copy-start = (bf16[512,1024]{1,0:T(8,128)(2,1)S(1)}, bf16[512,1024]{1,0:T(8,128)(2,1)}, u32[]{:S(2)}) copy-start(bf16[512,1024]{1,0:T(8,128)(2,1)} %w_up_ref.1) | copy-start | bytes 3145732
  26.7 4.8 %collective-permute-start.3 = (f32[32,512]{1,0:T(8,128)S(1)}, f32[32,512]{1,0:T(8,128)S(1)}, u32[]{:S(2)}, u32[]{:S(2)}) collective-permute-start(f32[32,512]{1,0:T(8,128)S(1)} %convolution_bitcast_fusion), channel_id=1, source_target_pairs={{0,1},{1,0},{2,3},{3,2},{4,5},{5,4},{6,7},{7,6},{8,9},{9,8},{10,11... | collective-permute-start | bytes 196616 | tf_op jit(solution)/shard_map/ppermute | solution.py:16
  28.5 6.1 %collective-permute-start.5 = (f32[32,512]{1,0:T(8,128)S(1)}, f32[32,512]{1,0:T(8,128)S(1)}, u32[]{:S(2)}, u32[]{:S(2)}) collective-permute-start(f32[32,512]{1,0:T(8,128)S(1)} %convolution_bitcast_fusion), channel_id=1, source_target_pairs={{0,3},{1,2},{2,1},{3,0},{4,7},{5,6},{6,5},{7,4},{8,11},{9,10},{10,... | collective-permute-start | bytes 196616 | tf_op jit(solution)/shard_map/ppermute | solution.py:16
  31.0 5.4 %collective-permute-start.4 = (f32[32,512]{1,0:T(8,128)S(1)}, f32[32,512]{1,0:T(8,128)S(1)}, u32[]{:S(2)}, u32[]{:S(2)}) collective-permute-start(f32[32,512]{1,0:T(8,128)S(1)} %convolution_bitcast_fusion), channel_id=1, source_target_pairs={{0,2},{1,3},{2,0},{3,1},{4,6},{5,7},{6,4},{7,5},{8,10},{9,11},{10,... | collective-permute-start | bytes 196616 | tf_op jit(solution)/shard_map/ppermute | solution.py:16
  36.5 12.2 %copy-start.2 = (f32[1024]{0:T(1024)S(1)}, f32[1024]{0:T(1024)}, u32[]{:S(2)}) copy-start(f32[1024]{0:T(1024)} %param.10) | copy-start | bytes 12292
  36.8 8.0 %collective-permute-start.11 = (bf16[32,512]{1,0:T(8,128)(2,1)S(1)}, bf16[32,512]{1,0:T(8,128)(2,1)S(1)}, u32[]{:S(2)}, u32[]{:S(2)}) collective-permute-start(bf16[32,512]{1,0:T(8,128)(2,1)S(1)} %copy-done.3), channel_id=1, source_target_pairs={{0,24},{4,28},{8,16},{12,20},{16,8},{20,12},{24,0},{28,4},{1,25},{... | collective-permute-start | bytes 98312 | tf_op jit(solution)/shard_map/ppermute | solution.py:16
  38.8 9.9 %collective-permute-start.8 = (bf16[32,1024]{1,0:T(8,128)(2,1)S(1)}, bf16[32,1024]{1,0:T(8,128)(2,1)S(1)}, u32[]{:S(2)}, u32[]{:S(2)}) collective-permute-start(bf16[32,1024]{1,0:T(8,128)(2,1)S(1)} %convolution_convert_fusion.refs_0_), channel_id=1, source_target_pairs={{0,3},{1,2},{2,1},{3,0},{4,7},{5,6},{6,5},{7,4},{8,11},{9,10},{10,... | collective-permute-start | bytes 196616 | tf_op jit(solution)/shard_map/ppermute | solution.py:16
  41.4 7.3 %collective-permute-start.7 = (bf16[32,1024]{1,0:T(8,128)(2,1)S(1)}, bf16[32,1024]{1,0:T(8,128)(2,1)S(1)}, u32[]{:S(2)}, u32[]{:S(2)}) collective-permute-start(bf16[32,1024]{1,0:T(8,128)(2,1)S(1)} %convolution_convert_fusion.refs_0_), channel_id=1, source_target_pairs={{0,2},{1,3},{2,0},{3,1},{4,6},{5,7},{6,4},{7,5},{8,10},{9,11},{10,... | collective-permute-start | bytes 196616 | tf_op jit(solution)/shard_map/ppermute | solution.py:16
  41.4 7.3 %collective-permute-start.6 = (bf16[32,1024]{1,0:T(8,128)(2,1)S(1)}, bf16[32,1024]{1,0:T(8,128)(2,1)S(1)}, u32[]{:S(2)}, u32[]{:S(2)}) collective-permute-start(bf16[32,1024]{1,0:T(8,128)(2,1)S(1)} %convolution_convert_fusion.refs_0_), channel_id=1, source_target_pairs={{0,1},{1,0},{2,3},{3,2},{4,5},{5,4},{6,7},{7,6},{8,9},{9,8},{10,11... | collective-permute-start | bytes 196616 | tf_op jit(solution)/shard_map/ppermute | solution.py:16
  43.3 3.9 %collective-permute-start.10 = (bf16[32,512]{1,0:T(8,128)(2,1)S(1)}, bf16[32,512]{1,0:T(8,128)(2,1)S(1)}, u32[]{:S(2)}, u32[]{:S(2)}) collective-permute-start(bf16[32,512]{1,0:T(8,128)(2,1)S(1)} %copy-done.3), channel_id=1, source_target_pairs={{0,16},{4,20},{8,24},{12,28},{16,0},{20,4},{24,8},{28,12},{1,17},{... | collective-permute-start | bytes 98312 | tf_op jit(solution)/shard_map/ppermute | solution.py:16
  44.8 3.9 %collective-permute-start.9 = (bf16[32,512]{1,0:T(8,128)(2,1)S(1)}, bf16[32,512]{1,0:T(8,128)(2,1)S(1)}, u32[]{:S(2)}, u32[]{:S(2)}) collective-permute-start(bf16[32,512]{1,0:T(8,128)(2,1)S(1)} %copy-done.3), channel_id=1, source_target_pairs={{0,8},{4,12},{8,0},{12,4},{16,24},{20,28},{24,16},{28,20},{1,9},{5... | collective-permute-start | bytes 98312 | tf_op jit(solution)/shard_map/ppermute | solution.py:16
  50.3 13.0 %all-to-all-start.2 = ((f32[32,16,128]{2,1,0:T(8,128)}), f32[32,16,128]{2,1,0:T(8,128)S(1)}, u32[]{:S(2)}, u32[]{:S(2)}) async-start(f32[32,16,128]{2,1,0:T(8,128)} %get-tuple-element.28), calls=%async_computation.2 | async-start | bytes 524288 | tf_op jit(solution)/shard_map/all_to_all | solution.py:192
  53.1 6.5 %collective-permute-start.15 = (bf16[32,768]{1,0:T(8,128)(2,1)S(1)}, bf16[32,768]{1,0:T(8,128)(2,1)S(1)}, u32[]{:S(2)}, u32[]{:S(2)}) collective-permute-start(bf16[32,768]{1,0:T(8,128)(2,1)S(1)} %get-tuple-element.37), channel_id=1, source_target_pairs={{0,24},{4,28},{8,16},{12,20},{16,8},{20,12},{24,0},{28,4},{1,25},{... | collective-permute-start | bytes 147464 | tf_op jit(solution)/shard_map/ppermute | solution.py:16
  55.9 5.0 %collective-permute-start.14 = (bf16[32,768]{1,0:T(8,128)(2,1)S(1)}, bf16[32,768]{1,0:T(8,128)(2,1)S(1)}, u32[]{:S(2)}, u32[]{:S(2)}) collective-permute-start(bf16[32,768]{1,0:T(8,128)(2,1)S(1)} %get-tuple-element.38), channel_id=1, source_target_pairs={{0,16},{4,20},{8,24},{12,28},{16,0},{20,4},{24,8},{28,12},{1,17},{... | collective-permute-start | bytes 147464 | tf_op jit(solution)/shard_map/ppermute | solution.py:16
  56.4 4.4 %collective-permute-start.13 = (bf16[32,768]{1,0:T(8,128)(2,1)S(1)}, bf16[32,768]{1,0:T(8,128)(2,1)S(1)}, u32[]{:S(2)}, u32[]{:S(2)}) collective-permute-start(bf16[32,768]{1,0:T(8,128)(2,1)S(1)} %get-tuple-element.39), channel_id=1, source_target_pairs={{0,8},{4,12},{8,0},{12,4},{16,24},{20,28},{24,16},{28,20},{1,9},{5... | collective-permute-start | bytes 147464 | tf_op jit(solution)/shard_map/ppermute | solution.py:16
  60.9 1.7 %collective-permute-start.16 = (bf16[128,768]{1,0:T(8,128)(2,1)S(1)}, bf16[128,768]{1,0:T(8,128)(2,1)S(1)}, u32[]{:S(2)}, u32[]{:S(2)}) collective-permute-start(bf16[128,768]{1,0:T(8,128)(2,1)S(1)} %pad_maximum_fusion.refs_2_), channel_id=1, source_target_pairs={{0,4},{4,0},{8,12},{12,8},{16,20},{20,16},{24,28},{28,24},{1,5},{5... | collective-permute-start | bytes 589832 | tf_op jit(solution)/shard_map/ppermute | solution.py:16
  61.0 1.6 %collective-permute-start.12 = (bf16[128,512]{1,0:T(8,128)(2,1)S(1)}, bf16[128,512]{1,0:T(8,128)(2,1)S(1)}, u32[]{:S(2)}, u32[]{:S(2)}) collective-permute-start(bf16[128,512]{1,0:T(8,128)(2,1)S(1)} %constant_dynamic-update-slice_fusion.refs_0_), channel_id=1, source_target_pairs={{0,4},{4,0},{8,12},{12,8},{16,20},{20,16},{24,28},{28,24},{1,5},{5... | collective-permute-start | bytes 393224 | tf_op jit(solution)/shard_map/ppermute | solution.py:16

commit v6 on v5

--- a/solution.py
+++ b/solution.py
@@ -163,9 +163,10 @@
     fetched, count, upstream_full = lax.optimization_barrier((fetched, count, upstream_full))
 
     slot_scores = jnp.einsum("ud,sd->us", targets, fetched, preferred_element_type=jnp.float32)
+    late_targets, slot_scores = lax.optimization_barrier((targets, slot_scores))
     parts = [slot_scores] + [swap(slot_scores, "latent", k) for k in range(1, latents)]
-    parts[1], late_targets = lax.optimization_barrier((parts[1], targets))
-    even_targets = [targets] + [swap(late_targets, "batch", k) for k in range(2, owners, 2)]
+    near_targets = [swap(late_targets, "batch", k) for k in range(2, owners, 2)[:1]]
+    parts, near_targets = lax.optimization_barrier((parts, near_targets))
     scores = sum(parts[1:], parts[0]) * SCALE
     top = jnp.max(jnp.where(count > 0, scores, -jnp.inf), axis=1, keepdims=True)
     raised = jnp.where(count > 0, count * jnp.exp(scores - top), 0.0)
@@ -173,10 +174,9 @@
 
     pooled = jnp.dot(weight.astype(bf16), fetched, preferred_element_type=jnp.float32).astype(bf16)
     partial_hidden = jnp.dot(pooled, w_up, preferred_element_type=jnp.float32).astype(bf16)
+    partial_hidden, late_targets = lax.optimization_barrier((partial_hidden, targets))
     parts = [partial_hidden] + [swap(partial_hidden, "latent", k) for k in range(1, latents)]
-    parts, even_targets = lax.optimization_barrier((parts, even_targets))
-    even_targets = jnp.concatenate(even_targets, axis=0)
-    odd_targets = swap(even_targets, "batch", 1)
+    far_targets = [swap(late_targets, "batch", k) for k in range(2, owners, 2)[1:2]]
     activated, pooled_grad, sending = call(
         functools.partial(turn, owners),
         (
@@ -189,6 +189,7 @@
     )
     output = lax.dynamic_slice_in_dim(activated, latent * hidden_share, hidden_share, axis=1)
 
+    sending, far_targets = lax.optimization_barrier((sending, far_targets))
     sent = lax.all_to_all(sending, ("batch", "latent"), split_axis=0, concat_axis=0, tiled=True)
     late = call(
         make_late,
@@ -196,9 +197,16 @@
         (me, weight, pooled_grad),
         [smem, vmem, vmem],
     )
-    even_late = [late[0]] + [swap(late[k // 2], "batch", k) for k in range(2, owners, 2)]
+    even_late = [late[0]] + [swap(late[k // 2], "batch", k) for k in range(2, owners, 2)[:2]]
+    even_targets = [targets] + near_targets + far_targets
+    for k in range(2, owners, 2)[2:]:
+        both = swap(jnp.concatenate([late[k // 2], targets], axis=1), "batch", k)
+        even_late.append(both[:, : late.shape[2]])
+        even_targets.append(both[:, late.shape[2] :])
     even_late = jnp.concatenate(even_late, axis=0)
     odd_late = swap(even_late, "batch", 1)
+    even_targets = jnp.concatenate(even_targets, axis=0)
+    odd_targets = swap(even_targets, "batch", 1)
     depth = owners * 4 * members
     row_grad = call(
         functools.partial(add_rows, latents),

time: 65.8 us -> 62.2 us (0.945)
  waiting for transfers between devices: 19.6 us -> 17.6 us
  starting transfers between devices: 32.5 us -> 30.8 us
    ppermute x17 -> x16, starting transfers between devices: 20.6 us -> 18.3 us  [swap(): return lax.ppermute(x, axis, [(i, i ^ k) for i in range(n)])]
    ppermute x17 -> x16, waiting for transfers between devices: 13.6 us -> 12.3 us  [swap(): return lax.ppermute(x, axis, [(i, i ^ k) for i in range(n)])]
    all_to_all x1, waiting for transfers between devices: 0.69 us -> 0.01 us  [on_device(): lax.all_to_all(sending, ('batch', 'latent'), split_axis=0, concat_axis=0,...]
  transfers between devices with their start and end apart: 20 -> 19, of which waited for: 11 -> 9; matrix products, arithmetic and copies ran while one was open for 9% -> 9% of each run, Pallas kernels for 2% -> 5%
where the time goes in v6:
time: 62.2 us; the launch traced here: 61.7 us
  starting transfers between devices  30.8 us (50%)
  waiting for transfers between devices  17.6 us (28%)
  other arithmetic  5.14 us (8%)
  Pallas kernels  4.94 us (8%)
  local copies, waits for them, and re-layouts  1.71 us (3%)
  between operations  0.83 us (1%)
  matrix products  0.68 us (1%)
    ppermute x16, starting transfers between devices, swap(): return lax.ppermute(x, axis, [(i, i ^ k) for i in range(n)])  18.3 us
    ppermute x16, waiting for transfers between devices, swap(): return lax.ppermute(x, axis, [(i, i ^ k) for i in range(n)])  12.3 us
    all_to_all x2, starting transfers between devices, exchange(): return lax.all_to_all(x, 'batch', split_axis=0, concat_axis=0, tiled=True)  9.1 us
    all_to_all x2, waiting for transfers between devices, exchange(): return lax.all_to_all(x, 'batch', split_axis=0, concat_axis=0, tiled=True)  5.35 us
    pallas_call x4, Pallas kernels, call(): pl.pallas_call(kernel, out_shape=shapes, in_specs=specs, out_specs=jax.tr...  4.94 us
    reduce_sum x1, other arithmetic, on_device(): count = jnp.sum((history[:, :, None] == slots).astype(jnp.float32), axis=1)  4.66 us
    all_to_all x1, starting transfers between devices, on_device(): lax.all_to_all(sending, ('batch', 'latent'), split_axis=0, concat_axis=0,...  3.44 us
  transfers between devices with their start and end apart: 19, of which 9 were waited for; matrix products, arithmetic and copies ran while one was open for 9% of the time, Pallas kernels for 5%

profile of v6, /device:TPU:0, one launch (start us, length us, event | category | flops | bytes accessed | tf_op | source)
XLA Modules:
  0.0 61.7 jit_solution(13145339208139750678)
XLA Ops:
  0.6 5.2 %all-to-all-start = ((s32[8,1,64]{2,1,0:T(1,128)}), s32[8,1,64]{2,1,0:T(1,128)S(1)}, u32[]{:S(2)}, u32[]{:S(2)}) async-start(s32[8,1,64]{2,1,0:T(1,128)} %bitcast.39), calls=%async_computation | async-start | bytes 8192 | tf_op jit(solution)/shard_map/all_to_all | solution.py:20
  5.8 1.6 %collective-permute-start = (bf16[32,256]{1,0:T(8,128)(2,1)}, bf16[32,256]{1,0:T(8,128)(2,1)S(1)}, u32[]{:S(2)}, u32[]{:S(2)}) collective-permute-start(bf16[32,256]{1,0:T(8,128)(2,1)} %param.13), channel_id=1, source_target_pairs={{0,1},{1,0},{2,3},{3,2},{4,5},{5,4},{6,7},{7,6},{8,9},{9,8},{10,11... | collective-permute-start | bytes 49160 | tf_op jit(solution)/shard_map/ppermute | solution.py:16
  7.4 2.5 %collective-permute-start.2 = (bf16[32,256]{1,0:T(8,128)(2,1)}, bf16[32,256]{1,0:T(8,128)(2,1)S(1)}, u32[]{:S(2)}, u32[]{:S(2)}) collective-permute-start(bf16[32,256]{1,0:T(8,128)(2,1)} %param.13), channel_id=1, source_target_pairs={{0,3},{1,2},{2,1},{3,0},{4,7},{5,6},{6,5},{7,4},{8,11},{9,10},{10,... | collective-permute-start | bytes 49160 | tf_op jit(solution)/shard_map/ppermute | solution.py:16
  9.9 0.1 collective-permute-start.1
  10.0 0.4 all-to-all-done.wanted_ref
  10.4 1.0 %copy-done.1 = bf16[512,512]{1,0:T(8,128)(2,1)S(1)} copy-done((bf16[512,512]{1,0:T(8,128)(2,1)S(1)}, bf16[512,512]{1,0:T(8,128)(2,1)}, u32[]{:S(2)}) %copy-start.1) | copy-done | bytes 524312
  11.4 1.3 %pick_rows.1 = bf16[512,512]{1,0:T(8,128)(2,1)} custom-call(s32[8,1,64]{2,1,0:T(1,128)S(1)} %all-to-all-done.wanted_ref, bf16[512,512]{1,0:T(8,128)(2,1)S(1)} %copy-done.1), custom_call_target="tpu_custom_call" | custom-call | tf_op jit(solution)/shard_map/pick_rows/pallas_call | solution.py:24
  12.8 3.9 %all-to-all-start.1 = ((bf16[8,64,512]{2,1,0:T(8,128)(2,1)}), bf16[8,64,512]{2,1,0:T(8,128)(2,1)S(1)}, u32[]{:S(2)}, u32[]{:S(2)}) async-start(bf16[8,64,512]{2,1,0:T(8,128)(2,1)} %bitcast.1), calls=%async_computation.1 | async-start | bytes 1048576 | tf_op jit(solution)/shard_map/all_to_all | solution.py:20
  16.7 0.0 copy-start
  16.7 4.7 %convert_reduce_fusion = f32[32,512]{1,0:T(8,128)S(1)} fusion(s32[32,512]{1,0:T(8,128)S(1)} %copy-done.4), kind=kLoop, calls=%fused_computation | loop fusion | flops 25149440 | bytes 131072 | tf_op jit(solution)/shard_map/reduce_sum | solution.py:161
  21.4 0.0 collective-permute-done
  21.4 0.0 collective-permute-done.2
  21.4 0.0 collective-permute-done.1
  21.5 4.9 %all-to-all-done.1 = bf16[8,64,512]{2,1,0:T(8,128)(2,1)S(1)} async-done(((bf16[8,64,512]{2,1,0:T(8,128)(2,1)}), bf16[8,64,512]{2,1,0:T(8,128)(2,1)S(1)}, u32[]{:S(2)}, u32[]{:S(2)}) %all-to-all-start.1) | async-done | bytes 524320 | tf_op jit(solution)/shard_map/all_to_all | solution.py:20
  26.5 0.2 convolution_bitcast_fusion
  26.7 3.3 %collective-permute-start.5 = (f32[32,512]{1,0:T(8,128)S(1)}, f32[32,512]{1,0:T(8,128)S(1)}, u32[]{:S(2)}, u32[]{:S(2)}) collective-permute-start(f32[32,512]{1,0:T(8,128)S(1)} %convolution_bitcast_fusion), channel_id=1, source_target_pairs={{0,3},{1,2},{2,1},{3,0},{4,7},{5,6},{6,5},{7,4},{8,11},{9,10},{10,... | collective-permute-start | bytes 196616 | tf_op jit(solution)/shard_map/ppermute | solution.py:16
  30.0 0.0 collective-permute-start.4
  30.0 1.1 %collective-permute-start.3 = (f32[32,512]{1,0:T(8,128)S(1)}, f32[32,512]{1,0:T(8,128)S(1)}, u32[]{:S(2)}, u32[]{:S(2)}) collective-permute-start(f32[32,512]{1,0:T(8,128)S(1)} %convolution_bitcast_fusion), channel_id=1, source_target_pairs={{0,1},{1,0},{2,3},{3,2},{4,5},{5,4},{6,7},{7,6},{8,9},{9,8},{10,11... | collective-permute-start | bytes 196616 | tf_op jit(solution)/shard_map/ppermute | solution.py:16
  31.1 0.6 collective-permute-start.6
  31.7 3.4 %collective-permute-done.6 = bf16[32,512]{1,0:T(8,128)(2,1)S(1)} collective-permute-done((bf16[32,512]{1,0:T(8,128)(2,1)S(1)}, bf16[32,512]{1,0:T(8,128)(2,1)S(1)}, u32[]{:S(2)}, u32[]{:S(2)}) %collective-permute-start.6) | collective-permute-done | bytes 32800 | tf_op jit(solution)/shard_map/ppermute | solution.py:16
  35.0 0.0 collective-permute-done.5
  35.0 0.4 collective-permute-done.4
  35.4 0.0 collective-permute-done.3
  35.4 0.1 select_reduce_fusion
  35.5 0.2 fusion.2
  35.7 0.1 broadcast_divide_fusion.weight_ref
  35.9 0.4 convolution_convert_fusion.refs_0_
  36.3 2.9 %collective-permute-start.9 = (bf16[32,1024]{1,0:T(8,128)(2,1)S(1)}, bf16[32,1024]{1,0:T(8,128)(2,1)S(1)}, u32[]{:S(2)}, u32[]{:S(2)}) collective-permute-start(bf16[32,1024]{1,0:T(8,128)(2,1)S(1)} %convolution_convert_fusion.refs_0_), channel_id=1, source_target_pairs={{0,3},{1,2},{2,1},{3,0},{4,7},{5,6},{6,5},{7,4},{8,11},{9,10},{10,... | collective-permute-start | bytes 196616 | tf_op jit(solution)/shard_map/ppermute | solution.py:16
  39.2 0.0 collective-permute-start.8
  39.2 1.5 %collective-permute-start.7 = (bf16[32,1024]{1,0:T(8,128)(2,1)S(1)}, bf16[32,1024]{1,0:T(8,128)(2,1)S(1)}, u32[]{:S(2)}, u32[]{:S(2)}) collective-permute-start(bf16[32,1024]{1,0:T(8,128)(2,1)S(1)} %convolution_convert_fusion.refs_0_), channel_id=1, source_target_pairs={{0,1},{1,0},{2,3},{3,2},{4,5},{5,4},{6,7},{7,6},{8,9},{9,8},{10,11... | collective-permute-start | bytes 196616 | tf_op jit(solution)/shard_map/ppermute | solution.py:16
  40.7 0.6 collective-permute-start.10
  41.3 1.1 %collective-permute-done.9.refs_3_ = bf16[32,1024]{1,0:T(8,128)(2,1)S(1)} collective-permute-done((bf16[32,1024]{1,0:T(8,128)(2,1)S(1)}, bf16[32,1024]{1,0:T(8,128)(2,1)S(1)}, u32[]{:S(2)}, u32[]{:S(2)}) %collective-permute-start.9) | collective-permute-done | bytes 65568 | tf_op jit(solution)/shard_map/ppermute | solution.py:16
  42.4 2.0 %collective-permute-done.8.refs_2_ = bf16[32,1024]{1,0:T(8,128)(2,1)S(1)} collective-permute-done((bf16[32,1024]{1,0:T(8,128)(2,1)S(1)}, bf16[32,1024]{1,0:T(8,128)(2,1)S(1)}, u32[]{:S(2)}, u32[]{:S(2)}) %collective-permute-start.8) | collective-permute-done | bytes 65568 | tf_op jit(solution)/shard_map/ppermute | solution.py:16
  44.4 0.0 collective-permute-done.7.refs_1_
  44.4 1.5 %turn.1 = (bf16[32,1024]{1,0:T(8,128)(2,1)S(1)}, bf16[32,512]{1,0:T(8,128)(2,1)S(1)}, f32[32,16,128]{2,1,0:T(8,128)}) custom-call(bf16[32,1024]{1,0:T(8,128)(2,1)S(1)} %pad_maximum_fusion.4.upstream_ref, f32[1,1024]{1,0:T(1,128)S(1)} %bitcast.34, bf16[512,1024]{1,0:T(8,128)(2,1)S(1)} %copy-done, bf16[512,512]{1,0:T(8,128)(2,1)S(1)} %bitcast.33, ...), custom_call_target="tpu_custom_call" | custom-call | tf_op jit(solution)/shard_map/turn/pallas_call | solution.py:24
  45.9 0.0 collective-permute-done.10
  45.9 3.4 %all-to-all-start.2 = ((f32[32,16,128]{2,1,0:T(8,128)}), f32[32,16,128]{2,1,0:T(8,128)S(1)}, u32[]{:S(2)}, u32[]{:S(2)}) async-start(f32[32,16,128]{2,1,0:T(8,128)} %get-tuple-element.32), calls=%async_computation.2 | async-start | bytes 524288 | tf_op jit(solution)/shard_map/all_to_all | solution.py:193
  49.4 2.7 %collective-permute-start.11 = (bf16[32,1280]{1,0:T(8,128)(2,1)S(1)}, bf16[32,1280]{1,0:T(8,128)(2,1)S(1)}, u32[]{:S(2)}, u32[]{:S(2)}) collective-permute-start(bf16[32,1280]{1,0:T(8,128)(2,1)S(1)} %pad_maximum_fusion.2), channel_id=1, source_target_pairs={{0,24},{4,28},{8,16},{12,20},{16,8},{20,12},{24,0},{28,4},{1,25},{... | collective-permute-start | bytes 245768 | tf_op jit(solution)/shard_map/ppermute | solution.py:16
  52.1 0.6 collective-permute-start.14
  52.7 0.3 collective-permute-start.13
  52.9 4.3 %collective-permute-done.11 = bf16[32,1280]{1,0:T(8,128)(2,1)S(1)} collective-permute-done((bf16[32,1280]{1,0:T(8,128)(2,1)S(1)}, bf16[32,1280]{1,0:T(8,128)(2,1)S(1)}, u32[]{:S(2)}, u32[]{:S(2)}) %collective-permute-start.11) | collective-permute-done | bytes 81952 | tf_op jit(solution)/shard_map/ppermute | solution.py:16
  57.3 0.7 %collective-permute-done.14 = bf16[32,768]{1,0:T(8,128)(2,1)S(1)} collective-permute-done((bf16[32,768]{1,0:T(8,128)(2,1)S(1)}, bf16[32,768]{1,0:T(8,128)(2,1)S(1)}, u32[]{:S(2)}, u32[]{:S(2)}) %collective-permute-start.14) | collective-permute-done | bytes 49184 | tf_op jit(solution)/shard_map/ppermute | solution.py:16
  58.0 0.1 collective-permute-start.15
  58.1 0.5 collective-permute-start.12
  58.6 0.6 constant_dynamic-slice_fusion
  59.2 0.4 collective-permute-done.12.refs_1_
  59.7 0.0 collective-permute-done.15.refs_3_
  59.7 2.1 %add_rows.1 = f32[512,512]{1,0:T(8,128)} custom-call(s32[1]{0:T(128)} %bitcast.13.me_ref, s32[8,1,64]{2,1,0:T(1,128)S(1)} %all-to-all-done.wanted_ref, f32[32,16,128]{2,1,0:T(8,128)S(1)} %all-to-all-done.2.sent_ref, bf16[128,512]{1,0:T(8,128)(2,1)S(1)} %pad_maximum_fusion.1.refs_0_, bf16[128,512]{1,0:T(8,128)(2,1)S(1)} %collective-permute-done.12.refs_1_, ...), custom_call_target="tpu_custom_call" | custom-call | tf_op jit(solution)/shard_map/add_rows/pallas_call | solution.py:24
  (22 shorter events, 0.1 us)
Async XLA Ops:
  0.6 9.8 %all-to-all-start = ((s32[8,1,64]{2,1,0:T(1,128)}), s32[8,1,64]{2,1,0:T(1,128)S(1)}, u32[]{:S(2)}, u32[]{:S(2)}) async-start(s32[8,1,64]{2,1,0:T(1,128)} %bitcast.39), calls=%async_computation | async-start | bytes 8192 | tf_op jit(solution)/shard_map/all_to_all | solution.py:20
  5.8 15.6 %collective-permute-start = (bf16[32,256]{1,0:T(8,128)(2,1)}, bf16[32,256]{1,0:T(8,128)(2,1)S(1)}, u32[]{:S(2)}, u32[]{:S(2)}) collective-permute-start(bf16[32,256]{1,0:T(8,128)(2,1)} %param.13), channel_id=1, source_target_pairs={{0,1},{1,0},{2,3},{3,2},{4,5},{5,4},{6,7},{7,6},{8,9},{9,8},{10,11... | collective-permute-start | bytes 49160 | tf_op jit(solution)/shard_map/ppermute | solution.py:16
  7.4 14.0 %collective-permute-start.2 = (bf16[32,256]{1,0:T(8,128)(2,1)}, bf16[32,256]{1,0:T(8,128)(2,1)S(1)}, u32[]{:S(2)}, u32[]{:S(2)}) collective-permute-start(bf16[32,256]{1,0:T(8,128)(2,1)} %param.13), channel_id=1, source_target_pairs={{0,3},{1,2},{2,1},{3,0},{4,7},{5,6},{6,5},{7,4},{8,11},{9,10},{10,... | collective-permute-start | bytes 49160 | tf_op jit(solution)/shard_map/ppermute | solution.py:16
  9.9 11.6 %collective-permute-start.1 = (bf16[32,256]{1,0:T(8,128)(2,1)}, bf16[32,256]{1,0:T(8,128)(2,1)S(1)}, u32[]{:S(2)}, u32[]{:S(2)}) collective-permute-start(bf16[32,256]{1,0:T(8,128)(2,1)} %param.13), channel_id=1, source_target_pairs={{0,2},{1,3},{2,0},{3,1},{4,6},{5,7},{6,4},{7,5},{8,10},{9,11},{10,... | collective-permute-start | bytes 49160 | tf_op jit(solution)/shard_map/ppermute | solution.py:16
  10.4 1.0 %copy-start.1 = (bf16[512,512]{1,0:T(8,128)(2,1)S(1)}, bf16[512,512]{1,0:T(8,128)(2,1)}, u32[]{:S(2)}) copy-start(bf16[512,512]{1,0:T(8,128)(2,1)} %rows_ref.1) | copy-start | bytes 1572868
  11.4 5.3 %copy-start.4 = (s32[32,512]{1,0:T(8,128)S(1)}, s32[32,512]{1,0:T(8,128)}, u32[]{:S(2)}) copy-start(s32[32,512]{1,0:T(8,128)} %param.11) | copy-start | bytes 196612
  11.4 10.0 %copy-start.5 = (bf16[32,256]{1,0:T(8,128)(2,1)S(1)}, bf16[32,256]{1,0:T(8,128)(2,1)}, u32[]{:S(2)}) copy-start(bf16[32,256]{1,0:T(8,128)(2,1)} %param.13) | copy-start | bytes 49156
  12.8 13.7 %copy-start.3 = (bf16[32,512]{1,0:T(8,128)(2,1)S(1)}, bf16[32,512]{1,0:T(8,128)(2,1)}, u32[]{:S(2)}) copy-start(bf16[32,512]{1,0:T(8,128)(2,1)} %param.8) | copy-start | bytes 98308
  12.8 13.7 %all-to-all-start.1 = ((bf16[8,64,512]{2,1,0:T(8,128)(2,1)}), bf16[8,64,512]{2,1,0:T(8,128)(2,1)S(1)}, u32[]{:S(2)}, u32[]{:S(2)}) async-start(bf16[8,64,512]{2,1,0:T(8,128)(2,1)} %bitcast.1), calls=%async_computation.1 | async-start | bytes 1048576 | tf_op jit(solution)/shard_map/all_to_all | solution.py:20
  16.7 19.1 %copy-start = (bf16[512,1024]{1,0:T(8,128)(2,1)S(1)}, bf16[512,1024]{1,0:T(8,128)(2,1)}, u32[]{:S(2)}) copy-start(bf16[512,1024]{1,0:T(8,128)(2,1)} %w_up_ref.1) | copy-start | bytes 3145732
  26.7 8.3 %collective-permute-start.5 = (f32[32,512]{1,0:T(8,128)S(1)}, f32[32,512]{1,0:T(8,128)S(1)}, u32[]{:S(2)}, u32[]{:S(2)}) collective-permute-start(f32[32,512]{1,0:T(8,128)S(1)} %convolution_bitcast_fusion), channel_id=1, source_target_pairs={{0,3},{1,2},{2,1},{3,0},{4,7},{5,6},{6,5},{7,4},{8,11},{9,10},{10,... | collective-permute-start | bytes 196616 | tf_op jit(solution)/shard_map/ppermute | solution.py:16
  30.0 5.4 %collective-permute-start.4 = (f32[32,512]{1,0:T(8,128)S(1)}, f32[32,512]{1,0:T(8,128)S(1)}, u32[]{:S(2)}, u32[]{:S(2)}) collective-permute-start(f32[32,512]{1,0:T(8,128)S(1)} %convolution_bitcast_fusion), channel_id=1, source_target_pairs={{0,2},{1,3},{2,0},{3,1},{4,6},{5,7},{6,4},{7,5},{8,10},{9,11},{10,... | collective-permute-start | bytes 196616 | tf_op jit(solution)/shard_map/ppermute | solution.py:16
  30.0 5.4 %collective-permute-start.3 = (f32[32,512]{1,0:T(8,128)S(1)}, f32[32,512]{1,0:T(8,128)S(1)}, u32[]{:S(2)}, u32[]{:S(2)}) collective-permute-start(f32[32,512]{1,0:T(8,128)S(1)} %convolution_bitcast_fusion), channel_id=1, source_target_pairs={{0,1},{1,0},{2,3},{3,2},{4,5},{5,4},{6,7},{7,6},{8,9},{9,8},{10,11... | collective-permute-start | bytes 196616 | tf_op jit(solution)/shard_map/ppermute | solution.py:16
  31.1 3.9 %collective-permute-start.6 = (bf16[32,512]{1,0:T(8,128)(2,1)S(1)}, bf16[32,512]{1,0:T(8,128)(2,1)S(1)}, u32[]{:S(2)}, u32[]{:S(2)}) collective-permute-start(bf16[32,512]{1,0:T(8,128)(2,1)S(1)} %copy-done.3), channel_id=1, source_target_pairs={{0,8},{4,12},{8,0},{12,4},{16,24},{20,28},{24,16},{28,20},{1,9},{5... | collective-permute-start | bytes 98312 | tf_op jit(solution)/shard_map/ppermute | solution.py:16
  35.5 8.8 %copy-start.2 = (f32[1024]{0:T(1024)S(1)}, f32[1024]{0:T(1024)}, u32[]{:S(2)}) copy-start(f32[1024]{0:T(1024)} %param.10) | copy-start | bytes 12292
  36.3 6.1 %collective-permute-start.9 = (bf16[32,1024]{1,0:T(8,128)(2,1)S(1)}, bf16[32,1024]{1,0:T(8,128)(2,1)S(1)}, u32[]{:S(2)}, u32[]{:S(2)}) collective-permute-start(bf16[32,1024]{1,0:T(8,128)(2,1)S(1)} %convolution_convert_fusion.refs_0_), channel_id=1, source_target_pairs={{0,3},{1,2},{2,1},{3,0},{4,7},{5,6},{6,5},{7,4},{8,11},{9,10},{10,... | collective-permute-start | bytes 196616 | tf_op jit(solution)/shard_map/ppermute | solution.py:16
  39.2 5.2 %collective-permute-start.8 = (bf16[32,1024]{1,0:T(8,128)(2,1)S(1)}, bf16[32,1024]{1,0:T(8,128)(2,1)S(1)}, u32[]{:S(2)}, u32[]{:S(2)}) collective-permute-start(bf16[32,1024]{1,0:T(8,128)(2,1)S(1)} %convolution_convert_fusion.refs_0_), channel_id=1, source_target_pairs={{0,2},{1,3},{2,0},{3,1},{4,6},{5,7},{6,4},{7,5},{8,10},{9,11},{10,... | collective-permute-start | bytes 196616 | tf_op jit(solution)/shard_map/ppermute | solution.py:16
  39.2 5.2 %collective-permute-start.7 = (bf16[32,1024]{1,0:T(8,128)(2,1)S(1)}, bf16[32,1024]{1,0:T(8,128)(2,1)S(1)}, u32[]{:S(2)}, u32[]{:S(2)}) collective-permute-start(bf16[32,1024]{1,0:T(8,128)(2,1)S(1)} %convolution_convert_fusion.refs_0_), channel_id=1, source_target_pairs={{0,1},{1,0},{2,3},{3,2},{4,5},{5,4},{6,7},{7,6},{8,9},{9,8},{10,11... | collective-permute-start | bytes 196616 | tf_op jit(solution)/shard_map/ppermute | solution.py:16
  40.7 5.2 %collective-permute-start.10 = (bf16[32,512]{1,0:T(8,128)(2,1)S(1)}, bf16[32,512]{1,0:T(8,128)(2,1)S(1)}, u32[]{:S(2)}, u32[]{:S(2)}) collective-permute-start(bf16[32,512]{1,0:T(8,128)(2,1)S(1)} %copy-done.3), channel_id=1, source_target_pairs={{0,16},{4,20},{8,24},{12,28},{16,0},{20,4},{24,8},{28,12},{1,17},{... | collective-permute-start | bytes 98312 | tf_op jit(solution)/shard_map/ppermute | solution.py:16
  45.9 13.8 %all-to-all-start.2 = ((f32[32,16,128]{2,1,0:T(8,128)}), f32[32,16,128]{2,1,0:T(8,128)S(1)}, u32[]{:S(2)}, u32[]{:S(2)}) async-start(f32[32,16,128]{2,1,0:T(8,128)} %get-tuple-element.32), calls=%async_computation.2 | async-start | bytes 524288 | tf_op jit(solution)/shard_map/all_to_all | solution.py:193
  49.4 7.9 %collective-permute-start.11 = (bf16[32,1280]{1,0:T(8,128)(2,1)S(1)}, bf16[32,1280]{1,0:T(8,128)(2,1)S(1)}, u32[]{:S(2)}, u32[]{:S(2)}) collective-permute-start(bf16[32,1280]{1,0:T(8,128)(2,1)S(1)} %pad_maximum_fusion.2), channel_id=1, source_target_pairs={{0,24},{4,28},{8,16},{12,20},{16,8},{20,12},{24,0},{28,4},{1,25},{... | collective-permute-start | bytes 245768 | tf_op jit(solution)/shard_map/ppermute | solution.py:16
  52.1 5.8 %collective-permute-start.14 = (bf16[32,768]{1,0:T(8,128)(2,1)S(1)}, bf16[32,768]{1,0:T(8,128)(2,1)S(1)}, u32[]{:S(2)}, u32[]{:S(2)}) collective-permute-start(bf16[32,768]{1,0:T(8,128)(2,1)S(1)} %get-tuple-element.39), channel_id=1, source_target_pairs={{0,16},{4,20},{8,24},{12,28},{16,0},{20,4},{24,8},{28,12},{1,17},{... | collective-permute-start | bytes 147464 | tf_op jit(solution)/shard_map/ppermute | solution.py:16
  52.7 5.3 %collective-permute-start.13 = (bf16[32,768]{1,0:T(8,128)(2,1)S(1)}, bf16[32,768]{1,0:T(8,128)(2,1)S(1)}, u32[]{:S(2)}, u32[]{:S(2)}) collective-permute-start(bf16[32,768]{1,0:T(8,128)(2,1)S(1)} %get-tuple-element.40), channel_id=1, source_target_pairs={{0,8},{4,12},{8,0},{12,4},{16,24},{20,28},{24,16},{28,20},{1,9},{5... | collective-permute-start | bytes 147464 | tf_op jit(solution)/shard_map/ppermute | solution.py:16
  58.0 1.7 %collective-permute-start.15 = (bf16[128,768]{1,0:T(8,128)(2,1)S(1)}, bf16[128,768]{1,0:T(8,128)(2,1)S(1)}, u32[]{:S(2)}, u32[]{:S(2)}) collective-permute-start(bf16[128,768]{1,0:T(8,128)(2,1)S(1)} %pad_maximum_fusion.refs_2_), channel_id=1, source_target_pairs={{0,4},{4,0},{8,12},{12,8},{16,20},{20,16},{24,28},{28,24},{1,5},{5... | collective-permute-start | bytes 589832 | tf_op jit(solution)/shard_map/ppermute | solution.py:16
  58.1 1.6 %collective-permute-start.12 = (bf16[128,512]{1,0:T(8,128)(2,1)S(1)}, bf16[128,512]{1,0:T(8,128)(2,1)S(1)}, u32[]{:S(2)}, u32[]{:S(2)}) collective-permute-start(bf16[128,512]{1,0:T(8,128)(2,1)S(1)} %pad_maximum_fusion.1.refs_0_), channel_id=1, source_target_pairs={{0,4},{4,0},{8,12},{12,8},{16,20},{20,16},{24,28},{28,24},{1,5},{5... | collective-permute-start | bytes 393224 | tf_op jit(solution)/shard_map/ppermute | solution.py:16

commit v7 on v6

--- a/solution.py
+++ b/solution.py
@@ -32,6 +32,10 @@
     )(*operands)
 
 
+def hold_rows(rows_ref, out_ref):
+    out_ref[...] = rows_ref[...]
+
+
 def pick_rows(wanted_ref, rows_ref, out_ref):
     owners, capacity = wanted_ref.shape[0], wanted_ref.shape[2]
     stored = rows_ref.shape[0]
@@ -43,6 +47,37 @@
     out_ref[...] = jnp.dot(chosen, rows_ref[...], preferred_element_type=jnp.float32).astype(
         jnp.bfloat16
     )
+
+
+def count_slots(history_ref, out_ref):
+    members, listed = history_ref.shape
+    lanes = 128
+    blocks = out_ref.shape[1] // lanes
+    padded = -(-blocks // 8) * 8
+    block_of = lax.broadcasted_iota(jnp.int32, (padded, listed), 0)
+    lane_of = lax.broadcasted_iota(jnp.int32, (lanes, listed), 0)
+    history = history_ref[...]
+    block, lane = jnp.right_shift(history, 7), jnp.bitwise_and(history, lanes - 1)
+
+    def marks(x, places, users):
+        return jnp.concatenate(
+            [(x[u : u + 1, :] == places).astype(jnp.bfloat16) for u in users], axis=0
+        )
+
+    for first in range(0, members, 2):
+        users = (first, first + 1)
+        counts = lax.dot_general(
+            marks(block, block_of, users),
+            marks(lane, lane_of, users),
+            (((1,), (1,)), ((), ())),
+            preferred_element_type=jnp.float32,
+        )
+        for i, u in enumerate(users):
+            for b in range(blocks):
+                row = i * padded + b
+                out_ref[u : u + 1, b * lanes : (b + 1) * lanes] = counts[
+                    row : row + 1, i * lanes : (i + 1) * lanes
+                ]
 
 
 def turn(owners, upstream_ref, bias_ref, w_up_ref, fetched_ref, weight_ref, *refs):
@@ -153,14 +188,17 @@
         [lax.dynamic_index_in_dim(parts, latent ^ z, 0, keepdims=False) for z in range(latents)],
         axis=1,
     )
+    count = call(
+        count_slots, shape((members, slot_count), jnp.float32), (history,), [vmem]
+    )
+    held = call(hold_rows, shape(rows.shape, bf16), (rows,), [vmem])
+    wanted, count = lax.optimization_barrier((wanted, count))
     chosen = call(
-        pick_rows, shape((slot_count, row_width), bf16), (wanted, rows), [vmem, vmem]
-    )
-
-    slots = lax.broadcasted_iota(jnp.int32, (1, 1, slot_count), 2)
-    count = jnp.sum((history[:, :, None] == slots).astype(jnp.float32), axis=1)
+        pick_rows, shape((slot_count, row_width), bf16), (wanted, held), [vmem, vmem]
+    )
+
     fetched = exchange(chosen.reshape(owners, capacity, row_width)).reshape(slot_count, row_width)
-    fetched, count, upstream_full = lax.optimization_barrier((fetched, count, upstream_full))
+    fetched, upstream_full = lax.optimization_barrier((fetched, upstream_full))
 
     slot_scores = jnp.einsum("ud,sd->us", targets, fetched, preferred_element_type=jnp.float32)
     late_targets, slot_scores = lax.optimization_barrier((targets, slot_scores))

time: 62.2 us -> 61.2 us (0.984)
  other arithmetic: 5.14 us -> 0.48 us
  Pallas kernels: 4.94 us -> 6.16 us
  waiting for transfers between devices: 17.6 us -> 18.8 us
  local copies, waits for them, and re-layouts: 1.71 us -> 2.56 us
    reduce_sum x1 -> x0, other arithmetic: 4.66 us -> none  [on_device(): count = jnp.sum((history[:, :, None] == slots).astype(jnp.float32), axis=1)]
    ppermute x16, waiting for transfers between devices: 12.3 us -> 16.5 us  [swap(): return lax.ppermute(x, axis, [(i, i ^ k) for i in range(n)])]
    all_to_all x2, waiting for transfers between devices: 5.35 us -> 2.26 us  [exchange(): return lax.all_to_all(x, 'batch', split_axis=0, concat_axis=0, tiled=True)]
    pallas_call x4 -> x6, Pallas kernels: 4.94 us -> 6.16 us  [call(): pl.pallas_call(kernel, out_shape=shapes, in_specs=specs, out_specs=jax.tr...]
    unnamed x12, local copies, waits for them, and re-layouts: 1.06 us -> 1.91 us
    ppermute x16, starting transfers between devices: 18.3 us -> 19 us  [swap(): return lax.ppermute(x, axis, [(i, i ^ k) for i in range(n)])]
  transfers between devices with their start and end apart: 19 -> 19, of which waited for: 9 -> 11; matrix products, arithmetic and copies ran while one was open for 9% -> 1% of each run, Pallas kernels for 5% -> 5%
where the time goes in v7:
time: 61.2 us; the launch traced here: 60.7 us
  starting transfers between devices  31.3 us (51%)
  waiting for transfers between devices  18.8 us (31%)
  Pallas kernels  6.16 us (10%)
  local copies, waits for them, and re-layouts  2.56 us (4%)
  between operations  0.79 us (1%)
  matrix products  0.69 us (1%)
    ppermute x16, starting transfers between devices, swap(): return lax.ppermute(x, axis, [(i, i ^ k) for i in range(n)])  19 us
    ppermute x16, waiting for transfers between devices, swap(): return lax.ppermute(x, axis, [(i, i ^ k) for i in range(n)])  16.5 us
    all_to_all x2, starting transfers between devices, exchange(): return lax.all_to_all(x, 'batch', split_axis=0, concat_axis=0, tiled=True)  8.81 us
    pallas_call x6, Pallas kernels, call(): pl.pallas_call(kernel, out_shape=shapes, in_specs=specs, out_specs=jax.tr...  6.16 us
    all_to_all x1, starting transfers between devices, on_device(): lax.all_to_all(sending, ('batch', 'latent'), split_axis=0, concat_axis=0,...  3.44 us
    all_to_all x2, waiting for transfers between devices, exchange(): return lax.all_to_all(x, 'batch', split_axis=0, concat_axis=0, tiled=True)  2.26 us
    unnamed x12, local copies, waits for them, and re-layouts  1.91 us
  transfers between devices with their start and end apart: 19, of which 11 were waited for; matrix products, arithmetic and copies ran while one was open for 1% of the time, Pallas kernels for 5%

profile of v7, /device:TPU:0, one launch (start us, length us, event | category | flops | bytes accessed | tf_op | source)
XLA Modules:
  0.0 60.7 jit_solution(16423917928464621778)
XLA Ops:
  0.6 5.2 %all-to-all-start = ((s32[8,1,64]{2,1,0:T(1,128)}), s32[8,1,64]{2,1,0:T(1,128)S(1)}, u32[]{:S(2)}, u32[]{:S(2)}) async-start(s32[8,1,64]{2,1,0:T(1,128)} %bitcast.39), calls=%async_computation | async-start | bytes 8192 | tf_op jit(solution)/shard_map/all_to_all | solution.py:20
  5.8 0.8 %copy-done.2 = s32[32,512]{1,0:T(8,128)S(1)} copy-done((s32[32,512]{1,0:T(8,128)S(1)}, s32[32,512]{1,0:T(8,128)}, u32[]{:S(2)}) %copy-start.2) | copy-done | bytes 65560
  6.7 1.2 %count_slots.1 = f32[32,512]{1,0:T(8,128)S(1)} custom-call(s32[32,512]{1,0:T(8,128)S(1)} %copy-done.2), custom_call_target="tpu_custom_call" | custom-call | tf_op jit(solution)/shard_map/count_slots/pallas_call | solution.py:24
  7.9 1.1 %copy-done.1 = bf16[512,512]{1,0:T(8,128)(2,1)S(1)} copy-done((bf16[512,512]{1,0:T(8,128)(2,1)S(1)}, bf16[512,512]{1,0:T(8,128)(2,1)}, u32[]{:S(2)}) %copy-start.1) | copy-done | bytes 524312
  8.9 1.5 %all-to-all-done.wanted_ref = s32[8,1,64]{2,1,0:T(1,128)S(1)} async-done(((s32[8,1,64]{2,1,0:T(1,128)}), s32[8,1,64]{2,1,0:T(1,128)S(1)}, u32[]{:S(2)}, u32[]{:S(2)}) %all-to-all-start) | async-done | bytes 2080 | tf_op jit(solution)/shard_map/all_to_all | solution.py:20
  10.4 1.3 %pick_rows.1 = bf16[512,512]{1,0:T(8,128)(2,1)} custom-call(s32[8,1,64]{2,1,0:T(1,128)S(1)} %all-to-all-done.wanted_ref, bf16[512,512]{1,0:T(8,128)(2,1)S(1)} %hold_rows.1.rows_ref), custom_call_target="tpu_custom_call" | custom-call | tf_op jit(solution)/shard_map/pick_rows/pallas_call | solution.py:24
  11.8 3.6 %all-to-all-start.1 = ((bf16[8,64,512]{2,1,0:T(8,128)(2,1)}), bf16[8,64,512]{2,1,0:T(8,128)(2,1)S(1)}, u32[]{:S(2)}, u32[]{:S(2)}) async-start(bf16[8,64,512]{2,1,0:T(8,128)(2,1)} %bitcast.1), calls=%async_computation.1 | async-start | bytes 1048576 | tf_op jit(solution)/shard_map/all_to_all | solution.py:20
  15.4 0.0 copy-start
  15.4 1.7 %collective-permute-start = (bf16[32,256]{1,0:T(8,128)(2,1)S(1)}, bf16[32,256]{1,0:T(8,128)(2,1)S(1)}, u32[]{:S(2)}, u32[]{:S(2)}) collective-permute-start(bf16[32,256]{1,0:T(8,128)(2,1)S(1)} %copy-done.5), channel_id=1, source_target_pairs={{0,1},{1,0},{2,3},{3,2},{4,5},{5,4},{6,7},{7,6},{8,9},{9,8},{10,11... | collective-permute-start | bytes 49160 | tf_op jit(solution)/shard_map/ppermute | solution.py:16
  17.1 2.5 %collective-permute-start.2 = (bf16[32,256]{1,0:T(8,128)(2,1)S(1)}, bf16[32,256]{1,0:T(8,128)(2,1)S(1)}, u32[]{:S(2)}, u32[]{:S(2)}) collective-permute-start(bf16[32,256]{1,0:T(8,128)(2,1)S(1)} %copy-done.5), channel_id=1, source_target_pairs={{0,3},{1,2},{2,1},{3,0},{4,7},{5,6},{6,5},{7,4},{8,11},{9,10},{10,... | collective-permute-start | bytes 49160 | tf_op jit(solution)/shard_map/ppermute | solution.py:16
  19.5 0.1 collective-permute-start.1
  19.7 0.0 collective-permute-done
  19.7 2.9 %collective-permute-done.2 = bf16[32,256]{1,0:T(8,128)(2,1)S(1)} collective-permute-done((bf16[32,256]{1,0:T(8,128)(2,1)S(1)}, bf16[32,256]{1,0:T(8,128)(2,1)S(1)}, u32[]{:S(2)}, u32[]{:S(2)}) %collective-permute-start.2) | collective-permute-done | bytes 16416 | tf_op jit(solution)/shard_map/ppermute | solution.py:16
  22.6 1.6 %collective-permute-done.1 = bf16[32,256]{1,0:T(8,128)(2,1)S(1)} collective-permute-done((bf16[32,256]{1,0:T(8,128)(2,1)S(1)}, bf16[32,256]{1,0:T(8,128)(2,1)S(1)}, u32[]{:S(2)}, u32[]{:S(2)}) %collective-permute-start.1) | collective-permute-done | bytes 16416 | tf_op jit(solution)/shard_map/ppermute | solution.py:16
  24.2 0.8 %all-to-all-done.1 = bf16[8,64,512]{2,1,0:T(8,128)(2,1)S(1)} async-done(((bf16[8,64,512]{2,1,0:T(8,128)(2,1)}), bf16[8,64,512]{2,1,0:T(8,128)(2,1)S(1)}, u32[]{:S(2)}, u32[]{:S(2)}) %all-to-all-start.1) | async-done | bytes 524320 | tf_op jit(solution)/shard_map/all_to_all | solution.py:20
  25.1 0.2 convolution_bitcast_fusion
  25.3 3.6 %collective-permute-start.5 = (f32[32,512]{1,0:T(8,128)S(1)}, f32[32,512]{1,0:T(8,128)S(1)}, u32[]{:S(2)}, u32[]{:S(2)}) collective-permute-start(f32[32,512]{1,0:T(8,128)S(1)} %convolution_bitcast_fusion), channel_id=1, source_target_pairs={{0,3},{1,2},{2,1},{3,0},{4,7},{5,6},{6,5},{7,4},{8,11},{9,10},{10,... | collective-permute-start | bytes 196616 | tf_op jit(solution)/shard_map/ppermute | solution.py:16
  28.9 0.0 collective-permute-start.4
  28.9 0.8 %collective-permute-start.3 = (f32[32,512]{1,0:T(8,128)S(1)}, f32[32,512]{1,0:T(8,128)S(1)}, u32[]{:S(2)}, u32[]{:S(2)}) collective-permute-start(f32[32,512]{1,0:T(8,128)S(1)} %convolution_bitcast_fusion), channel_id=1, source_target_pairs={{0,1},{1,0},{2,3},{3,2},{4,5},{5,4},{6,7},{7,6},{8,9},{9,8},{10,11... | collective-permute-start | bytes 196616 | tf_op jit(solution)/shard_map/ppermute | solution.py:16
  29.7 1.1 %collective-permute-start.6 = (bf16[32,512]{1,0:T(8,128)(2,1)S(1)}, bf16[32,512]{1,0:T(8,128)(2,1)S(1)}, u32[]{:S(2)}, u32[]{:S(2)}) collective-permute-start(bf16[32,512]{1,0:T(8,128)(2,1)S(1)} %copy-done.4), channel_id=1, source_target_pairs={{0,8},{4,12},{8,0},{12,4},{16,24},{20,28},{24,16},{28,20},{1,9},{5... | collective-permute-start | bytes 98312 | tf_op jit(solution)/shard_map/ppermute | solution.py:16
  30.8 2.8 %collective-permute-done.6 = bf16[32,512]{1,0:T(8,128)(2,1)S(1)} collective-permute-done((bf16[32,512]{1,0:T(8,128)(2,1)S(1)}, bf16[32,512]{1,0:T(8,128)(2,1)S(1)}, u32[]{:S(2)}, u32[]{:S(2)}) %collective-permute-start.6) | collective-permute-done | bytes 32800 | tf_op jit(solution)/shard_map/ppermute | solution.py:16
  33.6 0.0 collective-permute-done.5
  33.6 0.5 collective-permute-done.4
  34.1 0.1 select_reduce_fusion
  34.2 0.2 fusion.2
  34.4 0.1 broadcast_divide_fusion.weight_ref
  34.5 0.4 convolution_convert_fusion.refs_0_
  35.0 0.0 copy-start.3
  35.0 3.2 %collective-permute-start.9 = (bf16[32,1024]{1,0:T(8,128)(2,1)S(1)}, bf16[32,1024]{1,0:T(8,128)(2,1)S(1)}, u32[]{:S(2)}, u32[]{:S(2)}) collective-permute-start(bf16[32,1024]{1,0:T(8,128)(2,1)S(1)} %convolution_convert_fusion.refs_0_), channel_id=1, source_target_pairs={{0,3},{1,2},{2,1},{3,0},{4,7},{5,6},{6,5},{7,4},{8,11},{9,10},{10,... | collective-permute-start | bytes 196616 | tf_op jit(solution)/shard_map/ppermute | solution.py:16
  38.2 0.0 collective-permute-start.8
  38.2 1.2 %collective-permute-start.7 = (bf16[32,1024]{1,0:T(8,128)(2,1)S(1)}, bf16[32,1024]{1,0:T(8,128)(2,1)S(1)}, u32[]{:S(2)}, u32[]{:S(2)}) collective-permute-start(bf16[32,1024]{1,0:T(8,128)(2,1)S(1)} %convolution_convert_fusion.refs_0_), channel_id=1, source_target_pairs={{0,1},{1,0},{2,3},{3,2},{4,5},{5,4},{6,7},{7,6},{8,9},{9,8},{10,11... | collective-permute-start | bytes 196616 | tf_op jit(solution)/shard_map/ppermute | solution.py:16
  39.5 0.7 %collective-permute-start.10 = (bf16[32,512]{1,0:T(8,128)(2,1)S(1)}, bf16[32,512]{1,0:T(8,128)(2,1)S(1)}, u32[]{:S(2)}, u32[]{:S(2)}) collective-permute-start(bf16[32,512]{1,0:T(8,128)(2,1)S(1)} %copy-done.4), channel_id=1, source_target_pairs={{0,16},{4,20},{8,24},{12,28},{16,0},{20,4},{24,8},{28,12},{1,17},{... | collective-permute-start | bytes 98312 | tf_op jit(solution)/shard_map/ppermute | solution.py:16
  40.1 1.1 %collective-permute-done.9.refs_3_ = bf16[32,1024]{1,0:T(8,128)(2,1)S(1)} collective-permute-done((bf16[32,1024]{1,0:T(8,128)(2,1)S(1)}, bf16[32,1024]{1,0:T(8,128)(2,1)S(1)}, u32[]{:S(2)}, u32[]{:S(2)}) %collective-permute-start.9) | collective-permute-done | bytes 65568 | tf_op jit(solution)/shard_map/ppermute | solution.py:16
  41.2 2.2 %collective-permute-done.8.refs_2_ = bf16[32,1024]{1,0:T(8,128)(2,1)S(1)} collective-permute-done((bf16[32,1024]{1,0:T(8,128)(2,1)S(1)}, bf16[32,1024]{1,0:T(8,128)(2,1)S(1)}, u32[]{:S(2)}, u32[]{:S(2)}) %collective-permute-start.8) | collective-permute-done | bytes 65568 | tf_op jit(solution)/shard_map/ppermute | solution.py:16
  43.4 0.0 collective-permute-done.7.refs_1_
  43.4 1.5 %turn.1 = (bf16[32,1024]{1,0:T(8,128)(2,1)S(1)}, bf16[32,512]{1,0:T(8,128)(2,1)S(1)}, f32[32,16,128]{2,1,0:T(8,128)}) custom-call(bf16[32,1024]{1,0:T(8,128)(2,1)S(1)} %pad_maximum_fusion.4.upstream_ref, f32[1,1024]{1,0:T(1,128)S(1)} %bitcast.34, bf16[512,1024]{1,0:T(8,128)(2,1)S(1)} %copy-done, bf16[512,512]{1,0:T(8,128)(2,1)S(1)} %bitcast.33, ...), custom_call_target="tpu_custom_call" | custom-call | tf_op jit(solution)/shard_map/turn/pallas_call | solution.py:24
  44.9 3.4 %all-to-all-start.2 = ((f32[32,16,128]{2,1,0:T(8,128)}), f32[32,16,128]{2,1,0:T(8,128)S(1)}, u32[]{:S(2)}, u32[]{:S(2)}) async-start(f32[32,16,128]{2,1,0:T(8,128)} %get-tuple-element.34), calls=%async_computation.2 | async-start | bytes 524288 | tf_op jit(solution)/shard_map/all_to_all | solution.py:231
  48.4 2.7 %collective-permute-start.11 = (bf16[32,1280]{1,0:T(8,128)(2,1)S(1)}, bf16[32,1280]{1,0:T(8,128)(2,1)S(1)}, u32[]{:S(2)}, u32[]{:S(2)}) collective-permute-start(bf16[32,1280]{1,0:T(8,128)(2,1)S(1)} %pad_maximum_fusion.2), channel_id=1, source_target_pairs={{0,24},{4,28},{8,16},{12,20},{16,8},{20,12},{24,0},{28,4},{1,25},{... | collective-permute-start | bytes 245768 | tf_op jit(solution)/shard_map/ppermute | solution.py:16
  51.1 0.6 collective-permute-start.14
  51.7 0.3 collective-permute-start.13
  51.9 4.3 %collective-permute-done.11 = bf16[32,1280]{1,0:T(8,128)(2,1)S(1)} collective-permute-done((bf16[32,1280]{1,0:T(8,128)(2,1)S(1)}, bf16[32,1280]{1,0:T(8,128)(2,1)S(1)}, u32[]{:S(2)}, u32[]{:S(2)}) %collective-permute-start.11) | collective-permute-done | bytes 81952 | tf_op jit(solution)/shard_map/ppermute | solution.py:16
  56.3 0.7 %collective-permute-done.14 = bf16[32,768]{1,0:T(8,128)(2,1)S(1)} collective-permute-done((bf16[32,768]{1,0:T(8,128)(2,1)S(1)}, bf16[32,768]{1,0:T(8,128)(2,1)S(1)}, u32[]{:S(2)}, u32[]{:S(2)}) %collective-permute-start.14) | collective-permute-done | bytes 49184 | tf_op jit(solution)/shard_map/ppermute | solution.py:16
  56.9 0.0 collective-permute-done.13
  57.0 0.1 collective-permute-start.15
  57.1 0.5 collective-permute-start.12
  57.6 0.6 constant_dynamic-slice_fusion
  58.2 0.4 collective-permute-done.12.refs_1_
  58.7 2.1 %add_rows.1 = f32[512,512]{1,0:T(8,128)} custom-call(s32[1]{0:T(128)} %bitcast.13.me_ref, s32[8,1,64]{2,1,0:T(1,128)S(1)} %all-to-all-done.wanted_ref, f32[32,16,128]{2,1,0:T(8,128)S(1)} %all-to-all-done.2.sent_ref, bf16[128,512]{1,0:T(8,128)(2,1)S(1)} %pad_maximum_fusion.1.refs_0_, bf16[128,512]{1,0:T(8,128)(2,1)S(1)} %collective-permute-done.12.refs_1_, ...), custom_call_target="tpu_custom_call" | custom-call | tf_op jit(solution)/shard_map/add_rows/pallas_call | solution.py:24
  (23 shorter events, 0.2 us)
Async XLA Ops:
  0.6 9.8 %all-to-all-start = ((s32[8,1,64]{2,1,0:T(1,128)}), s32[8,1,64]{2,1,0:T(1,128)S(1)}, u32[]{:S(2)}, u32[]{:S(2)}) async-start(s32[8,1,64]{2,1,0:T(1,128)} %bitcast.39), calls=%async_computation | async-start | bytes 8192 | tf_op jit(solution)/shard_map/all_to_all | solution.py:20
  5.8 0.8 %copy-start.2 = (s32[32,512]{1,0:T(8,128)S(1)}, s32[32,512]{1,0:T(8,128)}, u32[]{:S(2)}) copy-start(s32[32,512]{1,0:T(8,128)} %history_ref.1) | copy-start | bytes 196612
  7.9 1.1 %copy-start.1 = (bf16[512,512]{1,0:T(8,128)(2,1)S(1)}, bf16[512,512]{1,0:T(8,128)(2,1)}, u32[]{:S(2)}) copy-start(bf16[512,512]{1,0:T(8,128)(2,1)} %rows_ref.1) | copy-start | bytes 1572868
  11.7 3.6 %copy-start.5 = (bf16[32,256]{1,0:T(8,128)(2,1)S(1)}, bf16[32,256]{1,0:T(8,128)(2,1)}, u32[]{:S(2)}) copy-start(bf16[32,256]{1,0:T(8,128)(2,1)} %param.13) | copy-start | bytes 49156
  11.7 13.3 %copy-start.4 = (bf16[32,512]{1,0:T(8,128)(2,1)S(1)}, bf16[32,512]{1,0:T(8,128)(2,1)}, u32[]{:S(2)}) copy-start(bf16[32,512]{1,0:T(8,128)(2,1)} %param.8) | copy-start | bytes 98308
  11.8 13.3 %all-to-all-start.1 = ((bf16[8,64,512]{2,1,0:T(8,128)(2,1)}), bf16[8,64,512]{2,1,0:T(8,128)(2,1)S(1)}, u32[]{:S(2)}, u32[]{:S(2)}) async-start(bf16[8,64,512]{2,1,0:T(8,128)(2,1)} %bitcast.1), calls=%async_computation.1 | async-start | bytes 1048576 | tf_op jit(solution)/shard_map/all_to_all | solution.py:20
  15.4 19.1 %copy-start = (bf16[512,1024]{1,0:T(8,128)(2,1)S(1)}, bf16[512,1024]{1,0:T(8,128)(2,1)}, u32[]{:S(2)}) copy-start(bf16[512,1024]{1,0:T(8,128)(2,1)} %w_up_ref.1) | copy-start | bytes 3145732
  15.4 4.3 %collective-permute-start = (bf16[32,256]{1,0:T(8,128)(2,1)S(1)}, bf16[32,256]{1,0:T(8,128)(2,1)S(1)}, u32[]{:S(2)}, u32[]{:S(2)}) collective-permute-start(bf16[32,256]{1,0:T(8,128)(2,1)S(1)} %copy-done.5), channel_id=1, source_target_pairs={{0,1},{1,0},{2,3},{3,2},{4,5},{5,4},{6,7},{7,6},{8,9},{9,8},{10,11... | collective-permute-start | bytes 49160 | tf_op jit(solution)/shard_map/ppermute | solution.py:16
  17.1 5.5 %collective-permute-start.2 = (bf16[32,256]{1,0:T(8,128)(2,1)S(1)}, bf16[32,256]{1,0:T(8,128)(2,1)S(1)}, u32[]{:S(2)}, u32[]{:S(2)}) collective-permute-start(bf16[32,256]{1,0:T(8,128)(2,1)S(1)} %copy-done.5), channel_id=1, source_target_pairs={{0,3},{1,2},{2,1},{3,0},{4,7},{5,6},{6,5},{7,4},{8,11},{9,10},{10,... | collective-permute-start | bytes 49160 | tf_op jit(solution)/shard_map/ppermute | solution.py:16
  19.5 4.6 %collective-permute-start.1 = (bf16[32,256]{1,0:T(8,128)(2,1)S(1)}, bf16[32,256]{1,0:T(8,128)(2,1)S(1)}, u32[]{:S(2)}, u32[]{:S(2)}) collective-permute-start(bf16[32,256]{1,0:T(8,128)(2,1)S(1)} %copy-done.5), channel_id=1, source_target_pairs={{0,2},{1,3},{2,0},{3,1},{4,6},{5,7},{6,4},{7,5},{8,10},{9,11},{10,... | collective-permute-start | bytes 49160 | tf_op jit(solution)/shard_map/ppermute | solution.py:16
  25.3 8.3 %collective-permute-start.5 = (f32[32,512]{1,0:T(8,128)S(1)}, f32[32,512]{1,0:T(8,128)S(1)}, u32[]{:S(2)}, u32[]{:S(2)}) collective-permute-start(f32[32,512]{1,0:T(8,128)S(1)} %convolution_bitcast_fusion), channel_id=1, source_target_pairs={{0,3},{1,2},{2,1},{3,0},{4,7},{5,6},{6,5},{7,4},{8,11},{9,10},{10,... | collective-permute-start | bytes 196616 | tf_op jit(solution)/shard_map/ppermute | solution.py:16
  28.9 5.2 %collective-permute-start.4 = (f32[32,512]{1,0:T(8,128)S(1)}, f32[32,512]{1,0:T(8,128)S(1)}, u32[]{:S(2)}, u32[]{:S(2)}) collective-permute-start(f32[32,512]{1,0:T(8,128)S(1)} %convolution_bitcast_fusion), channel_id=1, source_target_pairs={{0,2},{1,3},{2,0},{3,1},{4,6},{5,7},{6,4},{7,5},{8,10},{9,11},{10,... | collective-permute-start | bytes 196616 | tf_op jit(solution)/shard_map/ppermute | solution.py:16
  28.9 5.2 %collective-permute-start.3 = (f32[32,512]{1,0:T(8,128)S(1)}, f32[32,512]{1,0:T(8,128)S(1)}, u32[]{:S(2)}, u32[]{:S(2)}) collective-permute-start(f32[32,512]{1,0:T(8,128)S(1)} %convolution_bitcast_fusion), channel_id=1, source_target_pairs={{0,1},{1,0},{2,3},{3,2},{4,5},{5,4},{6,7},{7,6},{8,9},{9,8},{10,11... | collective-permute-start | bytes 196616 | tf_op jit(solution)/shard_map/ppermute | solution.py:16
  29.7 3.9 %collective-permute-start.6 = (bf16[32,512]{1,0:T(8,128)(2,1)S(1)}, bf16[32,512]{1,0:T(8,128)(2,1)S(1)}, u32[]{:S(2)}, u32[]{:S(2)}) collective-permute-start(bf16[32,512]{1,0:T(8,128)(2,1)S(1)} %copy-done.4), channel_id=1, source_target_pairs={{0,8},{4,12},{8,0},{12,4},{16,24},{20,28},{24,16},{28,20},{1,9},{5... | collective-permute-start | bytes 98312 | tf_op jit(solution)/shard_map/ppermute | solution.py:16
  35.0 8.4 %copy-start.3 = (f32[1024]{0:T(1024)S(1)}, f32[1024]{0:T(1024)}, u32[]{:S(2)}) copy-start(f32[1024]{0:T(1024)} %param.10) | copy-start | bytes 12292
  35.0 6.2 %collective-permute-start.9 = (bf16[32,1024]{1,0:T(8,128)(2,1)S(1)}, bf16[32,1024]{1,0:T(8,128)(2,1)S(1)}, u32[]{:S(2)}, u32[]{:S(2)}) collective-permute-start(bf16[32,1024]{1,0:T(8,128)(2,1)S(1)} %convolution_convert_fusion.refs_0_), channel_id=1, source_target_pairs={{0,3},{1,2},{2,1},{3,0},{4,7},{5,6},{6,5},{7,4},{8,11},{9,10},{10,... | collective-permute-start | bytes 196616 | tf_op jit(solution)/shard_map/ppermute | solution.py:16
  38.2 5.2 %collective-permute-start.8 = (bf16[32,1024]{1,0:T(8,128)(2,1)S(1)}, bf16[32,1024]{1,0:T(8,128)(2,1)S(1)}, u32[]{:S(2)}, u32[]{:S(2)}) collective-permute-start(bf16[32,1024]{1,0:T(8,128)(2,1)S(1)} %convolution_convert_fusion.refs_0_), channel_id=1, source_target_pairs={{0,2},{1,3},{2,0},{3,1},{4,6},{5,7},{6,4},{7,5},{8,10},{9,11},{10,... | collective-permute-start | bytes 196616 | tf_op jit(solution)/shard_map/ppermute | solution.py:16
  38.2 5.2 %collective-permute-start.7 = (bf16[32,1024]{1,0:T(8,128)(2,1)S(1)}, bf16[32,1024]{1,0:T(8,128)(2,1)S(1)}, u32[]{:S(2)}, u32[]{:S(2)}) collective-permute-start(bf16[32,1024]{1,0:T(8,128)(2,1)S(1)} %convolution_convert_fusion.refs_0_), channel_id=1, source_target_pairs={{0,1},{1,0},{2,3},{3,2},{4,5},{5,4},{6,7},{7,6},{8,9},{9,8},{10,11... | collective-permute-start | bytes 196616 | tf_op jit(solution)/shard_map/ppermute | solution.py:16
  39.5 5.4 %collective-permute-start.10 = (bf16[32,512]{1,0:T(8,128)(2,1)S(1)}, bf16[32,512]{1,0:T(8,128)(2,1)S(1)}, u32[]{:S(2)}, u32[]{:S(2)}) collective-permute-start(bf16[32,512]{1,0:T(8,128)(2,1)S(1)} %copy-done.4), channel_id=1, source_target_pairs={{0,16},{4,20},{8,24},{12,28},{16,0},{20,4},{24,8},{28,12},{1,17},{... | collective-permute-start | bytes 98312 | tf_op jit(solution)/shard_map/ppermute | solution.py:16
  44.9 13.8 %all-to-all-start.2 = ((f32[32,16,128]{2,1,0:T(8,128)}), f32[32,16,128]{2,1,0:T(8,128)S(1)}, u32[]{:S(2)}, u32[]{:S(2)}) async-start(f32[32,16,128]{2,1,0:T(8,128)} %get-tuple-element.34), calls=%async_computation.2 | async-start | bytes 524288 | tf_op jit(solution)/shard_map/all_to_all | solution.py:231
  48.4 7.9 %collective-permute-start.11 = (bf16[32,1280]{1,0:T(8,128)(2,1)S(1)}, bf16[32,1280]{1,0:T(8,128)(2,1)S(1)}, u32[]{:S(2)}, u32[]{:S(2)}) collective-permute-start(bf16[32,1280]{1,0:T(8,128)(2,1)S(1)} %pad_maximum_fusion.2), channel_id=1, source_target_pairs={{0,24},{4,28},{8,16},{12,20},{16,8},{20,12},{24,0},{28,4},{1,25},{... | collective-permute-start | bytes 245768 | tf_op jit(solution)/shard_map/ppermute | solution.py:16
  51.1 5.8 %collective-permute-start.14 = (bf16[32,768]{1,0:T(8,128)(2,1)S(1)}, bf16[32,768]{1,0:T(8,128)(2,1)S(1)}, u32[]{:S(2)}, u32[]{:S(2)}) collective-permute-start(bf16[32,768]{1,0:T(8,128)(2,1)S(1)} %get-tuple-element.41), channel_id=1, source_target_pairs={{0,16},{4,20},{8,24},{12,28},{16,0},{20,4},{24,8},{28,12},{1,17},{... | collective-permute-start | bytes 147464 | tf_op jit(solution)/shard_map/ppermute | solution.py:16
  51.7 5.3 %collective-permute-start.13 = (bf16[32,768]{1,0:T(8,128)(2,1)S(1)}, bf16[32,768]{1,0:T(8,128)(2,1)S(1)}, u32[]{:S(2)}, u32[]{:S(2)}) collective-permute-start(bf16[32,768]{1,0:T(8,128)(2,1)S(1)} %get-tuple-element.42), channel_id=1, source_target_pairs={{0,8},{4,12},{8,0},{12,4},{16,24},{20,28},{24,16},{28,20},{1,9},{5... | collective-permute-start | bytes 147464 | tf_op jit(solution)/shard_map/ppermute | solution.py:16
  57.0 1.7 %collective-permute-start.15 = (bf16[128,768]{1,0:T(8,128)(2,1)S(1)}, bf16[128,768]{1,0:T(8,128)(2,1)S(1)}, u32[]{:S(2)}, u32[]{:S(2)}) collective-permute-start(bf16[128,768]{1,0:T(8,128)(2,1)S(1)} %pad_maximum_fusion.refs_2_), channel_id=1, source_target_pairs={{0,4},{4,0},{8,12},{12,8},{16,20},{20,16},{24,28},{28,24},{1,5},{5... | collective-permute-start | bytes 589832 | tf_op jit(solution)/shard_map/ppermute | solution.py:16
  57.1 1.6 %collective-permute-start.12 = (bf16[128,512]{1,0:T(8,128)(2,1)S(1)}, bf16[128,512]{1,0:T(8,128)(2,1)S(1)}, u32[]{:S(2)}, u32[]{:S(2)}) collective-permute-start(bf16[128,512]{1,0:T(8,128)(2,1)S(1)} %pad_maximum_fusion.1.refs_0_), channel_id=1, source_target_pairs={{0,4},{4,0},{8,12},{12,8},{16,20},{20,16},{24,28},{28,24},{1,5},{5... | collective-permute-start | bytes 393224 | tf_op jit(solution)/shard_map/ppermute | solution.py:16

commit v8 on v7

--- a/solution.py
+++ b/solution.py
@@ -78,6 +78,25 @@
                 out_ref[u : u + 1, b * lanes : (b + 1) * lanes] = counts[
                     row : row + 1, i * lanes : (i + 1) * lanes
                 ]
+
+
+def weigh(count_ref, fetched_ref, w_up_ref, *refs):
+    part_refs, (weight_ref, hidden_ref) = refs[:-2], refs[-2:]
+    scores = part_refs[0][...]
+    for part_ref in part_refs[1:]:
+        scores = scores + part_ref[...]
+    scores = scores * SCALE
+    count = count_ref[...]
+    top = jnp.max(jnp.where(count > 0, scores, -jnp.inf), axis=1, keepdims=True)
+    raised = jnp.where(count > 0, count * jnp.exp(scores - top), 0.0)
+    weight = raised / jnp.sum(raised, axis=1, keepdims=True)
+    weight_ref[...] = weight
+    pooled = jnp.dot(
+        weight.astype(jnp.bfloat16), fetched_ref[...], preferred_element_type=jnp.float32
+    ).astype(jnp.bfloat16)
+    hidden_ref[...] = jnp.dot(
+        pooled, w_up_ref[...], preferred_element_type=jnp.float32
+    ).astype(jnp.bfloat16)
 
 
 def turn(owners, upstream_ref, bias_ref, w_up_ref, fetched_ref, weight_ref, *refs):
@@ -105,7 +124,7 @@
     part = weight * (slot_slopes - jnp.sum(weight * slot_slopes, axis=1, keepdims=True)) * SCALE
     for o in range(owners):
         block = part[:, o * capacity : (o + 1) * capacity]
-        block = jnp.concatenate([block[:half], block[half:]], axis=1)
+        block = jnp.concatenate([block[:half], block[half:]], axis=1).astype(jnp.bfloat16)
         for z in range(latents):
             sending_ref[o * latents + z] = block
 
@@ -122,11 +141,11 @@
         out_ref[i, :, 2 * pair :] = grad_ref[...]
 
 
-def add_rows(latents, me_ref, wanted_ref, sent_ref, *refs):
-    target_refs, late_refs, (out_ref, left_ref, right_ref) = refs[:2], refs[2:4], refs[4:]
+def add_rows(latents, early, me_ref, wanted_ref, sent_ref, *refs):
+    target_refs, late_refs, (out_ref, left_ref, right_ref) = refs[:2], refs[2:-3], refs[-3:]
     owners, capacity = wanted_ref.shape[0], wanted_ref.shape[2]
     stored, width = out_ref.shape
-    members = late_refs[0].shape[0] // (owners // 2)
+    members = late_refs[0].shape[0]
     pair = 2 * capacity
     depth = 4 * members
     places = lax.broadcasted_iota(jnp.int32, (stored, capacity), 0)
@@ -138,20 +157,22 @@
         return jnp.where(first, x[:, :capacity], x[:, capacity:]).astype(jnp.bfloat16)
 
     for k in range(owners):
-        d = me ^ k
-        block = sent_ref[pl.ds(d * latents, latents)]
+        d, i, side = me ^ k, k // 2, k % 2
+        block = sent_ref[pl.ds(d * latents, latents)].astype(jnp.float32)
         slope = block[0]
         for z in range(1, latents):
             slope = slope + block[z]
         slope = jnp.concatenate([slope[:, :capacity], slope[:, capacity:]], axis=0)
         slope_high = slope.astype(jnp.bfloat16)
         slope_low = (slope - slope_high.astype(jnp.float32)).astype(jnp.bfloat16)
-        piece = slice((k // 2) * members, (k // 2 + 1) * members)
-        targets = target_refs[k % 2][piece, :]
-        side = late_refs[k % 2][piece, :]
-        grads = side[:, 2 * pair :]
-        weight_high = of_me(side[:, :pair])
-        weight_low = of_me(side[:, pair : 2 * pair])
+        late_ref = late_refs[side * (owners // 2) + i]
+        grads = late_ref[:, 2 * pair : 2 * pair + width]
+        if i < early:
+            targets = target_refs[side][i * members : (i + 1) * members, :]
+        else:
+            targets = late_refs[side * (owners // 2) + (i ^ 1)][:, 2 * pair + width :]
+        weight_high = of_me(late_ref[:, :pair])
+        weight_low = of_me(late_ref[:, pair : 2 * pair])
         chosen = (wanted_ref[d] == places).astype(jnp.bfloat16)
         spread = lax.dot_general(
             chosen,
@@ -205,13 +226,12 @@
     parts = [slot_scores] + [swap(slot_scores, "latent", k) for k in range(1, latents)]
     near_targets = [swap(late_targets, "batch", k) for k in range(2, owners, 2)[:1]]
     parts, near_targets = lax.optimization_barrier((parts, near_targets))
-    scores = sum(parts[1:], parts[0]) * SCALE
-    top = jnp.max(jnp.where(count > 0, scores, -jnp.inf), axis=1, keepdims=True)
-    raised = jnp.where(count > 0, count * jnp.exp(scores - top), 0.0)
-    weight = raised / jnp.sum(raised, axis=1, keepdims=True)
-
-    pooled = jnp.dot(weight.astype(bf16), fetched, preferred_element_type=jnp.float32).astype(bf16)
-    partial_hidden = jnp.dot(pooled, w_up, preferred_element_type=jnp.float32).astype(bf16)
+    weight, partial_hidden = call(
+        weigh,
+        (shape((members, slot_count), jnp.float32), shape((members, bias.shape[0]), bf16)),
+        (count, fetched, w_up, *parts),
+        [vmem] * (3 + latents),
+    )
     partial_hidden, late_targets = lax.optimization_barrier((partial_hidden, targets))
     parts = [partial_hidden] + [swap(partial_hidden, "latent", k) for k in range(1, latents)]
     far_targets = [swap(late_targets, "batch", k) for k in range(2, owners, 2)[1:2]]
@@ -220,7 +240,7 @@
         (
             shape(partial_hidden.shape, bf16),
             shape((members, row_width), bf16),
-            shape((owners * latents, half, 2 * capacity), jnp.float32),
+            shape((owners * latents, half, 2 * capacity), bf16),
         ),
         (upstream_full, bias.reshape(1, -1), w_up, fetched, weight, *parts),
         [vmem] * (5 + latents),
@@ -235,22 +255,23 @@
         (me, weight, pooled_grad),
         [smem, vmem, vmem],
     )
-    even_late = [late[0]] + [swap(late[k // 2], "batch", k) for k in range(2, owners, 2)[:2]]
     even_targets = [targets] + near_targets + far_targets
-    for k in range(2, owners, 2)[2:]:
-        both = swap(jnp.concatenate([late[k // 2], targets], axis=1), "batch", k)
-        even_late.append(both[:, : late.shape[2]])
-        even_targets.append(both[:, late.shape[2] :])
-    even_late = jnp.concatenate(even_late, axis=0)
-    odd_late = swap(even_late, "batch", 1)
+    early = len(even_targets)
+    even_late = [late[0]]
+    for k in range(2, owners, 2):
+        message = late[k // 2]
+        if (k ^ 2) // 2 >= early:
+            message = jnp.concatenate([message, near_targets[0]], axis=1)
+        even_late.append(swap(message, "batch", k))
+    odd_late = [swap(x, "batch", 1) for x in even_late]
     even_targets = jnp.concatenate(even_targets, axis=0)
     odd_targets = swap(even_targets, "batch", 1)
     depth = owners * 4 * members
     row_grad = call(
-        functools.partial(add_rows, latents),
+        functools.partial(add_rows, latents, early),
         shape((stored, row_width), jnp.float32),
-        (me, wanted, sent, even_targets, odd_targets, even_late, odd_late),
-        [smem] + [vmem] * 6,
+        (me, wanted, sent, even_targets, odd_targets, *even_late, *odd_late),
+        [smem] + [vmem] * (4 + owners),
         [pltpu.VMEM((stored, depth), bf16), pltpu.VMEM((depth, row_width), bf16)],
     )
     return (output, row_grad)

time: 61.2 us -> 59.8 us (0.977)
  waiting for transfers between devices: 18.8 us -> 16.6 us
  starting transfers between devices: 31.3 us -> 32.5 us
    ppermute x16 -> x19, waiting for transfers between devices: 16.5 us -> 14.3 us  [swap(): return lax.ppermute(x, axis, [(i, i ^ k) for i in range(n)])]
    ppermute x16 -> x19, starting transfers between devices: 19 us -> 20.2 us  [swap(): return lax.ppermute(x, axis, [(i, i ^ k) for i in range(n)])]
    pallas_call x6 -> x7, Pallas kernels: 6.16 us -> 6.72 us  [call(): pl.pallas_call(kernel, out_shape=shapes, in_specs=specs, out_specs=jax.tr...]
    unnamed x12 -> x14, local copies, waits for them, and re-layouts: 1.91 us -> 1.91 us
  transfers between devices with their start and end apart: 19 -> 22, of which waited for: 11 -> 12; matrix products, arithmetic and copies ran while one was open for 1% -> 1% of each run, Pallas kernels for 5% -> 5%
where the time goes in v8:
time: 59.8 us; the launch traced here: 59.4 us
  starting transfers between devices  32.5 us (54%)
  waiting for transfers between devices  16.6 us (28%)
  Pallas kernels  6.72 us (11%)
  local copies, waits for them, and re-layouts  2.56 us (4%)
  between operations  0.75 us (1%)
    ppermute x19, starting transfers between devices, swap(): return lax.ppermute(x, axis, [(i, i ^ k) for i in range(n)])  20.2 us
    ppermute x19, waiting for transfers between devices, swap(): return lax.ppermute(x, axis, [(i, i ^ k) for i in range(n)])  14.3 us
    all_to_all x2, starting transfers between devices, exchange(): return lax.all_to_all(x, 'batch', split_axis=0, concat_axis=0, tiled=True)  8.81 us
    pallas_call x7, Pallas kernels, call(): pl.pallas_call(kernel, out_shape=shapes, in_specs=specs, out_specs=jax.tr...  6.72 us
    all_to_all x1, starting transfers between devices, on_device(): lax.all_to_all(sending, ('batch', 'latent'), split_axis=0, concat_axis=0,...  3.5 us
    all_to_all x2, waiting for transfers between devices, exchange(): return lax.all_to_all(x, 'batch', split_axis=0, concat_axis=0, tiled=True)  2.28 us
    unnamed x14, local copies, waits for them, and re-layouts  1.91 us
  transfers between devices with their start and end apart: 22, of which 12 were waited for; matrix products, arithmetic and copies ran while one was open for 1% of the time, Pallas kernels for 5%

profile of v8, /device:TPU:0, one launch (start us, length us, event | category | flops | bytes accessed | tf_op | source)
XLA Modules:
  0.0 59.4 jit_solution(12215700790139179127)
XLA Ops:
  0.6 5.2 %all-to-all-start = ((s32[8,1,64]{2,1,0:T(1,128)}), s32[8,1,64]{2,1,0:T(1,128)S(1)}, u32[]{:S(2)}, u32[]{:S(2)}) async-start(s32[8,1,64]{2,1,0:T(1,128)} %bitcast.37), calls=%async_computation | async-start | bytes 8192 | tf_op jit(solution)/shard_map/all_to_all | solution.py:20
  5.8 0.8 %copy-done.2 = s32[32,512]{1,0:T(8,128)S(1)} copy-done((s32[32,512]{1,0:T(8,128)S(1)}, s32[32,512]{1,0:T(8,128)}, u32[]{:S(2)}) %copy-start.2) | copy-done | bytes 65560
  6.7 1.2 %count_slots.1.count_ref = f32[32,512]{1,0:T(8,128)S(1)} custom-call(s32[32,512]{1,0:T(8,128)S(1)} %copy-done.2), custom_call_target="tpu_custom_call" | custom-call | tf_op jit(solution)/shard_map/count_slots/pallas_call | solution.py:24
  7.9 1.1 %copy-done.1 = bf16[512,512]{1,0:T(8,128)(2,1)S(1)} copy-done((bf16[512,512]{1,0:T(8,128)(2,1)S(1)}, bf16[512,512]{1,0:T(8,128)(2,1)}, u32[]{:S(2)}) %copy-start.1) | copy-done | bytes 524312
  8.9 1.5 %all-to-all-done.wanted_ref = s32[8,1,64]{2,1,0:T(1,128)S(1)} async-done(((s32[8,1,64]{2,1,0:T(1,128)}), s32[8,1,64]{2,1,0:T(1,128)S(1)}, u32[]{:S(2)}, u32[]{:S(2)}) %all-to-all-start) | async-done | bytes 2080 | tf_op jit(solution)/shard_map/all_to_all | solution.py:20
  10.4 1.3 %pick_rows.1 = bf16[512,512]{1,0:T(8,128)(2,1)} custom-call(s32[8,1,64]{2,1,0:T(1,128)S(1)} %all-to-all-done.wanted_ref, bf16[512,512]{1,0:T(8,128)(2,1)S(1)} %hold_rows.1.rows_ref), custom_call_target="tpu_custom_call" | custom-call | tf_op jit(solution)/shard_map/pick_rows/pallas_call | solution.py:24
  11.8 3.6 %all-to-all-start.1 = ((bf16[8,64,512]{2,1,0:T(8,128)(2,1)}), bf16[8,64,512]{2,1,0:T(8,128)(2,1)S(1)}, u32[]{:S(2)}, u32[]{:S(2)}) async-start(bf16[8,64,512]{2,1,0:T(8,128)(2,1)} %bitcast.1), calls=%async_computation.1 | async-start | bytes 1048576 | tf_op jit(solution)/shard_map/all_to_all | solution.py:20
  15.4 1.6 %collective-permute-start = (bf16[32,256]{1,0:T(8,128)(2,1)S(1)}, bf16[32,256]{1,0:T(8,128)(2,1)S(1)}, u32[]{:S(2)}, u32[]{:S(2)}) collective-permute-start(bf16[32,256]{1,0:T(8,128)(2,1)S(1)} %copy-done.5), channel_id=1, source_target_pairs={{0,1},{1,0},{2,3},{3,2},{4,5},{5,4},{6,7},{7,6},{8,9},{9,8},{10,11... | collective-permute-start | bytes 49160 | tf_op jit(solution)/shard_map/ppermute | solution.py:16
  17.0 2.5 %collective-permute-start.2 = (bf16[32,256]{1,0:T(8,128)(2,1)S(1)}, bf16[32,256]{1,0:T(8,128)(2,1)S(1)}, u32[]{:S(2)}, u32[]{:S(2)}) collective-permute-start(bf16[32,256]{1,0:T(8,128)(2,1)S(1)} %copy-done.5), channel_id=1, source_target_pairs={{0,3},{1,2},{2,1},{3,0},{4,7},{5,6},{6,5},{7,4},{8,11},{9,10},{10,... | collective-permute-start | bytes 49160 | tf_op jit(solution)/shard_map/ppermute | solution.py:16
  19.5 0.1 collective-permute-start.1
  19.6 0.0 collective-permute-done
  19.6 2.9 %collective-permute-done.2 = bf16[32,256]{1,0:T(8,128)(2,1)S(1)} collective-permute-done((bf16[32,256]{1,0:T(8,128)(2,1)S(1)}, bf16[32,256]{1,0:T(8,128)(2,1)S(1)}, u32[]{:S(2)}, u32[]{:S(2)}) %collective-permute-start.2) | collective-permute-done | bytes 16416 | tf_op jit(solution)/shard_map/ppermute | solution.py:16
  22.6 1.6 %collective-permute-done.1 = bf16[32,256]{1,0:T(8,128)(2,1)S(1)} collective-permute-done((bf16[32,256]{1,0:T(8,128)(2,1)S(1)}, bf16[32,256]{1,0:T(8,128)(2,1)S(1)}, u32[]{:S(2)}, u32[]{:S(2)}) %collective-permute-start.1) | collective-permute-done | bytes 16416 | tf_op jit(solution)/shard_map/ppermute | solution.py:16
  24.2 0.0 copy-start.4
  24.2 0.8 %all-to-all-done.1 = bf16[8,64,512]{2,1,0:T(8,128)(2,1)S(1)} async-done(((bf16[8,64,512]{2,1,0:T(8,128)(2,1)}), bf16[8,64,512]{2,1,0:T(8,128)(2,1)S(1)}, u32[]{:S(2)}, u32[]{:S(2)}) %all-to-all-start.1) | async-done | bytes 524320 | tf_op jit(solution)/shard_map/all_to_all | solution.py:20
  25.1 0.2 convolution_bitcast_fusion.refs_0_
  25.3 3.6 %collective-permute-start.5 = (f32[32,512]{1,0:T(8,128)S(1)}, f32[32,512]{1,0:T(8,128)S(1)}, u32[]{:S(2)}, u32[]{:S(2)}) collective-permute-start(f32[32,512]{1,0:T(8,128)S(1)} %convolution_bitcast_fusion.refs_0_), channel_id=1, source_target_pairs={{0,3},{1,2},{2,1},{3,0},{4,7},{5,6},{6,5},{7,4},{8,11},{9,10},{10,... | collective-permute-start | bytes 196616 | tf_op jit(solution)/shard_map/ppermute | solution.py:16
  28.9 0.0 collective-permute-start.4
  28.9 0.8 %collective-permute-start.3 = (f32[32,512]{1,0:T(8,128)S(1)}, f32[32,512]{1,0:T(8,128)S(1)}, u32[]{:S(2)}, u32[]{:S(2)}) collective-permute-start(f32[32,512]{1,0:T(8,128)S(1)} %convolution_bitcast_fusion.refs_0_), channel_id=1, source_target_pairs={{0,1},{1,0},{2,3},{3,2},{4,5},{5,4},{6,7},{7,6},{8,9},{9,8},{10,11... | collective-permute-start | bytes 196616 | tf_op jit(solution)/shard_map/ppermute | solution.py:16
  29.7 1.8 %collective-permute-start.6 = (bf16[32,512]{1,0:T(8,128)(2,1)S(1)}, bf16[32,512]{1,0:T(8,128)(2,1)S(1)}, u32[]{:S(2)}, u32[]{:S(2)}) collective-permute-start(bf16[32,512]{1,0:T(8,128)(2,1)S(1)} %copy-done.4), channel_id=1, source_target_pairs={{0,8},{4,12},{8,0},{12,4},{16,24},{20,28},{24,16},{28,20},{1,9},{5... | collective-permute-start | bytes 98312 | tf_op jit(solution)/shard_map/ppermute | solution.py:16
  31.5 2.2 %collective-permute-done.6 = bf16[32,512]{1,0:T(8,128)(2,1)S(1)} collective-permute-done((bf16[32,512]{1,0:T(8,128)(2,1)S(1)}, bf16[32,512]{1,0:T(8,128)(2,1)S(1)}, u32[]{:S(2)}, u32[]{:S(2)}) %collective-permute-start.6) | collective-permute-done | bytes 32800 | tf_op jit(solution)/shard_map/ppermute | solution.py:16
  33.6 0.5 collective-permute-done.4.refs_2_
  34.1 0.0 collective-permute-done.3.refs_1_
  34.1 0.6 %weigh.1 = (f32[32,512]{1,0:T(8,128)S(1)}, bf16[32,1024]{1,0:T(8,128)(2,1)S(1)}) custom-call(f32[32,512]{1,0:T(8,128)S(1)} %count_slots.1.count_ref, bf16[512,512]{1,0:T(8,128)(2,1)S(1)} %bitcast.30, bf16[512,1024]{1,0:T(8,128)(2,1)S(1)} %copy-done, f32[32,512]{1,0:T(8,128)S(1)} %convolution_bitcast_fusion.refs_0_, ...), custom_call_target="tpu_custom_call" | custom-call | tf_op jit(solution)/shard_map/weigh/pallas_call | solution.py:24
  34.7 3.2 %collective-permute-start.9 = (bf16[32,1024]{1,0:T(8,128)(2,1)S(1)}, bf16[32,1024]{1,0:T(8,128)(2,1)S(1)}, u32[]{:S(2)}, u32[]{:S(2)}) collective-permute-start(bf16[32,1024]{1,0:T(8,128)(2,1)S(1)} %get-tuple-element.34.refs_0_), channel_id=1, source_target_pairs={{0,3},{1,2},{2,1},{3,0},{4,7},{5,6},{6,5},{7,4},{8,11},{9,10},{10,... | collective-permute-start | bytes 196616 | tf_op jit(solution)/shard_map/ppermute | solution.py:16
  37.9 0.0 collective-permute-start.8
  37.9 1.2 %collective-permute-start.7 = (bf16[32,1024]{1,0:T(8,128)(2,1)S(1)}, bf16[32,1024]{1,0:T(8,128)(2,1)S(1)}, u32[]{:S(2)}, u32[]{:S(2)}) collective-permute-start(bf16[32,1024]{1,0:T(8,128)(2,1)S(1)} %get-tuple-element.34.refs_0_), channel_id=1, source_target_pairs={{0,1},{1,0},{2,3},{3,2},{4,5},{5,4},{6,7},{7,6},{8,9},{9,8},{10,11... | collective-permute-start | bytes 196616 | tf_op jit(solution)/shard_map/ppermute | solution.py:16
  39.1 1.3 %collective-permute-start.10 = (bf16[32,512]{1,0:T(8,128)(2,1)S(1)}, bf16[32,512]{1,0:T(8,128)(2,1)S(1)}, u32[]{:S(2)}, u32[]{:S(2)}) collective-permute-start(bf16[32,512]{1,0:T(8,128)(2,1)S(1)} %copy-done.4), channel_id=1, source_target_pairs={{0,16},{4,20},{8,24},{12,28},{16,0},{20,4},{24,8},{28,12},{1,17},{... | collective-permute-start | bytes 98312 | tf_op jit(solution)/shard_map/ppermute | solution.py:16
  40.5 0.4 collective-permute-done.9.refs_3_
  40.9 2.2 %collective-permute-done.8.refs_2_ = bf16[32,1024]{1,0:T(8,128)(2,1)S(1)} collective-permute-done((bf16[32,1024]{1,0:T(8,128)(2,1)S(1)}, bf16[32,1024]{1,0:T(8,128)(2,1)S(1)}, u32[]{:S(2)}, u32[]{:S(2)}) %collective-permute-start.8) | collective-permute-done | bytes 65568 | tf_op jit(solution)/shard_map/ppermute | solution.py:16
  43.1 1.4 %turn.1 = (bf16[32,1024]{1,0:T(8,128)(2,1)S(1)}, bf16[32,512]{1,0:T(8,128)(2,1)S(1)}, bf16[32,16,128]{2,1,0:T(8,128)(2,1)}) custom-call(bf16[32,1024]{1,0:T(8,128)(2,1)S(1)} %pad_maximum_fusion.2.upstream_ref, f32[1,1024]{1,0:T(1,128)S(1)} %bitcast.32, bf16[512,1024]{1,0:T(8,128)(2,1)S(1)} %copy-done, bf16[512,512]{1,0:T(8,128)(2,1)S(1)} %bitcast.31, ...), custom_call_target="tpu_custom_call" | custom-call | tf_op jit(solution)/shard_map/turn/pallas_call | solution.py:24
  44.5 3.5 %all-to-all-start.2 = ((bf16[32,16,128]{2,1,0:T(8,128)(2,1)}), bf16[32,16,128]{2,1,0:T(8,128)(2,1)S(1)}, u32[]{:S(2)}, u32[]{:S(2)}) async-start(bf16[32,16,128]{2,1,0:T(8,128)(2,1)} %get-tuple-element.38), calls=%async_computation.2 | async-start | bytes 262144 | tf_op jit(solution)/shard_map/all_to_all | solution.py:251
  48.1 2.7 %collective-permute-start.14 = (bf16[32,768]{1,0:T(8,128)(2,1)S(1)}, bf16[32,768]{1,0:T(8,128)(2,1)S(1)}, u32[]{:S(2)}, u32[]{:S(2)}) collective-permute-start(bf16[32,768]{1,0:T(8,128)(2,1)S(1)} %get-tuple-element.42), channel_id=1, source_target_pairs={{0,24},{4,28},{8,16},{12,20},{16,8},{20,12},{24,0},{28,4},{1,25},{... | collective-permute-start | bytes 147464 | tf_op jit(solution)/shard_map/ppermute | solution.py:16
  50.8 0.6 collective-permute-start.12
  51.4 0.3 collective-permute-start.13
  51.6 0.5 collective-permute-start.15
  52.1 1.7 %collective-permute-done.14.refs_5_ = bf16[32,768]{1,0:T(8,128)(2,1)S(1)} collective-permute-done((bf16[32,768]{1,0:T(8,128)(2,1)S(1)}, bf16[32,768]{1,0:T(8,128)(2,1)S(1)}, u32[]{:S(2)}, u32[]{:S(2)}) %collective-permute-start.14) | collective-permute-done | bytes 49184 | tf_op jit(solution)/shard_map/ppermute | solution.py:16
  53.8 1.2 %collective-permute-done.12.refs_3_ = bf16[32,768]{1,0:T(8,128)(2,1)S(1)} collective-permute-done((bf16[32,768]{1,0:T(8,128)(2,1)S(1)}, bf16[32,768]{1,0:T(8,128)(2,1)S(1)}, u32[]{:S(2)}, u32[]{:S(2)}) %collective-permute-start.12) | collective-permute-done | bytes 49184 | tf_op jit(solution)/shard_map/ppermute | solution.py:16
  55.0 0.0 collective-permute-start.16
  55.0 1.0 %collective-permute-done.13.refs_4_ = bf16[32,1280]{1,0:T(8,128)(2,1)S(1)} collective-permute-done((bf16[32,1280]{1,0:T(8,128)(2,1)S(1)}, bf16[32,1280]{1,0:T(8,128)(2,1)S(1)}, u32[]{:S(2)}, u32[]{:S(2)}) %collective-permute-start.13) | collective-permute-done | bytes 81952 | tf_op jit(solution)/shard_map/ppermute | solution.py:16
  56.1 0.0 collective-permute-start.17
  56.1 0.6 %constant_dynamic-slice_fusion = bf16[32,256]{1,0:T(8,128)(2,1)} fusion(bf16[32,1024]{1,0:T(8,128)(2,1)S(1)} %get-tuple-element.35, s32[]{:T(128)S(6)} %select_n.20), kind=kLoop, calls=%fused_computation.15 | loop fusion | bytes 32772 | tf_op jit(solution)/shard_map/dynamic_slice | solution.py:248
  56.7 0.0 collective-permute-done.15.refs_6_
  56.7 0.0 collective-permute-done.11.refs_1_
  56.7 0.0 collective-permute-done.18.refs_9_
  56.7 0.6 %collective-permute-done.17.refs_8_ = bf16[32,1280]{1,0:T(8,128)(2,1)S(1)} collective-permute-done((bf16[32,1280]{1,0:T(8,128)(2,1)S(1)}, bf16[32,1280]{1,0:T(8,128)(2,1)S(1)}, u32[]{:S(2)}, u32[]{:S(2)}) %collective-permute-start.17) | collective-permute-done | bytes 81952 | tf_op jit(solution)/shard_map/ppermute | solution.py:16
  57.3 0.0 all-to-all-done.2.sent_ref
  57.3 2.1 %add_rows.1 = f32[512,512]{1,0:T(8,128)} custom-call(s32[1]{0:T(128)} %bitcast.13.me_ref, s32[8,1,64]{2,1,0:T(1,128)S(1)} %all-to-all-done.wanted_ref, bf16[32,16,128]{2,1,0:T(8,128)(2,1)S(1)} %all-to-all-done.2.sent_ref, bf16[96,512]{1,0:T(8,128)(2,1)S(1)} %constant_dynamic-update-slice_fusion.refs_0_, bf16[96,512]{1,0:T(8,128)(2,1)S(1)} %collective-permute-done.11.refs_1_, ...), custom_call_target="tpu_custom_call" | custom-call | tf_op jit(solution)/shard_map/add_rows/pallas_call | solution.py:24
  (25 shorter events, 0.2 us)
Async XLA Ops:
  0.6 9.8 %all-to-all-start = ((s32[8,1,64]{2,1,0:T(1,128)}), s32[8,1,64]{2,1,0:T(1,128)S(1)}, u32[]{:S(2)}, u32[]{:S(2)}) async-start(s32[8,1,64]{2,1,0:T(1,128)} %bitcast.37), calls=%async_computation | async-start | bytes 8192 | tf_op jit(solution)/shard_map/all_to_all | solution.py:20
  5.8 0.8 %copy-start.2 = (s32[32,512]{1,0:T(8,128)S(1)}, s32[32,512]{1,0:T(8,128)}, u32[]{:S(2)}) copy-start(s32[32,512]{1,0:T(8,128)} %history_ref.1) | copy-start | bytes 196612
  7.9 1.1 %copy-start.1 = (bf16[512,512]{1,0:T(8,128)(2,1)S(1)}, bf16[512,512]{1,0:T(8,128)(2,1)}, u32[]{:S(2)}) copy-start(bf16[512,512]{1,0:T(8,128)(2,1)} %rows_ref.1) | copy-start | bytes 1572868
  10.4 5.0 %copy-start.5 = (bf16[32,256]{1,0:T(8,128)(2,1)S(1)}, bf16[32,256]{1,0:T(8,128)(2,1)}, u32[]{:S(2)}) copy-start(bf16[32,256]{1,0:T(8,128)(2,1)} %param.13) | copy-start | bytes 49156
  11.7 22.4 %copy-start = (bf16[512,1024]{1,0:T(8,128)(2,1)S(1)}, bf16[512,1024]{1,0:T(8,128)(2,1)}, u32[]{:S(2)}) copy-start(bf16[512,1024]{1,0:T(8,128)(2,1)} %w_up_ref.3) | copy-start | bytes 3145732
  11.8 13.3 %all-to-all-start.1 = ((bf16[8,64,512]{2,1,0:T(8,128)(2,1)}), bf16[8,64,512]{2,1,0:T(8,128)(2,1)S(1)}, u32[]{:S(2)}, u32[]{:S(2)}) async-start(bf16[8,64,512]{2,1,0:T(8,128)(2,1)} %bitcast.1), calls=%async_computation.1 | async-start | bytes 1048576 | tf_op jit(solution)/shard_map/all_to_all | solution.py:20
  15.4 4.2 %collective-permute-start = (bf16[32,256]{1,0:T(8,128)(2,1)S(1)}, bf16[32,256]{1,0:T(8,128)(2,1)S(1)}, u32[]{:S(2)}, u32[]{:S(2)}) collective-permute-start(bf16[32,256]{1,0:T(8,128)(2,1)S(1)} %copy-done.5), channel_id=1, source_target_pairs={{0,1},{1,0},{2,3},{3,2},{4,5},{5,4},{6,7},{7,6},{8,9},{9,8},{10,11... | collective-permute-start | bytes 49160 | tf_op jit(solution)/shard_map/ppermute | solution.py:16
  17.0 5.5 %collective-permute-start.2 = (bf16[32,256]{1,0:T(8,128)(2,1)S(1)}, bf16[32,256]{1,0:T(8,128)(2,1)S(1)}, u32[]{:S(2)}, u32[]{:S(2)}) collective-permute-start(bf16[32,256]{1,0:T(8,128)(2,1)S(1)} %copy-done.5), channel_id=1, source_target_pairs={{0,3},{1,2},{2,1},{3,0},{4,7},{5,6},{6,5},{7,4},{8,11},{9,10},{10,... | collective-permute-start | bytes 49160 | tf_op jit(solution)/shard_map/ppermute | solution.py:16
  19.5 4.6 %collective-permute-start.1 = (bf16[32,256]{1,0:T(8,128)(2,1)S(1)}, bf16[32,256]{1,0:T(8,128)(2,1)S(1)}, u32[]{:S(2)}, u32[]{:S(2)}) collective-permute-start(bf16[32,256]{1,0:T(8,128)(2,1)S(1)} %copy-done.5), channel_id=1, source_target_pairs={{0,2},{1,3},{2,0},{3,1},{4,6},{5,7},{6,4},{7,5},{8,10},{9,11},{10,... | collective-permute-start | bytes 49160 | tf_op jit(solution)/shard_map/ppermute | solution.py:16
  24.2 0.9 %copy-start.4 = (bf16[32,512]{1,0:T(8,128)(2,1)S(1)}, bf16[32,512]{1,0:T(8,128)(2,1)}, u32[]{:S(2)}) copy-start(bf16[32,512]{1,0:T(8,128)(2,1)} %param.8) | copy-start | bytes 98308
  25.3 8.3 %collective-permute-start.5 = (f32[32,512]{1,0:T(8,128)S(1)}, f32[32,512]{1,0:T(8,128)S(1)}, u32[]{:S(2)}, u32[]{:S(2)}) collective-permute-start(f32[32,512]{1,0:T(8,128)S(1)} %convolution_bitcast_fusion.refs_0_), channel_id=1, source_target_pairs={{0,3},{1,2},{2,1},{3,0},{4,7},{5,6},{6,5},{7,4},{8,11},{9,10},{10,... | collective-permute-start | bytes 196616 | tf_op jit(solution)/shard_map/ppermute | solution.py:16
  28.9 5.2 %collective-permute-start.4 = (f32[32,512]{1,0:T(8,128)S(1)}, f32[32,512]{1,0:T(8,128)S(1)}, u32[]{:S(2)}, u32[]{:S(2)}) collective-permute-start(f32[32,512]{1,0:T(8,128)S(1)} %convolution_bitcast_fusion.refs_0_), channel_id=1, source_target_pairs={{0,2},{1,3},{2,0},{3,1},{4,6},{5,7},{6,4},{7,5},{8,10},{9,11},{10,... | collective-permute-start | bytes 196616 | tf_op jit(solution)/shard_map/ppermute | solution.py:16
  28.9 5.2 %collective-permute-start.3 = (f32[32,512]{1,0:T(8,128)S(1)}, f32[32,512]{1,0:T(8,128)S(1)}, u32[]{:S(2)}, u32[]{:S(2)}) collective-permute-start(f32[32,512]{1,0:T(8,128)S(1)} %convolution_bitcast_fusion.refs_0_), channel_id=1, source_target_pairs={{0,1},{1,0},{2,3},{3,2},{4,5},{5,4},{6,7},{7,6},{8,9},{9,8},{10,11... | collective-permute-start | bytes 196616 | tf_op jit(solution)/shard_map/ppermute | solution.py:16
  29.7 3.9 %collective-permute-start.6 = (bf16[32,512]{1,0:T(8,128)(2,1)S(1)}, bf16[32,512]{1,0:T(8,128)(2,1)S(1)}, u32[]{:S(2)}, u32[]{:S(2)}) collective-permute-start(bf16[32,512]{1,0:T(8,128)(2,1)S(1)} %copy-done.4), channel_id=1, source_target_pairs={{0,8},{4,12},{8,0},{12,4},{16,24},{20,28},{24,16},{28,20},{1,9},{5... | collective-permute-start | bytes 98312 | tf_op jit(solution)/shard_map/ppermute | solution.py:16
  34.7 6.2 %collective-permute-start.9 = (bf16[32,1024]{1,0:T(8,128)(2,1)S(1)}, bf16[32,1024]{1,0:T(8,128)(2,1)S(1)}, u32[]{:S(2)}, u32[]{:S(2)}) collective-permute-start(bf16[32,1024]{1,0:T(8,128)(2,1)S(1)} %get-tuple-element.34.refs_0_), channel_id=1, source_target_pairs={{0,3},{1,2},{2,1},{3,0},{4,7},{5,6},{6,5},{7,4},{8,11},{9,10},{10,... | collective-permute-start | bytes 196616 | tf_op jit(solution)/shard_map/ppermute | solution.py:16
  37.9 5.2 %collective-permute-start.8 = (bf16[32,1024]{1,0:T(8,128)(2,1)S(1)}, bf16[32,1024]{1,0:T(8,128)(2,1)S(1)}, u32[]{:S(2)}, u32[]{:S(2)}) collective-permute-start(bf16[32,1024]{1,0:T(8,128)(2,1)S(1)} %get-tuple-element.34.refs_0_), channel_id=1, source_target_pairs={{0,2},{1,3},{2,0},{3,1},{4,6},{5,7},{6,4},{7,5},{8,10},{9,11},{10,... | collective-permute-start | bytes 196616 | tf_op jit(solution)/shard_map/ppermute | solution.py:16
  37.9 5.2 %collective-permute-start.7 = (bf16[32,1024]{1,0:T(8,128)(2,1)S(1)}, bf16[32,1024]{1,0:T(8,128)(2,1)S(1)}, u32[]{:S(2)}, u32[]{:S(2)}) collective-permute-start(bf16[32,1024]{1,0:T(8,128)(2,1)S(1)} %get-tuple-element.34.refs_0_), channel_id=1, source_target_pairs={{0,1},{1,0},{2,3},{3,2},{4,5},{5,4},{6,7},{7,6},{8,9},{9,8},{10,11... | collective-permute-start | bytes 196616 | tf_op jit(solution)/shard_map/ppermute | solution.py:16
  39.1 5.4 %collective-permute-start.10 = (bf16[32,512]{1,0:T(8,128)(2,1)S(1)}, bf16[32,512]{1,0:T(8,128)(2,1)S(1)}, u32[]{:S(2)}, u32[]{:S(2)}) collective-permute-start(bf16[32,512]{1,0:T(8,128)(2,1)S(1)} %copy-done.4), channel_id=1, source_target_pairs={{0,16},{4,20},{8,24},{12,28},{16,0},{20,4},{24,8},{28,12},{1,17},{... | collective-permute-start | bytes 98312 | tf_op jit(solution)/shard_map/ppermute | solution.py:16
  40.4 2.6 %copy-start.3 = (f32[1024]{0:T(1024)S(1)}, f32[1024]{0:T(1024)}, u32[]{:S(2)}) copy-start(f32[1024]{0:T(1024)} %param.10) | copy-start | bytes 12292
  44.5 12.8 %all-to-all-start.2 = ((bf16[32,16,128]{2,1,0:T(8,128)(2,1)}), bf16[32,16,128]{2,1,0:T(8,128)(2,1)S(1)}, u32[]{:S(2)}, u32[]{:S(2)}) async-start(bf16[32,16,128]{2,1,0:T(8,128)(2,1)} %get-tuple-element.38), calls=%async_computation.2 | async-start | bytes 262144 | tf_op jit(solution)/shard_map/all_to_all | solution.py:251
  48.1 5.7 %collective-permute-start.14 = (bf16[32,768]{1,0:T(8,128)(2,1)S(1)}, bf16[32,768]{1,0:T(8,128)(2,1)S(1)}, u32[]{:S(2)}, u32[]{:S(2)}) collective-permute-start(bf16[32,768]{1,0:T(8,128)(2,1)S(1)} %get-tuple-element.42), channel_id=1, source_target_pairs={{0,24},{4,28},{8,16},{12,20},{16,8},{20,12},{24,0},{28,4},{1,25},{... | collective-permute-start | bytes 147464 | tf_op jit(solution)/shard_map/ppermute | solution.py:16
  50.8 4.2 %collective-permute-start.12 = (bf16[32,768]{1,0:T(8,128)(2,1)S(1)}, bf16[32,768]{1,0:T(8,128)(2,1)S(1)}, u32[]{:S(2)}, u32[]{:S(2)}) collective-permute-start(bf16[32,768]{1,0:T(8,128)(2,1)S(1)} %get-tuple-element.44), channel_id=1, source_target_pairs={{0,8},{4,12},{8,0},{12,4},{16,24},{20,28},{24,16},{28,20},{1,9},{5... | collective-permute-start | bytes 147464 | tf_op jit(solution)/shard_map/ppermute | solution.py:16
  51.4 4.7 %collective-permute-start.13 = (bf16[32,1280]{1,0:T(8,128)(2,1)S(1)}, bf16[32,1280]{1,0:T(8,128)(2,1)S(1)}, u32[]{:S(2)}, u32[]{:S(2)}) collective-permute-start(bf16[32,1280]{1,0:T(8,128)(2,1)S(1)} %pad_maximum_fusion), channel_id=1, source_target_pairs={{0,16},{4,20},{8,24},{12,28},{16,0},{20,4},{24,8},{28,12},{1,17},{... | collective-permute-start | bytes 245768 | tf_op jit(solution)/shard_map/ppermute | solution.py:16
  51.6 5.0 %collective-permute-start.11 = (bf16[96,512]{1,0:T(8,128)(2,1)S(1)}, bf16[96,512]{1,0:T(8,128)(2,1)S(1)}, u32[]{:S(2)}, u32[]{:S(2)}) collective-permute-start(bf16[96,512]{1,0:T(8,128)(2,1)S(1)} %constant_dynamic-update-slice_fusion.refs_0_), channel_id=1, source_target_pairs={{0,4},{4,0},{8,12},{12,8},{16,20},{20,16},{24,28},{28,24},{1,5},{5... | collective-permute-start | bytes 294920 | tf_op jit(solution)/shard_map/ppermute | solution.py:16
  51.6 5.0 %collective-permute-start.15 = (bf16[32,768]{1,0:T(8,128)(2,1)S(1)}, bf16[32,768]{1,0:T(8,128)(2,1)S(1)}, u32[]{:S(2)}, u32[]{:S(2)}) collective-permute-start(bf16[32,768]{1,0:T(8,128)(2,1)S(1)} %get-tuple-element.45.refs_2_), channel_id=1, source_target_pairs={{0,4},{4,0},{8,12},{12,8},{16,20},{20,16},{24,28},{28,24},{1,5},{5... | collective-permute-start | bytes 147464 | tf_op jit(solution)/shard_map/ppermute | solution.py:16
  53.8 2.9 %collective-permute-start.18 = (bf16[32,768]{1,0:T(8,128)(2,1)S(1)}, bf16[32,768]{1,0:T(8,128)(2,1)S(1)}, u32[]{:S(2)}, u32[]{:S(2)}) collective-permute-start(bf16[32,768]{1,0:T(8,128)(2,1)S(1)} %collective-permute-done.14.refs_5_), channel_id=1, source_target_pairs={{0,4},{4,0},{8,12},{12,8},{16,20},{20,16},{24,28},{28,24},{1,5},{5... | collective-permute-start | bytes 147464 | tf_op jit(solution)/shard_map/ppermute | solution.py:16
  55.0 1.7 %collective-permute-start.16 = (bf16[32,768]{1,0:T(8,128)(2,1)S(1)}, bf16[32,768]{1,0:T(8,128)(2,1)S(1)}, u32[]{:S(2)}, u32[]{:S(2)}) collective-permute-start(bf16[32,768]{1,0:T(8,128)(2,1)S(1)} %collective-permute-done.12.refs_3_), channel_id=1, source_target_pairs={{0,4},{4,0},{8,12},{12,8},{16,20},{20,16},{24,28},{28,24},{1,5},{5... | collective-permute-start | bytes 147464 | tf_op jit(solution)/shard_map/ppermute | solution.py:16
  56.1 1.3 %collective-permute-start.17 = (bf16[32,1280]{1,0:T(8,128)(2,1)S(1)}, bf16[32,1280]{1,0:T(8,128)(2,1)S(1)}, u32[]{:S(2)}, u32[]{:S(2)}) collective-permute-start(bf16[32,1280]{1,0:T(8,128)(2,1)S(1)} %collective-permute-done.13.refs_4_), channel_id=1, source_target_pairs={{0,4},{4,0},{8,12},{12,8},{16,20},{20,16},{24,28},{28,24},{1,5},{5... | collective-permute-start | bytes 245768 | tf_op jit(solution)/shard_map/ppermute | solution.py:16

commit v9 on v8

--- a/solution.py
+++ b/solution.py
@@ -80,7 +80,7 @@
                 ]
 
 
-def weigh(count_ref, fetched_ref, w_up_ref, *refs):
+def weigh(count_ref, upstream_ref, fetched_ref, w_up_ref, *refs):
     part_refs, (weight_ref, hidden_ref) = refs[:-2], refs[-2:]
     scores = part_refs[0][...]
     for part_ref in part_refs[1:]:
@@ -94,24 +94,36 @@
     pooled = jnp.dot(
         weight.astype(jnp.bfloat16), fetched_ref[...], preferred_element_type=jnp.float32
     ).astype(jnp.bfloat16)
-    hidden_ref[...] = jnp.dot(
+    units = w_up_ref.shape[1]
+    hidden_ref[:, :units] = jnp.dot(
         pooled, w_up_ref[...], preferred_element_type=jnp.float32
     ).astype(jnp.bfloat16)
-
-
-def turn(owners, upstream_ref, bias_ref, w_up_ref, fetched_ref, weight_ref, *refs):
+    hidden_ref[:, units:] = upstream_ref[...]
+
+
+def turn(owners, latent_ref, bias_ref, w_up_ref, fetched_ref, weight_ref, *refs):
     part_refs, (activated_ref, grad_ref, sending_ref) = refs[:-3], refs[-3:]
     latents = len(part_refs)
     members, slot_count = weight_ref.shape
     capacity = slot_count // owners
     half = members // 2
-    hidden = part_refs[0][...].astype(jnp.float32)
+    units = bias_ref.shape[1]
+    hidden = part_refs[0][:, :units].astype(jnp.float32)
     for part_ref in part_refs[1:]:
-        hidden = hidden + part_ref[...].astype(jnp.float32)
+        hidden = hidden + part_ref[:, :units].astype(jnp.float32)
+    upstream = []
+    for z in range(latents):
+        piece = part_refs[0][:, units:].astype(jnp.float32)
+        for k in range(1, latents):
+            piece = jnp.where(
+                latent_ref[0] ^ z == k, part_refs[k][:, units:].astype(jnp.float32), piece
+            )
+        upstream.append(piece)
+    upstream = jnp.concatenate(upstream, axis=1)
     hidden = hidden + bias_ref[...]
     activated, backward = jax.vjp(jax.nn.gelu, hidden)
     activated_ref[...] = activated.astype(jnp.bfloat16)
-    slopes = backward(upstream_ref[...].astype(jnp.float32))[0].astype(jnp.bfloat16)
+    slopes = backward(upstream)[0].astype(jnp.bfloat16)
     along = (((1,), (1,)), ((), ()))
     grad = lax.dot_general(
         slopes, w_up_ref[...], along, preferred_element_type=jnp.float32
@@ -204,11 +216,6 @@
     bf16 = jnp.bfloat16
 
     wanted = exchange(requests.reshape(owners, 1, capacity))
-    parts = jnp.stack([upstream] + [swap(upstream, "latent", k) for k in range(1, latents)])
-    upstream_full = jnp.concatenate(
-        [lax.dynamic_index_in_dim(parts, latent ^ z, 0, keepdims=False) for z in range(latents)],
-        axis=1,
-    )
     count = call(
         count_slots, shape((members, slot_count), jnp.float32), (history,), [vmem]
     )
@@ -219,7 +226,6 @@
     )
 
     fetched = exchange(chosen.reshape(owners, capacity, row_width)).reshape(slot_count, row_width)
-    fetched, upstream_full = lax.optimization_barrier((fetched, upstream_full))
 
     slot_scores = jnp.einsum("ud,sd->us", targets, fetched, preferred_element_type=jnp.float32)
     late_targets, slot_scores = lax.optimization_barrier((targets, slot_scores))
@@ -228,9 +234,9 @@
     parts, near_targets = lax.optimization_barrier((parts, near_targets))
     weight, partial_hidden = call(
         weigh,
-        (shape((members, slot_count), jnp.float32), shape((members, bias.shape[0]), bf16)),
-        (count, fetched, w_up, *parts),
-        [vmem] * (3 + latents),
+        (shape((members, slot_count), jnp.float32), shape((members, bias.shape[0] + hidden_share), bf16)),
+        (count, upstream, fetched, w_up, *parts),
+        [vmem] * (4 + latents),
     )
     partial_hidden, late_targets = lax.optimization_barrier((partial_hidden, targets))
     parts = [partial_hidden] + [swap(partial_hidden, "latent", k) for k in range(1, latents)]
@@ -238,12 +244,12 @@
     activated, pooled_grad, sending = call(
         functools.partial(turn, owners),
         (
-            shape(partial_hidden.shape, bf16),
+            shape((members, bias.shape[0]), bf16),
             shape((members, row_width), bf16),
             shape((owners * latents, half, 2 * capacity), bf16),
         ),
-        (upstream_full, bias.reshape(1, -1), w_up, fetched, weight, *parts),
-        [vmem] * (5 + latents),
+        (latent.reshape(1).astype(jnp.int32), bias.reshape(1, -1), w_up, fetched, weight, *parts),
+        [smem] + [vmem] * (4 + latents),
     )
     output = lax.dynamic_slice_in_dim(activated, latent * hidden_share, hidden_share, axis=1)
 

time: 59.8 us -> 59.3 us (level)
  blocking collectives: 0 us -> 12.4 us
  starting transfers between devices: 32.5 us -> 22.8 us
  waiting for transfers between devices: 16.6 us -> 14.3 us
  Pallas kernels: 6.72 us -> 5.93 us
    all_to_all x0 -> x1, blocking collectives: none -> 12.4 us  [exchange(): return lax.all_to_all(x, 'batch', split_axis=0, concat_axis=0, tiled=True)]
    ppermute x19 -> x16, starting transfers between devices: 20.2 us -> 14 us  [swap(): return lax.ppermute(x, axis, [(i, i ^ k) for i in range(n)])]
    all_to_all x2 -> x1, starting transfers between devices: 8.81 us -> 5.18 us  [exchange(): return lax.all_to_all(x, 'batch', split_axis=0, concat_axis=0, tiled=True)]
    ppermute x19 -> x16, waiting for transfers between devices: 14.3 us -> 12.9 us  [swap(): return lax.ppermute(x, axis, [(i, i ^ k) for i in range(n)])]
    all_to_all x2 -> x1, waiting for transfers between devices: 2.28 us -> 1.45 us  [exchange(): return lax.all_to_all(x, 'batch', split_axis=0, concat_axis=0, tiled=True)]
    pallas_call x7, Pallas kernels: 6.72 us -> 5.93 us  [call(): pl.pallas_call(kernel, out_shape=shapes, in_specs=specs, out_specs=jax.tr...]
  transfers between devices with their start and end apart: 22 -> 18, of which waited for: 12 -> 9; matrix products, arithmetic and copies ran while one was open for 1% -> 1% of each run, Pallas kernels for 5% -> 5%
where the time goes in v9:
time: 59.3 us; the launch traced here: 59 us
  starting transfers between devices  22.8 us (38%)
  waiting for transfers between devices  14.3 us (24%)
  blocking collectives  12.4 us (21%)
  Pallas kernels  5.93 us (10%)
  local copies, waits for them, and re-layouts  2.54 us (4%)
  between operations  0.72 us (1%)
    ppermute x16, starting transfers between devices, swap(): return lax.ppermute(x, axis, [(i, i ^ k) for i in range(n)])  14 us
    ppermute x16, waiting for transfers between devices, swap(): return lax.ppermute(x, axis, [(i, i ^ k) for i in range(n)])  12.9 us
    all_to_all x1, blocking collectives, exchange(): return lax.all_to_all(x, 'batch', split_axis=0, concat_axis=0, tiled=True)  12.4 us
    pallas_call x7, Pallas kernels, call(): pl.pallas_call(kernel, out_shape=shapes, in_specs=specs, out_specs=jax.tr...  5.93 us
    all_to_all x1, starting transfers between devices, exchange(): return lax.all_to_all(x, 'batch', split_axis=0, concat_axis=0, tiled=True)  5.18 us
    all_to_all x1, starting transfers between devices, on_device(): lax.all_to_all(sending, ('batch', 'latent'), split_axis=0, concat_axis=0,...  3.56 us
    unnamed x14, local copies, waits for them, and re-layouts  1.91 us
    all_to_all x1, waiting for transfers between devices, exchange(): return lax.all_to_all(x, 'batch', split_axis=0, concat_axis=0, tiled=True)  1.45 us
  transfers between devices with their start and end apart: 18, of which 9 were waited for; matrix products, arithmetic and copies ran while one was open for 1% of the time, Pallas kernels for 5%

profile of v9, /device:TPU:0, one launch (start us, length us, event | category | flops | bytes accessed | tf_op | source)
XLA Modules:
  0.0 59.0 jit_solution(9927202610914303509)
XLA Ops:
  0.6 5.2 %all-to-all-start = ((s32[8,1,64]{2,1,0:T(1,128)}), s32[8,1,64]{2,1,0:T(1,128)S(1)}, u32[]{:S(2)}, u32[]{:S(2)}) async-start(s32[8,1,64]{2,1,0:T(1,128)} %bitcast.23), calls=%async_computation | async-start | bytes 8192 | tf_op jit(solution)/shard_map/all_to_all | solution.py:20
  5.8 0.8 %copy-done.2 = s32[32,512]{1,0:T(8,128)S(1)} copy-done((s32[32,512]{1,0:T(8,128)S(1)}, s32[32,512]{1,0:T(8,128)}, u32[]{:S(2)}) %copy-start.2) | copy-done | bytes 65560
  6.7 1.2 %count_slots.1.count_ref = f32[32,512]{1,0:T(8,128)S(1)} custom-call(s32[32,512]{1,0:T(8,128)S(1)} %copy-done.2), custom_call_target="tpu_custom_call" | custom-call | tf_op jit(solution)/shard_map/count_slots/pallas_call | solution.py:24
  7.9 1.1 %copy-done.1 = bf16[512,512]{1,0:T(8,128)(2,1)S(1)} copy-done((bf16[512,512]{1,0:T(8,128)(2,1)S(1)}, bf16[512,512]{1,0:T(8,128)(2,1)}, u32[]{:S(2)}) %copy-start.1) | copy-done | bytes 524312
  8.9 1.5 %all-to-all-done.wanted_ref = s32[8,1,64]{2,1,0:T(1,128)S(1)} async-done(((s32[8,1,64]{2,1,0:T(1,128)}), s32[8,1,64]{2,1,0:T(1,128)S(1)}, u32[]{:S(2)}, u32[]{:S(2)}) %all-to-all-start) | async-done | bytes 2080 | tf_op jit(solution)/shard_map/all_to_all | solution.py:20
  10.4 0.6 pick_rows.1
  11.0 0.0 copy-start
  11.0 12.4 %all_to_all.15 = bf16[8,64,512]{2,1,0:T(8,128)(2,1)S(1)} all-to-all(bf16[8,64,512]{2,1,0:T(8,128)(2,1)S(1)} %bitcast.21), channel_id=1, replica_groups=mesh['batch'=8,'latent'=4] {'batch'}, dimensions={0} | all-to-all | bytes 1048576 | tf_op jit(solution)/shard_map/all_to_all | solution.py:20
  23.4 0.0 copy-done.5
  23.4 0.2 convolution_bitcast_fusion.refs_0_
  23.7 3.6 %collective-permute-start.2 = (f32[32,512]{1,0:T(8,128)S(1)}, f32[32,512]{1,0:T(8,128)S(1)}, u32[]{:S(2)}, u32[]{:S(2)}) collective-permute-start(f32[32,512]{1,0:T(8,128)S(1)} %convolution_bitcast_fusion.refs_0_), channel_id=1, source_target_pairs={{0,3},{1,2},{2,1},{3,0},{4,7},{5,6},{6,5},{7,4},{8,11},{9,10},{10,... | collective-permute-start | bytes 196616 | tf_op jit(solution)/shard_map/ppermute | solution.py:16
  27.3 0.0 collective-permute-start.1
  27.3 0.8 %collective-permute-start = (f32[32,512]{1,0:T(8,128)S(1)}, f32[32,512]{1,0:T(8,128)S(1)}, u32[]{:S(2)}, u32[]{:S(2)}) collective-permute-start(f32[32,512]{1,0:T(8,128)S(1)} %convolution_bitcast_fusion.refs_0_), channel_id=1, source_target_pairs={{0,1},{1,0},{2,3},{3,2},{4,5},{5,4},{6,7},{7,6},{8,9},{9,8},{10,11... | collective-permute-start | bytes 196616 | tf_op jit(solution)/shard_map/ppermute | solution.py:16
  28.1 0.6 collective-permute-start.3
  28.6 3.3 %collective-permute-done.3 = bf16[32,512]{1,0:T(8,128)(2,1)S(1)} collective-permute-done((bf16[32,512]{1,0:T(8,128)(2,1)S(1)}, bf16[32,512]{1,0:T(8,128)(2,1)S(1)}, u32[]{:S(2)}, u32[]{:S(2)}) %collective-permute-start.3) | collective-permute-done | bytes 32800 | tf_op jit(solution)/shard_map/ppermute | solution.py:16
  32.0 0.0 collective-permute-done.2.refs_3_
  32.0 0.6 %collective-permute-done.1.refs_2_ = f32[32,512]{1,0:T(8,128)S(1)} collective-permute-done((f32[32,512]{1,0:T(8,128)S(1)}, f32[32,512]{1,0:T(8,128)S(1)}, u32[]{:S(2)}, u32[]{:S(2)}) %collective-permute-start.1) | collective-permute-done | bytes 65568 | tf_op jit(solution)/shard_map/ppermute | solution.py:16
  32.6 0.0 collective-permute-done.refs_1_
  32.6 0.6 %weigh.1 = (f32[32,512]{1,0:T(8,128)S(1)}, bf16[32,1280]{1,0:T(8,128)(2,1)S(1)}) custom-call(f32[32,512]{1,0:T(8,128)S(1)} %count_slots.1.count_ref, bf16[32,256]{1,0:T(8,128)(2,1)S(1)} %copy-done.3, bf16[512,512]{1,0:T(8,128)(2,1)S(1)} %bitcast.19, bf16[512,1024]{1,0:T(8,128)(2,1)S(1)} %copy-done, f32[32,512]{1,0:T(8,128)S(1)} %convolution_bitcast_fusion.refs_0_, ...), custom_call_target="tpu_custom_call" | custom-call | tf_op jit(solution)/shard_map/weigh/pallas_call | solution.py:24
  33.2 3.1 %collective-permute-start.6 = (bf16[32,1280]{1,0:T(8,128)(2,1)S(1)}, bf16[32,1280]{1,0:T(8,128)(2,1)S(1)}, u32[]{:S(2)}, u32[]{:S(2)}) collective-permute-start(bf16[32,1280]{1,0:T(8,128)(2,1)S(1)} %get-tuple-element.30.refs_0_), channel_id=1, source_target_pairs={{0,3},{1,2},{2,1},{3,0},{4,7},{5,6},{6,5},{7,4},{8,11},{9,10},{10,... | collective-permute-start | bytes 245768 | tf_op jit(solution)/shard_map/ppermute | solution.py:16
  36.2 0.0 collective-permute-start.5
  36.3 1.4 %collective-permute-start.4 = (bf16[32,1280]{1,0:T(8,128)(2,1)S(1)}, bf16[32,1280]{1,0:T(8,128)(2,1)S(1)}, u32[]{:S(2)}, u32[]{:S(2)}) collective-permute-start(bf16[32,1280]{1,0:T(8,128)(2,1)S(1)} %get-tuple-element.30.refs_0_), channel_id=1, source_target_pairs={{0,1},{1,0},{2,3},{3,2},{4,5},{5,4},{6,7},{7,6},{8,9},{9,8},{10,11... | collective-permute-start | bytes 245768 | tf_op jit(solution)/shard_map/ppermute | solution.py:16
  37.6 0.6 collective-permute-start.7
  38.2 1.7 %collective-permute-done.6.refs_3_ = bf16[32,1280]{1,0:T(8,128)(2,1)S(1)} collective-permute-done((bf16[32,1280]{1,0:T(8,128)(2,1)S(1)}, bf16[32,1280]{1,0:T(8,128)(2,1)S(1)}, u32[]{:S(2)}, u32[]{:S(2)}) %collective-permute-start.6) | collective-permute-done | bytes 81952 | tf_op jit(solution)/shard_map/ppermute | solution.py:16
  39.9 2.6 %collective-permute-done.5.refs_2_ = bf16[32,1280]{1,0:T(8,128)(2,1)S(1)} collective-permute-done((bf16[32,1280]{1,0:T(8,128)(2,1)S(1)}, bf16[32,1280]{1,0:T(8,128)(2,1)S(1)}, u32[]{:S(2)}, u32[]{:S(2)}) %collective-permute-start.5) | collective-permute-done | bytes 81952 | tf_op jit(solution)/shard_map/ppermute | solution.py:16
  42.5 0.0 collective-permute-done.4.refs_1_
  42.5 1.4 %turn.1 = (bf16[32,1024]{1,0:T(8,128)(2,1)S(1)}, bf16[32,512]{1,0:T(8,128)(2,1)S(1)}, bf16[32,16,128]{2,1,0:T(8,128)(2,1)}) custom-call(s32[1]{0:T(128)} %bitcast.latent_ref, f32[1,1024]{1,0:T(1,128)S(1)} %bitcast.22, bf16[512,1024]{1,0:T(8,128)(2,1)S(1)} %copy-done, bf16[512,512]{1,0:T(8,128)(2,1)S(1)} %bitcast.20, ...), custom_call_target="tpu_custom_call" | custom-call | tf_op jit(solution)/shard_map/turn/pallas_call | solution.py:24
  44.0 0.0 collective-permute-done.7
  44.0 3.6 %all-to-all-start.2 = ((bf16[32,16,128]{2,1,0:T(8,128)(2,1)}), bf16[32,16,128]{2,1,0:T(8,128)(2,1)S(1)}, u32[]{:S(2)}, u32[]{:S(2)}) async-start(bf16[32,16,128]{2,1,0:T(8,128)(2,1)} %get-tuple-element.34), calls=%async_computation.2 | async-start | bytes 262144 | tf_op jit(solution)/shard_map/all_to_all | solution.py:257
  47.6 2.7 %collective-permute-start.11 = (bf16[32,768]{1,0:T(8,128)(2,1)S(1)}, bf16[32,768]{1,0:T(8,128)(2,1)S(1)}, u32[]{:S(2)}, u32[]{:S(2)}) collective-permute-start(bf16[32,768]{1,0:T(8,128)(2,1)S(1)} %get-tuple-element.38), channel_id=1, source_target_pairs={{0,24},{4,28},{8,16},{12,20},{16,8},{20,12},{24,0},{28,4},{1,25},{... | collective-permute-start | bytes 147464 | tf_op jit(solution)/shard_map/ppermute | solution.py:16
  50.3 0.6 collective-permute-start.9
  50.9 0.3 collective-permute-start.10
  51.2 0.0 collective-permute-start.8
  51.2 0.5 collective-permute-start.12
  51.7 1.7 %collective-permute-done.11.refs_5_ = bf16[32,768]{1,0:T(8,128)(2,1)S(1)} collective-permute-done((bf16[32,768]{1,0:T(8,128)(2,1)S(1)}, bf16[32,768]{1,0:T(8,128)(2,1)S(1)}, u32[]{:S(2)}, u32[]{:S(2)}) %collective-permute-start.11) | collective-permute-done | bytes 49184 | tf_op jit(solution)/shard_map/ppermute | solution.py:16
  53.4 0.0 collective-permute-start.15
  53.4 1.2 %collective-permute-done.9.refs_3_ = bf16[32,768]{1,0:T(8,128)(2,1)S(1)} collective-permute-done((bf16[32,768]{1,0:T(8,128)(2,1)S(1)}, bf16[32,768]{1,0:T(8,128)(2,1)S(1)}, u32[]{:S(2)}, u32[]{:S(2)}) %collective-permute-start.9) | collective-permute-done | bytes 49184 | tf_op jit(solution)/shard_map/ppermute | solution.py:16
  54.6 0.0 collective-permute-start.13
  54.6 1.0 %collective-permute-done.10.refs_4_ = bf16[32,1280]{1,0:T(8,128)(2,1)S(1)} collective-permute-done((bf16[32,1280]{1,0:T(8,128)(2,1)S(1)}, bf16[32,1280]{1,0:T(8,128)(2,1)S(1)}, u32[]{:S(2)}, u32[]{:S(2)}) %collective-permute-start.10) | collective-permute-done | bytes 81952 | tf_op jit(solution)/shard_map/ppermute | solution.py:16
  55.6 0.0 collective-permute-start.14
  55.6 0.6 %constant_dynamic-slice_fusion = bf16[32,256]{1,0:T(8,128)(2,1)} fusion(bf16[32,1024]{1,0:T(8,128)(2,1)S(1)} %get-tuple-element.31, s32[]{:T(128)S(6)} %select_n.3), kind=kLoop, calls=%fused_computation.9 | loop fusion | bytes 32772 | tf_op jit(solution)/shard_map/dynamic_slice | solution.py:254
  56.2 0.0 collective-permute-done.12.refs_6_
  56.2 0.0 collective-permute-done.8.refs_1_
  56.2 0.0 collective-permute-done.15.refs_9_
  56.2 0.0 collective-permute-done.13.refs_7_
  56.2 0.6 %collective-permute-done.14.refs_8_ = bf16[32,1280]{1,0:T(8,128)(2,1)S(1)} collective-permute-done((bf16[32,1280]{1,0:T(8,128)(2,1)S(1)}, bf16[32,1280]{1,0:T(8,128)(2,1)S(1)}, u32[]{:S(2)}, u32[]{:S(2)}) %collective-permute-start.14) | collective-permute-done | bytes 81952 | tf_op jit(solution)/shard_map/ppermute | solution.py:16
  56.9 0.0 all-to-all-done.2.sent_ref
  56.9 2.1 %add_rows.1 = f32[512,512]{1,0:T(8,128)} custom-call(s32[1]{0:T(128)} %bitcast.6.me_ref, s32[8,1,64]{2,1,0:T(1,128)S(1)} %all-to-all-done.wanted_ref, bf16[32,16,128]{2,1,0:T(8,128)(2,1)S(1)} %all-to-all-done.2.sent_ref, bf16[96,512]{1,0:T(8,128)(2,1)S(1)} %constant_dynamic-update-slice_fusion.refs_0_, bf16[96,512]{1,0:T(8,128)(2,1)S(1)} %collective-permute-done.8.refs_1_, ...), custom_call_target="tpu_custom_call" | custom-call | tf_op jit(solution)/shard_map/add_rows/pallas_call | solution.py:24
  (15 shorter events, 0.1 us)
Async XLA Ops:
  0.6 9.8 %all-to-all-start = ((s32[8,1,64]{2,1,0:T(1,128)}), s32[8,1,64]{2,1,0:T(1,128)S(1)}, u32[]{:S(2)}, u32[]{:S(2)}) async-start(s32[8,1,64]{2,1,0:T(1,128)} %bitcast.23), calls=%async_computation | async-start | bytes 8192 | tf_op jit(solution)/shard_map/all_to_all | solution.py:20
  5.8 0.8 %copy-start.2 = (s32[32,512]{1,0:T(8,128)S(1)}, s32[32,512]{1,0:T(8,128)}, u32[]{:S(2)}) copy-start(s32[32,512]{1,0:T(8,128)} %history_ref.1) | copy-start | bytes 196612
  7.9 1.1 %copy-start.1 = (bf16[512,512]{1,0:T(8,128)(2,1)S(1)}, bf16[512,512]{1,0:T(8,128)(2,1)}, u32[]{:S(2)}) copy-start(bf16[512,512]{1,0:T(8,128)(2,1)} %rows_ref.1) | copy-start | bytes 1572868
  10.4 13.0 %copy-start.5 = (bf16[32,512]{1,0:T(8,128)(2,1)S(1)}, bf16[32,512]{1,0:T(8,128)(2,1)}, u32[]{:S(2)}) copy-start(bf16[32,512]{1,0:T(8,128)(2,1)} %param.8) | copy-start | bytes 98308
  11.0 21.6 %copy-start = (bf16[512,1024]{1,0:T(8,128)(2,1)S(1)}, bf16[512,1024]{1,0:T(8,128)(2,1)}, u32[]{:S(2)}) copy-start(bf16[512,1024]{1,0:T(8,128)(2,1)} %w_up_ref.3) | copy-start | bytes 3145732
  23.7 8.3 %collective-permute-start.2 = (f32[32,512]{1,0:T(8,128)S(1)}, f32[32,512]{1,0:T(8,128)S(1)}, u32[]{:S(2)}, u32[]{:S(2)}) collective-permute-start(f32[32,512]{1,0:T(8,128)S(1)} %convolution_bitcast_fusion.refs_0_), channel_id=1, source_target_pairs={{0,3},{1,2},{2,1},{3,0},{4,7},{5,6},{6,5},{7,4},{8,11},{9,10},{10,... | collective-permute-start | bytes 196616 | tf_op jit(solution)/shard_map/ppermute | solution.py:16
  27.3 5.3 %collective-permute-start.1 = (f32[32,512]{1,0:T(8,128)S(1)}, f32[32,512]{1,0:T(8,128)S(1)}, u32[]{:S(2)}, u32[]{:S(2)}) collective-permute-start(f32[32,512]{1,0:T(8,128)S(1)} %convolution_bitcast_fusion.refs_0_), channel_id=1, source_target_pairs={{0,2},{1,3},{2,0},{3,1},{4,6},{5,7},{6,4},{7,5},{8,10},{9,11},{10,... | collective-permute-start | bytes 196616 | tf_op jit(solution)/shard_map/ppermute | solution.py:16
  27.3 5.3 %collective-permute-start = (f32[32,512]{1,0:T(8,128)S(1)}, f32[32,512]{1,0:T(8,128)S(1)}, u32[]{:S(2)}, u32[]{:S(2)}) collective-permute-start(f32[32,512]{1,0:T(8,128)S(1)} %convolution_bitcast_fusion.refs_0_), channel_id=1, source_target_pairs={{0,1},{1,0},{2,3},{3,2},{4,5},{5,4},{6,7},{7,6},{8,9},{9,8},{10,11... | collective-permute-start | bytes 196616 | tf_op jit(solution)/shard_map/ppermute | solution.py:16
  28.1 3.9 %collective-permute-start.3 = (bf16[32,512]{1,0:T(8,128)(2,1)S(1)}, bf16[32,512]{1,0:T(8,128)(2,1)S(1)}, u32[]{:S(2)}, u32[]{:S(2)}) collective-permute-start(bf16[32,512]{1,0:T(8,128)(2,1)S(1)} %copy-done.5), channel_id=1, source_target_pairs={{0,8},{4,12},{8,0},{12,4},{16,24},{20,28},{24,16},{28,20},{1,9},{5... | collective-permute-start | bytes 98312 | tf_op jit(solution)/shard_map/ppermute | solution.py:16
  28.6 4.0 %copy-start.3 = (bf16[32,256]{1,0:T(8,128)(2,1)S(1)}, bf16[32,256]{1,0:T(8,128)(2,1)}, u32[]{:S(2)}) copy-start(bf16[32,256]{1,0:T(8,128)(2,1)} %upstream_ref.1) | copy-start | bytes 49156
  33.2 6.7 %collective-permute-start.6 = (bf16[32,1280]{1,0:T(8,128)(2,1)S(1)}, bf16[32,1280]{1,0:T(8,128)(2,1)S(1)}, u32[]{:S(2)}, u32[]{:S(2)}) collective-permute-start(bf16[32,1280]{1,0:T(8,128)(2,1)S(1)} %get-tuple-element.30.refs_0_), channel_id=1, source_target_pairs={{0,3},{1,2},{2,1},{3,0},{4,7},{5,6},{6,5},{7,4},{8,11},{9,10},{10,... | collective-permute-start | bytes 245768 | tf_op jit(solution)/shard_map/ppermute | solution.py:16
  36.2 6.3 %collective-permute-start.5 = (bf16[32,1280]{1,0:T(8,128)(2,1)S(1)}, bf16[32,1280]{1,0:T(8,128)(2,1)S(1)}, u32[]{:S(2)}, u32[]{:S(2)}) collective-permute-start(bf16[32,1280]{1,0:T(8,128)(2,1)S(1)} %get-tuple-element.30.refs_0_), channel_id=1, source_target_pairs={{0,2},{1,3},{2,0},{3,1},{4,6},{5,7},{6,4},{7,5},{8,10},{9,11},{10,... | collective-permute-start | bytes 245768 | tf_op jit(solution)/shard_map/ppermute | solution.py:16
  36.3 6.3 %collective-permute-start.4 = (bf16[32,1280]{1,0:T(8,128)(2,1)S(1)}, bf16[32,1280]{1,0:T(8,128)(2,1)S(1)}, u32[]{:S(2)}, u32[]{:S(2)}) collective-permute-start(bf16[32,1280]{1,0:T(8,128)(2,1)S(1)} %get-tuple-element.30.refs_0_), channel_id=1, source_target_pairs={{0,1},{1,0},{2,3},{3,2},{4,5},{5,4},{6,7},{7,6},{8,9},{9,8},{10,11... | collective-permute-start | bytes 245768 | tf_op jit(solution)/shard_map/ppermute | solution.py:16
  37.6 6.4 %collective-permute-start.7 = (bf16[32,512]{1,0:T(8,128)(2,1)S(1)}, bf16[32,512]{1,0:T(8,128)(2,1)S(1)}, u32[]{:S(2)}, u32[]{:S(2)}) collective-permute-start(bf16[32,512]{1,0:T(8,128)(2,1)S(1)} %copy-done.5), channel_id=1, source_target_pairs={{0,16},{4,20},{8,24},{12,28},{16,0},{20,4},{24,8},{28,12},{1,17},{... | collective-permute-start | bytes 98312 | tf_op jit(solution)/shard_map/ppermute | solution.py:16
  38.2 4.4 %copy-start.4 = (f32[1024]{0:T(1024)S(1)}, f32[1024]{0:T(1024)}, u32[]{:S(2)}) copy-start(f32[1024]{0:T(1024)} %param.10) | copy-start | bytes 12292
  44.0 12.9 %all-to-all-start.2 = ((bf16[32,16,128]{2,1,0:T(8,128)(2,1)}), bf16[32,16,128]{2,1,0:T(8,128)(2,1)S(1)}, u32[]{:S(2)}, u32[]{:S(2)}) async-start(bf16[32,16,128]{2,1,0:T(8,128)(2,1)} %get-tuple-element.34), calls=%async_computation.2 | async-start | bytes 262144 | tf_op jit(solution)/shard_map/all_to_all | solution.py:257
  47.6 5.7 %collective-permute-start.11 = (bf16[32,768]{1,0:T(8,128)(2,1)S(1)}, bf16[32,768]{1,0:T(8,128)(2,1)S(1)}, u32[]{:S(2)}, u32[]{:S(2)}) collective-permute-start(bf16[32,768]{1,0:T(8,128)(2,1)S(1)} %get-tuple-element.38), channel_id=1, source_target_pairs={{0,24},{4,28},{8,16},{12,20},{16,8},{20,12},{24,0},{28,4},{1,25},{... | collective-permute-start | bytes 147464 | tf_op jit(solution)/shard_map/ppermute | solution.py:16
  50.3 4.2 %collective-permute-start.9 = (bf16[32,768]{1,0:T(8,128)(2,1)S(1)}, bf16[32,768]{1,0:T(8,128)(2,1)S(1)}, u32[]{:S(2)}, u32[]{:S(2)}) collective-permute-start(bf16[32,768]{1,0:T(8,128)(2,1)S(1)} %get-tuple-element.40), channel_id=1, source_target_pairs={{0,8},{4,12},{8,0},{12,4},{16,24},{20,28},{24,16},{28,20},{1,9},{5... | collective-permute-start | bytes 147464 | tf_op jit(solution)/shard_map/ppermute | solution.py:16
  50.9 4.7 %collective-permute-start.10 = (bf16[32,1280]{1,0:T(8,128)(2,1)S(1)}, bf16[32,1280]{1,0:T(8,128)(2,1)S(1)}, u32[]{:S(2)}, u32[]{:S(2)}) collective-permute-start(bf16[32,1280]{1,0:T(8,128)(2,1)S(1)} %pad_maximum_fusion), channel_id=1, source_target_pairs={{0,16},{4,20},{8,24},{12,28},{16,0},{20,4},{24,8},{28,12},{1,17},{... | collective-permute-start | bytes 245768 | tf_op jit(solution)/shard_map/ppermute | solution.py:16
  51.2 5.0 %collective-permute-start.8 = (bf16[96,512]{1,0:T(8,128)(2,1)S(1)}, bf16[96,512]{1,0:T(8,128)(2,1)S(1)}, u32[]{:S(2)}, u32[]{:S(2)}) collective-permute-start(bf16[96,512]{1,0:T(8,128)(2,1)S(1)} %constant_dynamic-update-slice_fusion.refs_0_), channel_id=1, source_target_pairs={{0,4},{4,0},{8,12},{12,8},{16,20},{20,16},{24,28},{28,24},{1,5},{5... | collective-permute-start | bytes 294920 | tf_op jit(solution)/shard_map/ppermute | solution.py:16
  51.2 5.0 %collective-permute-start.12 = (bf16[32,768]{1,0:T(8,128)(2,1)S(1)}, bf16[32,768]{1,0:T(8,128)(2,1)S(1)}, u32[]{:S(2)}, u32[]{:S(2)}) collective-permute-start(bf16[32,768]{1,0:T(8,128)(2,1)S(1)} %get-tuple-element.41.refs_2_), channel_id=1, source_target_pairs={{0,4},{4,0},{8,12},{12,8},{16,20},{20,16},{24,28},{28,24},{1,5},{5... | collective-permute-start | bytes 147464 | tf_op jit(solution)/shard_map/ppermute | solution.py:16
  53.4 2.9 %collective-permute-start.15 = (bf16[32,768]{1,0:T(8,128)(2,1)S(1)}, bf16[32,768]{1,0:T(8,128)(2,1)S(1)}, u32[]{:S(2)}, u32[]{:S(2)}) collective-permute-start(bf16[32,768]{1,0:T(8,128)(2,1)S(1)} %collective-permute-done.11.refs_5_), channel_id=1, source_target_pairs={{0,4},{4,0},{8,12},{12,8},{16,20},{20,16},{24,28},{28,24},{1,5},{5... | collective-permute-start | bytes 147464 | tf_op jit(solution)/shard_map/ppermute | solution.py:16
  54.6 1.7 %collective-permute-start.13 = (bf16[32,768]{1,0:T(8,128)(2,1)S(1)}, bf16[32,768]{1,0:T(8,128)(2,1)S(1)}, u32[]{:S(2)}, u32[]{:S(2)}) collective-permute-start(bf16[32,768]{1,0:T(8,128)(2,1)S(1)} %collective-permute-done.9.refs_3_), channel_id=1, source_target_pairs={{0,4},{4,0},{8,12},{12,8},{16,20},{20,16},{24,28},{28,24},{1,5},{5... | collective-permute-start | bytes 147464 | tf_op jit(solution)/shard_map/ppermute | solution.py:16
  55.6 1.3 %collective-permute-start.14 = (bf16[32,1280]{1,0:T(8,128)(2,1)S(1)}, bf16[32,1280]{1,0:T(8,128)(2,1)S(1)}, u32[]{:S(2)}, u32[]{:S(2)}) collective-permute-start(bf16[32,1280]{1,0:T(8,128)(2,1)S(1)} %collective-permute-done.10.refs_4_), channel_id=1, source_target_pairs={{0,4},{4,0},{8,12},{12,8},{16,20},{20,16},{24,28},{28,24},{1,5},{5... | collective-permute-start | bytes 245768 | tf_op jit(solution)/shard_map/ppermute | solution.py:16

commit v10 on v9

--- a/solution.py
+++ b/solution.py
@@ -141,16 +141,28 @@
             sending_ref[o * latents + z] = block
 
 
-def make_late(me_ref, weight_ref, grad_ref, out_ref):
-    count, _, width = out_ref.shape
-    pair = (width - grad_ref.shape[1]) // 2
-    for i in range(count):
+def carried(k, early):
+    return (k ^ 2) // 2 >= early, (k ^ 4) // 2 >= early
+
+
+def make_late(early, me_ref, weight_ref, grad_ref, near_ref, far_ref, *out_refs):
+    width = grad_ref.shape[1]
+    pair = (out_refs[0].shape[1] - width) // 2
+    half = width // 2
+    for i, out_ref in enumerate(out_refs):
         first = pl.multiple_of((me_ref[0] // 2 ^ i) * pair, pair)
         weight = weight_ref[:, pl.ds(first, pair)]
         high = weight.astype(jnp.bfloat16)
-        out_ref[i, :, :pair] = high
-        out_ref[i, :, pair : 2 * pair] = (weight - high.astype(jnp.float32)).astype(jnp.bfloat16)
-        out_ref[i, :, 2 * pair :] = grad_ref[...]
+        out_ref[:, :pair] = high
+        out_ref[:, pair : 2 * pair] = (weight - high.astype(jnp.float32)).astype(jnp.bfloat16)
+        at = 2 * pair + width
+        out_ref[:, 2 * pair : at] = grad_ref[...]
+        near, far = carried(2 * i, early) if i else (False, False)
+        if near:
+            out_ref[:, at : at + half] = near_ref[:, half:]
+            at += half
+        if far:
+            out_ref[:, at : at + half] = far_ref[:, :half]
 
 
 def add_rows(latents, early, me_ref, wanted_ref, sent_ref, *refs):
@@ -182,7 +194,14 @@
         if i < early:
             targets = target_refs[side][i * members : (i + 1) * members, :]
         else:
-            targets = late_refs[side * (owners // 2) + (i ^ 1)][:, 2 * pair + width :]
+            half = width // 2
+            base = 2 * pair + width
+            near_ref = late_refs[side * (owners // 2) + (i ^ 1)]
+            far_ref = late_refs[side * (owners // 2) + (i ^ 2)]
+            at = base + (half if carried(2 * (i ^ 2), early)[0] else 0)
+            targets = jnp.concatenate(
+                [far_ref[:, at : at + half], near_ref[:, base : base + half]], axis=1
+            )
         weight_high = of_me(late_ref[:, :pair])
         weight_low = of_me(late_ref[:, pair : 2 * pair])
         chosen = (wanted_ref[d] == places).astype(jnp.bfloat16)
@@ -255,20 +274,19 @@
 
     sending, far_targets = lax.optimization_barrier((sending, far_targets))
     sent = lax.all_to_all(sending, ("batch", "latent"), split_axis=0, concat_axis=0, tiled=True)
-    late = call(
-        make_late,
-        shape((owners // 2, members, 4 * capacity + row_width), bf16),
-        (me, weight, pooled_grad),
-        [smem, vmem, vmem],
-    )
     even_targets = [targets] + near_targets + far_targets
     early = len(even_targets)
-    even_late = [late[0]]
-    for k in range(2, owners, 2):
-        message = late[k // 2]
-        if (k ^ 2) // 2 >= early:
-            message = jnp.concatenate([message, near_targets[0]], axis=1)
-        even_late.append(swap(message, "batch", k))
+    base = 4 * capacity + row_width
+    late = call(
+        functools.partial(make_late, early),
+        tuple(
+            shape((members, base + (sum(carried(k, early)) * row_width // 2 if k else 0)), bf16)
+            for k in range(0, owners, 2)
+        ),
+        (me, weight, pooled_grad, near_targets[0], far_targets[0]),
+        [smem] + [vmem] * 4,
+    )
+    even_late = [late[0]] + [swap(late[k // 2], "batch", k) for k in range(2, owners, 2)]
     odd_late = [swap(x, "batch", 1) for x in even_late]
     even_targets = jnp.concatenate(even_targets, axis=0)
     odd_targets = swap(even_targets, "batch", 1)

time: 59.3 us -> 59.1 us (level)
  transfers between devices with their start and end apart: 18 -> 18, of which waited for: 9 -> 10; matrix products, arithmetic and copies ran while one was open for 1% -> 1% of each run, Pallas kernels for 5% -> 5%
where the time goes in v10:
time: 59.1 us; the launch traced here: 58.7 us
  starting transfers between devices  22.8 us (39%)
  waiting for transfers between devices  14.1 us (24%)
  blocking collectives  12.4 us (21%)
  Pallas kernels  5.93 us (10%)
  local copies, waits for them, and re-layouts  2.52 us (4%)
  between operations  0.71 us (1%)
    ppermute x16, starting transfers between devices, swap(): return lax.ppermute(x, axis, [(i, i ^ k) for i in range(n)])  14 us
    ppermute x16, waiting for transfers between devices, swap(): return lax.ppermute(x, axis, [(i, i ^ k) for i in range(n)])  12.7 us
    all_to_all x1, blocking collectives, exchange(): return lax.all_to_all(x, 'batch', split_axis=0, concat_axis=0, tiled=True)  12.4 us
    pallas_call x7, Pallas kernels, call(): pl.pallas_call(kernel, out_shape=shapes, in_specs=specs, out_specs=jax.tr...  5.93 us
    all_to_all x1, starting transfers between devices, exchange(): return lax.all_to_all(x, 'batch', split_axis=0, concat_axis=0, tiled=True)  5.18 us
    all_to_all x1, starting transfers between devices, on_device(): lax.all_to_all(sending, ('batch', 'latent'), split_axis=0, concat_axis=0,...  3.56 us
    unnamed x14, local copies, waits for them, and re-layouts  1.91 us
    all_to_all x1, waiting for transfers between devices, exchange(): return lax.all_to_all(x, 'batch', split_axis=0, concat_axis=0, tiled=True)  1.45 us
  transfers between devices with their start and end apart: 18, of which 10 were waited for; matrix products, arithmetic and copies ran while one was open for 1% of the time, Pallas kernels for 5%

profile of v10, /device:TPU:0, one launch (start us, length us, event | category | flops | bytes accessed | tf_op | source)
XLA Modules:
  0.0 58.7 jit_solution(2066728694122809736)
XLA Ops:
  0.6 5.2 %all-to-all-start = ((s32[8,1,64]{2,1,0:T(1,128)}), s32[8,1,64]{2,1,0:T(1,128)S(1)}, u32[]{:S(2)}, u32[]{:S(2)}) async-start(s32[8,1,64]{2,1,0:T(1,128)} %bitcast.15), calls=%async_computation | async-start | bytes 8192 | tf_op jit(solution)/shard_map/all_to_all | solution.py:20
  5.8 0.8 %copy-done.2 = s32[32,512]{1,0:T(8,128)S(1)} copy-done((s32[32,512]{1,0:T(8,128)S(1)}, s32[32,512]{1,0:T(8,128)}, u32[]{:S(2)}) %copy-start.2) | copy-done | bytes 65560
  6.7 1.2 %count_slots.1.count_ref = f32[32,512]{1,0:T(8,128)S(1)} custom-call(s32[32,512]{1,0:T(8,128)S(1)} %copy-done.2), custom_call_target="tpu_custom_call" | custom-call | tf_op jit(solution)/shard_map/count_slots/pallas_call | solution.py:24
  7.9 1.1 %copy-done.1 = bf16[512,512]{1,0:T(8,128)(2,1)S(1)} copy-done((bf16[512,512]{1,0:T(8,128)(2,1)S(1)}, bf16[512,512]{1,0:T(8,128)(2,1)}, u32[]{:S(2)}) %copy-start.1) | copy-done | bytes 524312
  8.9 1.5 %all-to-all-done.wanted_ref = s32[8,1,64]{2,1,0:T(1,128)S(1)} async-done(((s32[8,1,64]{2,1,0:T(1,128)}), s32[8,1,64]{2,1,0:T(1,128)S(1)}, u32[]{:S(2)}, u32[]{:S(2)}) %all-to-all-start) | async-done | bytes 2080 | tf_op jit(solution)/shard_map/all_to_all | solution.py:20
  10.4 0.6 pick_rows.1
  11.0 0.0 copy-start
  11.0 12.4 %all_to_all.15 = bf16[8,64,512]{2,1,0:T(8,128)(2,1)S(1)} all-to-all(bf16[8,64,512]{2,1,0:T(8,128)(2,1)S(1)} %bitcast.13), channel_id=1, replica_groups=mesh['batch'=8,'latent'=4] {'batch'}, dimensions={0} | all-to-all | bytes 1048576 | tf_op jit(solution)/shard_map/all_to_all | solution.py:20
  23.4 0.2 convolution_bitcast_fusion.refs_0_
  23.7 3.6 %collective-permute-start.2 = (f32[32,512]{1,0:T(8,128)S(1)}, f32[32,512]{1,0:T(8,128)S(1)}, u32[]{:S(2)}, u32[]{:S(2)}) collective-permute-start(f32[32,512]{1,0:T(8,128)S(1)} %convolution_bitcast_fusion.refs_0_), channel_id=1, source_target_pairs={{0,3},{1,2},{2,1},{3,0},{4,7},{5,6},{6,5},{7,4},{8,11},{9,10},{10,... | collective-permute-start | bytes 196616 | tf_op jit(solution)/shard_map/ppermute | solution.py:16
  27.3 0.0 collective-permute-start.1
  27.3 0.8 %collective-permute-start = (f32[32,512]{1,0:T(8,128)S(1)}, f32[32,512]{1,0:T(8,128)S(1)}, u32[]{:S(2)}, u32[]{:S(2)}) collective-permute-start(f32[32,512]{1,0:T(8,128)S(1)} %convolution_bitcast_fusion.refs_0_), channel_id=1, source_target_pairs={{0,1},{1,0},{2,3},{3,2},{4,5},{5,4},{6,7},{7,6},{8,9},{9,8},{10,11... | collective-permute-start | bytes 196616 | tf_op jit(solution)/shard_map/ppermute | solution.py:16
  28.1 0.6 collective-permute-start.3
  28.6 3.4 %collective-permute-done.3.near_ref = bf16[32,512]{1,0:T(8,128)(2,1)S(1)} collective-permute-done((bf16[32,512]{1,0:T(8,128)(2,1)S(1)}, bf16[32,512]{1,0:T(8,128)(2,1)S(1)}, u32[]{:S(2)}, u32[]{:S(2)}) %collective-permute-start.3) | collective-permute-done | bytes 32800 | tf_op jit(solution)/shard_map/ppermute | solution.py:16
  32.0 0.0 collective-permute-done.2.refs_3_
  32.0 0.6 %collective-permute-done.1.refs_2_ = f32[32,512]{1,0:T(8,128)S(1)} collective-permute-done((f32[32,512]{1,0:T(8,128)S(1)}, f32[32,512]{1,0:T(8,128)S(1)}, u32[]{:S(2)}, u32[]{:S(2)}) %collective-permute-start.1) | collective-permute-done | bytes 65568 | tf_op jit(solution)/shard_map/ppermute | solution.py:16
  32.6 0.0 collective-permute-done.refs_1_
  32.6 0.0 copy-done
  32.6 0.6 %weigh.1 = (f32[32,512]{1,0:T(8,128)S(1)}, bf16[32,1280]{1,0:T(8,128)(2,1)S(1)}) custom-call(f32[32,512]{1,0:T(8,128)S(1)} %count_slots.1.count_ref, bf16[32,256]{1,0:T(8,128)(2,1)S(1)} %copy-done.3, bf16[512,512]{1,0:T(8,128)(2,1)S(1)} %bitcast.11, bf16[512,1024]{1,0:T(8,128)(2,1)S(1)} %copy-done, f32[32,512]{1,0:T(8,128)S(1)} %convolution_bitcast_fusion.refs_0_, ...), custom_call_target="tpu_custom_call" | custom-call | tf_op jit(solution)/shard_map/weigh/pallas_call | solution.py:24
  33.2 3.1 %collective-permute-start.6 = (bf16[32,1280]{1,0:T(8,128)(2,1)S(1)}, bf16[32,1280]{1,0:T(8,128)(2,1)S(1)}, u32[]{:S(2)}, u32[]{:S(2)}) collective-permute-start(bf16[32,1280]{1,0:T(8,128)(2,1)S(1)} %get-tuple-element.34.refs_0_), channel_id=1, source_target_pairs={{0,3},{1,2},{2,1},{3,0},{4,7},{5,6},{6,5},{7,4},{8,11},{9,10},{10,... | collective-permute-start | bytes 245768 | tf_op jit(solution)/shard_map/ppermute | solution.py:16
  36.3 0.0 collective-permute-start.5
  36.3 1.4 %collective-permute-start.4 = (bf16[32,1280]{1,0:T(8,128)(2,1)S(1)}, bf16[32,1280]{1,0:T(8,128)(2,1)S(1)}, u32[]{:S(2)}, u32[]{:S(2)}) collective-permute-start(bf16[32,1280]{1,0:T(8,128)(2,1)S(1)} %get-tuple-element.34.refs_0_), channel_id=1, source_target_pairs={{0,1},{1,0},{2,3},{3,2},{4,5},{5,4},{6,7},{7,6},{8,9},{9,8},{10,11... | collective-permute-start | bytes 245768 | tf_op jit(solution)/shard_map/ppermute | solution.py:16
  37.6 0.6 collective-permute-start.7
  38.2 1.7 %collective-permute-done.6.refs_3_ = bf16[32,1280]{1,0:T(8,128)(2,1)S(1)} collective-permute-done((bf16[32,1280]{1,0:T(8,128)(2,1)S(1)}, bf16[32,1280]{1,0:T(8,128)(2,1)S(1)}, u32[]{:S(2)}, u32[]{:S(2)}) %collective-permute-start.6) | collective-permute-done | bytes 81952 | tf_op jit(solution)/shard_map/ppermute | solution.py:16
  39.9 2.6 %collective-permute-done.5.refs_2_ = bf16[32,1280]{1,0:T(8,128)(2,1)S(1)} collective-permute-done((bf16[32,1280]{1,0:T(8,128)(2,1)S(1)}, bf16[32,1280]{1,0:T(8,128)(2,1)S(1)}, u32[]{:S(2)}, u32[]{:S(2)}) %collective-permute-start.5) | collective-permute-done | bytes 81952 | tf_op jit(solution)/shard_map/ppermute | solution.py:16
  42.5 0.0 collective-permute-done.4.refs_1_
  42.5 1.4 %turn.1 = (bf16[32,1024]{1,0:T(8,128)(2,1)S(1)}, bf16[32,512]{1,0:T(8,128)(2,1)S(1)}, bf16[32,16,128]{2,1,0:T(8,128)(2,1)}) custom-call(s32[1]{0:T(128)} %bitcast.latent_ref, f32[1,1024]{1,0:T(1,128)S(1)} %bitcast.14, bf16[512,1024]{1,0:T(8,128)(2,1)S(1)} %copy-done, bf16[512,512]{1,0:T(8,128)(2,1)S(1)} %bitcast.12, ...), custom_call_target="tpu_custom_call" | custom-call | tf_op jit(solution)/shard_map/turn/pallas_call | solution.py:24
  44.0 0.0 collective-permute-done.7.far_ref
  44.0 3.6 %all-to-all-start.2 = ((bf16[32,16,128]{2,1,0:T(8,128)(2,1)}), bf16[32,16,128]{2,1,0:T(8,128)(2,1)S(1)}, u32[]{:S(2)}, u32[]{:S(2)}) async-start(bf16[32,16,128]{2,1,0:T(8,128)(2,1)} %get-tuple-element.38), calls=%async_computation.2 | async-start | bytes 262144 | tf_op jit(solution)/shard_map/all_to_all | solution.py:276
  47.6 2.7 %collective-permute-start.11 = (bf16[32,768]{1,0:T(8,128)(2,1)S(1)}, bf16[32,768]{1,0:T(8,128)(2,1)S(1)}, u32[]{:S(2)}, u32[]{:S(2)}) collective-permute-start(bf16[32,768]{1,0:T(8,128)(2,1)S(1)} %get-tuple-element.45), channel_id=1, source_target_pairs={{0,24},{4,28},{8,16},{12,20},{16,8},{20,12},{24,0},{28,4},{1,25},{... | collective-permute-start | bytes 147464 | tf_op jit(solution)/shard_map/ppermute | solution.py:16
  50.3 0.6 collective-permute-start.9
  50.9 0.3 collective-permute-start.10
  51.1 0.0 collective-permute-start.12
  51.1 0.5 collective-permute-start.8
  51.7 1.7 %collective-permute-done.11.refs_5_ = bf16[32,768]{1,0:T(8,128)(2,1)S(1)} collective-permute-done((bf16[32,768]{1,0:T(8,128)(2,1)S(1)}, bf16[32,768]{1,0:T(8,128)(2,1)S(1)}, u32[]{:S(2)}, u32[]{:S(2)}) %collective-permute-start.11) | collective-permute-done | bytes 49184 | tf_op jit(solution)/shard_map/ppermute | solution.py:16
  53.3 0.0 collective-permute-start.15
  53.3 1.6 %collective-permute-done.9.refs_3_ = bf16[32,1024]{1,0:T(8,128)(2,1)S(1)} collective-permute-done((bf16[32,1024]{1,0:T(8,128)(2,1)S(1)}, bf16[32,1024]{1,0:T(8,128)(2,1)S(1)}, u32[]{:S(2)}, u32[]{:S(2)}) %collective-permute-start.9) | collective-permute-done | bytes 65568 | tf_op jit(solution)/shard_map/ppermute | solution.py:16
  54.9 0.0 collective-permute-start.13
  54.9 0.5 collective-permute-done.10.refs_4_
  55.4 0.0 collective-permute-start.14
  55.4 0.6 %constant_dynamic-slice_fusion = bf16[32,256]{1,0:T(8,128)(2,1)} fusion(bf16[32,1024]{1,0:T(8,128)(2,1)S(1)} %get-tuple-element.35, s32[]{:T(128)S(6)} %select_n.3), kind=kLoop, calls=%fused_computation.4 | loop fusion | bytes 32772 | tf_op jit(solution)/shard_map/dynamic_slice | solution.py:273
  56.0 0.0 collective-permute-done.12.refs_6_
  56.0 0.0 collective-permute-done.8.refs_1_
  56.1 0.0 collective-permute-done.15.refs_9_
  56.1 0.1 collective-permute-done.13.refs_7_
  56.2 0.5 collective-permute-done.14.refs_8_
  56.7 0.0 all-to-all-done.2.sent_ref
  56.7 2.1 %add_rows.1 = f32[512,512]{1,0:T(8,128)} custom-call(s32[1]{0:T(128)} %bitcast.6.me_ref, s32[8,1,64]{2,1,0:T(1,128)S(1)} %all-to-all-done.wanted_ref, bf16[32,16,128]{2,1,0:T(8,128)(2,1)S(1)} %all-to-all-done.2.sent_ref, bf16[96,512]{1,0:T(8,128)(2,1)S(1)} %constant_dynamic-update-slice_fusion.refs_0_, bf16[96,512]{1,0:T(8,128)(2,1)S(1)} %collective-permute-done.8.refs_1_, ...), custom_call_target="tpu_custom_call" | custom-call | tf_op jit(solution)/shard_map/add_rows/pallas_call | solution.py:24
  (13 shorter events, 0.1 us)
Async XLA Ops:
  0.6 9.8 %all-to-all-start = ((s32[8,1,64]{2,1,0:T(1,128)}), s32[8,1,64]{2,1,0:T(1,128)S(1)}, u32[]{:S(2)}, u32[]{:S(2)}) async-start(s32[8,1,64]{2,1,0:T(1,128)} %bitcast.15), calls=%async_computation | async-start | bytes 8192 | tf_op jit(solution)/shard_map/all_to_all | solution.py:20
  5.8 0.8 %copy-start.2 = (s32[32,512]{1,0:T(8,128)S(1)}, s32[32,512]{1,0:T(8,128)}, u32[]{:S(2)}) copy-start(s32[32,512]{1,0:T(8,128)} %history_ref.1) | copy-start | bytes 196612
  7.9 1.1 %copy-start.1 = (bf16[512,512]{1,0:T(8,128)(2,1)S(1)}, bf16[512,512]{1,0:T(8,128)(2,1)}, u32[]{:S(2)}) copy-start(bf16[512,512]{1,0:T(8,128)(2,1)} %rows_ref.1) | copy-start | bytes 1572868
  10.4 13.0 %copy-start.5 = (bf16[32,512]{1,0:T(8,128)(2,1)S(1)}, bf16[32,512]{1,0:T(8,128)(2,1)}, u32[]{:S(2)}) copy-start(bf16[32,512]{1,0:T(8,128)(2,1)} %param.8) | copy-start | bytes 98308
  11.0 21.6 %copy-start = (bf16[512,1024]{1,0:T(8,128)(2,1)S(1)}, bf16[512,1024]{1,0:T(8,128)(2,1)}, u32[]{:S(2)}) copy-start(bf16[512,1024]{1,0:T(8,128)(2,1)} %w_up_ref.3) | copy-start | bytes 3145732
  23.4 9.2 %copy-start.3 = (bf16[32,256]{1,0:T(8,128)(2,1)S(1)}, bf16[32,256]{1,0:T(8,128)(2,1)}, u32[]{:S(2)}) copy-start(bf16[32,256]{1,0:T(8,128)(2,1)} %upstream_ref.1) | copy-start | bytes 49156
  23.7 8.3 %collective-permute-start.2 = (f32[32,512]{1,0:T(8,128)S(1)}, f32[32,512]{1,0:T(8,128)S(1)}, u32[]{:S(2)}, u32[]{:S(2)}) collective-permute-start(f32[32,512]{1,0:T(8,128)S(1)} %convolution_bitcast_fusion.refs_0_), channel_id=1, source_target_pairs={{0,3},{1,2},{2,1},{3,0},{4,7},{5,6},{6,5},{7,4},{8,11},{9,10},{10,... | collective-permute-start | bytes 196616 | tf_op jit(solution)/shard_map/ppermute | solution.py:16
  27.3 5.3 %collective-permute-start.1 = (f32[32,512]{1,0:T(8,128)S(1)}, f32[32,512]{1,0:T(8,128)S(1)}, u32[]{:S(2)}, u32[]{:S(2)}) collective-permute-start(f32[32,512]{1,0:T(8,128)S(1)} %convolution_bitcast_fusion.refs_0_), channel_id=1, source_target_pairs={{0,2},{1,3},{2,0},{3,1},{4,6},{5,7},{6,4},{7,5},{8,10},{9,11},{10,... | collective-permute-start | bytes 196616 | tf_op jit(solution)/shard_map/ppermute | solution.py:16
  27.3 5.3 %collective-permute-start = (f32[32,512]{1,0:T(8,128)S(1)}, f32[32,512]{1,0:T(8,128)S(1)}, u32[]{:S(2)}, u32[]{:S(2)}) collective-permute-start(f32[32,512]{1,0:T(8,128)S(1)} %convolution_bitcast_fusion.refs_0_), channel_id=1, source_target_pairs={{0,1},{1,0},{2,3},{3,2},{4,5},{5,4},{6,7},{7,6},{8,9},{9,8},{10,11... | collective-permute-start | bytes 196616 | tf_op jit(solution)/shard_map/ppermute | solution.py:16
  28.1 3.9 %collective-permute-start.3 = (bf16[32,512]{1,0:T(8,128)(2,1)S(1)}, bf16[32,512]{1,0:T(8,128)(2,1)S(1)}, u32[]{:S(2)}, u32[]{:S(2)}) collective-permute-start(bf16[32,512]{1,0:T(8,128)(2,1)S(1)} %copy-done.5), channel_id=1, source_target_pairs={{0,8},{4,12},{8,0},{12,4},{16,24},{20,28},{24,16},{28,20},{1,9},{5... | collective-permute-start | bytes 98312 | tf_op jit(solution)/shard_map/ppermute | solution.py:16
  33.2 6.7 %collective-permute-start.6 = (bf16[32,1280]{1,0:T(8,128)(2,1)S(1)}, bf16[32,1280]{1,0:T(8,128)(2,1)S(1)}, u32[]{:S(2)}, u32[]{:S(2)}) collective-permute-start(bf16[32,1280]{1,0:T(8,128)(2,1)S(1)} %get-tuple-element.34.refs_0_), channel_id=1, source_target_pairs={{0,3},{1,2},{2,1},{3,0},{4,7},{5,6},{6,5},{7,4},{8,11},{9,10},{10,... | collective-permute-start | bytes 245768 | tf_op jit(solution)/shard_map/ppermute | solution.py:16
  36.3 6.3 %collective-permute-start.5 = (bf16[32,1280]{1,0:T(8,128)(2,1)S(1)}, bf16[32,1280]{1,0:T(8,128)(2,1)S(1)}, u32[]{:S(2)}, u32[]{:S(2)}) collective-permute-start(bf16[32,1280]{1,0:T(8,128)(2,1)S(1)} %get-tuple-element.34.refs_0_), channel_id=1, source_target_pairs={{0,2},{1,3},{2,0},{3,1},{4,6},{5,7},{6,4},{7,5},{8,10},{9,11},{10,... | collective-permute-start | bytes 245768 | tf_op jit(solution)/shard_map/ppermute | solution.py:16
  36.3 6.3 %collective-permute-start.4 = (bf16[32,1280]{1,0:T(8,128)(2,1)S(1)}, bf16[32,1280]{1,0:T(8,128)(2,1)S(1)}, u32[]{:S(2)}, u32[]{:S(2)}) collective-permute-start(bf16[32,1280]{1,0:T(8,128)(2,1)S(1)} %get-tuple-element.34.refs_0_), channel_id=1, source_target_pairs={{0,1},{1,0},{2,3},{3,2},{4,5},{5,4},{6,7},{7,6},{8,9},{9,8},{10,11... | collective-permute-start | bytes 245768 | tf_op jit(solution)/shard_map/ppermute | solution.py:16
  37.6 6.4 %collective-permute-start.7 = (bf16[32,512]{1,0:T(8,128)(2,1)S(1)}, bf16[32,512]{1,0:T(8,128)(2,1)S(1)}, u32[]{:S(2)}, u32[]{:S(2)}) collective-permute-start(bf16[32,512]{1,0:T(8,128)(2,1)S(1)} %copy-done.5), channel_id=1, source_target_pairs={{0,16},{4,20},{8,24},{12,28},{16,0},{20,4},{24,8},{28,12},{1,17},{... | collective-permute-start | bytes 98312 | tf_op jit(solution)/shard_map/ppermute | solution.py:16
  38.2 4.4 %copy-start.4 = (f32[1024]{0:T(1024)S(1)}, f32[1024]{0:T(1024)}, u32[]{:S(2)}) copy-start(f32[1024]{0:T(1024)} %param.10) | copy-start | bytes 12292
  44.0 12.7 %all-to-all-start.2 = ((bf16[32,16,128]{2,1,0:T(8,128)(2,1)}), bf16[32,16,128]{2,1,0:T(8,128)(2,1)S(1)}, u32[]{:S(2)}, u32[]{:S(2)}) async-start(bf16[32,16,128]{2,1,0:T(8,128)(2,1)} %get-tuple-element.38), calls=%async_computation.2 | async-start | bytes 262144 | tf_op jit(solution)/shard_map/all_to_all | solution.py:276
  47.6 5.7 %collective-permute-start.11 = (bf16[32,768]{1,0:T(8,128)(2,1)S(1)}, bf16[32,768]{1,0:T(8,128)(2,1)S(1)}, u32[]{:S(2)}, u32[]{:S(2)}) collective-permute-start(bf16[32,768]{1,0:T(8,128)(2,1)S(1)} %get-tuple-element.45), channel_id=1, source_target_pairs={{0,24},{4,28},{8,16},{12,20},{16,8},{20,12},{24,0},{28,4},{1,25},{... | collective-permute-start | bytes 147464 | tf_op jit(solution)/shard_map/ppermute | solution.py:16
  50.3 4.6 %collective-permute-start.9 = (bf16[32,1024]{1,0:T(8,128)(2,1)S(1)}, bf16[32,1024]{1,0:T(8,128)(2,1)S(1)}, u32[]{:S(2)}, u32[]{:S(2)}) collective-permute-start(bf16[32,1024]{1,0:T(8,128)(2,1)S(1)} %get-tuple-element.43), channel_id=1, source_target_pairs={{0,8},{4,12},{8,0},{12,4},{16,24},{20,28},{24,16},{28,20},{1,9},{5... | collective-permute-start | bytes 196616 | tf_op jit(solution)/shard_map/ppermute | solution.py:16
  50.9 4.5 %collective-permute-start.10 = (bf16[32,1024]{1,0:T(8,128)(2,1)S(1)}, bf16[32,1024]{1,0:T(8,128)(2,1)S(1)}, u32[]{:S(2)}, u32[]{:S(2)}) collective-permute-start(bf16[32,1024]{1,0:T(8,128)(2,1)S(1)} %get-tuple-element.44), channel_id=1, source_target_pairs={{0,16},{4,20},{8,24},{12,28},{16,0},{20,4},{24,8},{28,12},{1,17},{... | collective-permute-start | bytes 196616 | tf_op jit(solution)/shard_map/ppermute | solution.py:16
  51.1 4.9 %collective-permute-start.12 = (bf16[32,768]{1,0:T(8,128)(2,1)S(1)}, bf16[32,768]{1,0:T(8,128)(2,1)S(1)}, u32[]{:S(2)}, u32[]{:S(2)}) collective-permute-start(bf16[32,768]{1,0:T(8,128)(2,1)S(1)} %get-tuple-element.42.refs_2_), channel_id=1, source_target_pairs={{0,4},{4,0},{8,12},{12,8},{16,20},{20,16},{24,28},{28,24},{1,5},{5... | collective-permute-start | bytes 147464 | tf_op jit(solution)/shard_map/ppermute | solution.py:16
  51.1 4.9 %collective-permute-start.8 = (bf16[96,512]{1,0:T(8,128)(2,1)S(1)}, bf16[96,512]{1,0:T(8,128)(2,1)S(1)}, u32[]{:S(2)}, u32[]{:S(2)}) collective-permute-start(bf16[96,512]{1,0:T(8,128)(2,1)S(1)} %constant_dynamic-update-slice_fusion.refs_0_), channel_id=1, source_target_pairs={{0,4},{4,0},{8,12},{12,8},{16,20},{20,16},{24,28},{28,24},{1,5},{5... | collective-permute-start | bytes 294920 | tf_op jit(solution)/shard_map/ppermute | solution.py:16
  53.3 2.7 %collective-permute-start.15 = (bf16[32,768]{1,0:T(8,128)(2,1)S(1)}, bf16[32,768]{1,0:T(8,128)(2,1)S(1)}, u32[]{:S(2)}, u32[]{:S(2)}) collective-permute-start(bf16[32,768]{1,0:T(8,128)(2,1)S(1)} %collective-permute-done.11.refs_5_), channel_id=1, source_target_pairs={{0,4},{4,0},{8,12},{12,8},{16,20},{20,16},{24,28},{28,24},{1,5},{5... | collective-permute-start | bytes 147464 | tf_op jit(solution)/shard_map/ppermute | solution.py:16
  54.9 1.3 %collective-permute-start.13 = (bf16[32,1024]{1,0:T(8,128)(2,1)S(1)}, bf16[32,1024]{1,0:T(8,128)(2,1)S(1)}, u32[]{:S(2)}, u32[]{:S(2)}) collective-permute-start(bf16[32,1024]{1,0:T(8,128)(2,1)S(1)} %collective-permute-done.9.refs_3_), channel_id=1, source_target_pairs={{0,4},{4,0},{8,12},{12,8},{16,20},{20,16},{24,28},{28,24},{1,5},{5... | collective-permute-start | bytes 196616 | tf_op jit(solution)/shard_map/ppermute | solution.py:16
  55.4 1.3 %collective-permute-start.14 = (bf16[32,1024]{1,0:T(8,128)(2,1)S(1)}, bf16[32,1024]{1,0:T(8,128)(2,1)S(1)}, u32[]{:S(2)}, u32[]{:S(2)}) collective-permute-start(bf16[32,1024]{1,0:T(8,128)(2,1)S(1)} %collective-permute-done.10.refs_4_), channel_id=1, source_target_pairs={{0,4},{4,0},{8,12},{12,8},{16,20},{20,16},{24,28},{28,24},{1,5},{5... | collective-permute-start | bytes 196616 | tf_op jit(solution)/shard_map/ppermute | solution.py:16
